TPU v7x, 32 devices: a whole 2x2x4 slice. The times are simulated.
32 devices in a mesh: groups: 2 (over x), blk: 8 (over z, y), dim: 2 (over core).
Axes of the slice: x: 2, y: 2, z: 4, core: 2. Of those that a mesh axis runs over, the one named last changes fastest.
Arguments:
- gradients: bfloat16 [4096, 128, 128], P(('groups', 'blk'), 'dim'), parts along dimension 0, may hold values from -60 to 60
- owner_of: int32 [4096, 1], P(('groups', 'blk')), parts along dimension 0, may hold values from 0 to 7; in each aligned block of 256 rows (0 to 255, 256 to 511, ...) at most 48 rows name the same one
- pair_flags: int32 [16, 3], P('groups'), parts along dimension 0, may hold values from 0 to 1, as said below
- left_factor: bfloat16 [128, 128], replicated, may hold values from -0.5 to 0.5
- right_factor: bfloat16 [128, 128], replicated, may hold values from -0.5 to 0.5
Outputs:
- tiles: bfloat16 [96, 384, 384], P(('groups', 'blk'), None, 'dim'), parts along dimension 0
- self_influence: bfloat16 [6144], P(('groups', 'blk')), parts along dimension 0
There are 2 independent parts, one for each index of `groups`. A program takes and returns all parts, laid end to end along the dimension named above; an argument that names none is the same for every part. Nothing has to cross between parts.
Inputs may be any that keep to these rules, and one draw needn't show every extreme that they name: `owner_of`: at most 48 of the 256 examples of one producer name the same owner. `pair_flags`: 1 where block a is compared with block (a + j + 1) mod 8, else 0.
All inputs are finite; a program needn't handle non-finite values.
Results may differ from a plain program's by a relative error of at most 0.0031.
The roundings to bfloat16 on the way count: a program that leaves them out, or rounds other values in their place, can miss the bound.
Values may be sent and summed in bfloat16 or wider, within the bound.
No kernel may reach another device: no remote copies, remote signals or barrier semaphores. Data moves between devices by JAX's collectives and lax.ppermute only.
A program may use at most 128 MiB of HBM per device.

v0:
```python
import jax
import jax.numpy as jnp
from jax import lax
from jax.sharding import PartitionSpec as P


def from_behind(shard, axis, by):
    peers = lax.axis_size(axis)
    return lax.ppermute(shard, axis, [(i, (i + by) % peers) for i in range(peers)])


def per_device(gradients, owner_of, pair_flags, left_factor, right_factor):
    count, half, width = gradients.shape
    halves = lax.axis_size("dim")
    position = lax.axis_index("dim")
    feat = half * width * halves
    highest = lax.Precision.HIGHEST
    whole = lax.all_gather(gradients, "dim", axis=1, tiled=True)
    left_rows = lax.dynamic_slice_in_dim(left_factor, position * half, half, 0)
    left_side = jnp.einsum("ik,ekc->eic", left_rows, whole, preferred_element_type=jnp.float32)
    full = jnp.einsum("eic,cd->eid", left_side, right_factor.astype(jnp.float32), precision=highest)
    mean_sq = lax.psum(jnp.sum(full * full, axis=(1, 2)), "dim") / feat
    normed = (
        (full * lax.rsqrt(mean_sq + 1e-06)[:, None, None])
        .astype(jnp.bfloat16)
        .reshape(count, half * width)
    )
    influence = jnp.log1p(mean_sq).astype(jnp.bfloat16)
    owners_count = lax.axis_size("blk")
    slots = 3 * count // (2 * owners_count)
    block = owners_count * slots
    owners = owner_of[:, 0]
    onehot = (owners[:, None] == jnp.arange(owners_count, dtype=jnp.int32)[None, :]).astype(
        jnp.int32
    )
    earlier = jnp.cumsum(onehot, axis=0) - onehot
    rank = jnp.sum(earlier * onehot, axis=1)
    target = owners * slots + rank
    placing = (jnp.arange(block, dtype=jnp.int32)[:, None] == target[None, :]).astype(jnp.bfloat16)
    outgoing = jnp.dot(placing, normed, preferred_element_type=jnp.float32).astype(jnp.bfloat16)
    outgoing = outgoing.reshape(owners_count, slots, half * width)
    sent_influence = jnp.dot(placing, influence, preferred_element_type=jnp.float32).astype(
        jnp.bfloat16
    )
    sent_influence = sent_influence.reshape(owners_count, slots)
    received, got_influence = (
        lax.all_to_all(outgoing, "blk", split_axis=0, concat_axis=0, tiled=True),
        lax.all_to_all(sent_influence, "blk", split_axis=0, concat_axis=0, tiled=True),
    )
    own = received.reshape(block, half * width)
    self_influence = got_influence.reshape(block)
    reach = pair_flags.shape[1]
    owner_index = lax.axis_index("blk")
    picker = (jnp.arange(owners_count, dtype=jnp.int32) == owner_index).astype(jnp.float32)
    flags = pair_flags.astype(jnp.float32)
    ahead_flags = jnp.dot(picker, flags)
    scale = feat ** (-0.5)
    partials = []
    for step in range(1, reach + 1):
        ahead = from_behind(own, "blk", -step)
        product = jnp.dot(own, ahead.T, preferred_element_type=jnp.float32)
        partials.append(product * (ahead_flags[step - 1] * scale))
    partials = partials + [term.T for term in partials]
    summed = lax.psum_scatter(jnp.stack(partials), "dim", scatter_dimension=2, tiled=True).astype(
        jnp.bfloat16
    )
    returned = [from_behind(summed[reach + step - 1], "blk", step) for step in range(1, reach + 1)]
    summed = jnp.concatenate([summed[:reach], jnp.stack(returned)], axis=0)
    return (summed, self_influence)


def solution(mesh):
    return jax.shard_map(
        per_device,
        mesh=mesh,
        in_specs=(
            P(("groups", "blk"), "dim", None),
            P(("groups", "blk"), None),
            P("groups", None),
            P(),
            P(),
        ),
        out_specs=(P(("groups", "blk"), None, "dim"), P(("groups", "blk"))),
        check_vma=False,
    )
```

profile of v0, /device:TPU:5, one launch (start us, length us, event | category | flops | bytes accessed | tf_op | source)
XLA Modules:
  0.0 815.3 jit_solution(15423593893522446378)
XLA Ops:
  10.9 20.4 %all-gather.2.cloned.1.call-done = bf16[256,128,128]{2,1,0:T(8,128)(2,1)} async-done(((bf16[256,64,128]{2,1,0:T(8,128)(2,1)}), bf16[256,128,128]{2,1,0:T(8,128)(2,1)}) %all-gather.2.cloned.1.call-update) | async-done | bytes 8388624 | tf_op jit(solution)/shard_map/all_gather | solution.py:18
  31.4 4.6 convolution_bitcast_fusion
  36.0 13.8 %multiply_reduce_fusion = (f32[256]{0:T(256)S(1)}, f32[256,64,128]{0,2,1:T(8,128)}) fusion(bf16[128,128]{1,0:T(8,128)(2,1)S(1)} %copy-done, f32[256,64,128]{2,1,0:T(8,128)S(1)} %convolution_bitcast_fusion), kind=kOutput, calls=%fused_computation.4 | convolution fusion | flops 3225419520 | bytes 16811008 | tf_op jit(solution)/shard_map/eic,cd->eid/dot_general | solution.py:21
  49.9 2.5 psum.7
  52.3 4.5 multiply_convert_fusion
  56.8 1.8 convolution_convert_fusion
  58.7 142.6 %all_to_all.15 = bf16[8,48,8192]{2,1,0:T(8,128)(2,1)} all-to-all(bf16[8,48,8192]{2,1,0:T(8,128)(2,1)S(1)} %bitcast.64), channel_id=1, replica_groups=mesh['groups'=2,'blk'=8,'dim'=2] {'blk'}, dimensions={0} | all-to-all | bytes 12582912 | tf_op jit(solution)/shard_map/all_to_all | solution.py:47
  201.2 1.4 collective-permute-start.2
  202.7 1.2 collective-permute-start.1
  206.4 268.2 %collective-permute-done.2 = bf16[384,8192]{1,0:T(8,128)(2,1)} collective-permute-done((bf16[384,8192]{1,0:T(8,128)(2,1)}, bf16[384,8192]{1,0:T(8,128)(2,1)}, u32[]{:S(2)}, u32[]{:S(2)}) %collective-permute-start.2) | collective-permute-done | bytes 6291488 | tf_op jit(solution)/shard_map/ppermute | solution.py:9
  474.6 8.2 %convolution_multiply_fusion = f32[384,384]{1,0:T(8,128)S(1)} fusion(bf16[384,8192]{1,0:T(8,128)(2,1)} %bitcast.9, bf16[384,8192]{1,0:T(8,128)(2,1)} %collective-permute-done.2, f32[]{:T(128)} %bitcast.16), kind=kOutput, calls=%fused_computation.6 | convolution fusion | flops 2416066560 | bytes 13172740 | tf_op jit(solution)/shard_map/dot_general | solution.py:61
  483.0 8.2 %convolution_multiply_fusion.1 = f32[384,384]{1,0:T(8,128)S(1)} fusion(bf16[384,8192]{1,0:T(8,128)(2,1)} %bitcast.9, bf16[384,8192]{1,0:T(8,128)(2,1)} %collective-permute-done.1, f32[]{:T(128)} %bitcast.14), kind=kOutput, calls=%fused_computation.7 | convolution fusion | flops 2416066560 | bytes 13172740 | tf_op jit(solution)/shard_map/dot_general | solution.py:61
  491.5 118.1 %collective-permute-done = bf16[384,8192]{1,0:T(8,128)(2,1)} collective-permute-done((bf16[384,8192]{1,0:T(8,128)(2,1)}, bf16[384,8192]{1,0:T(8,128)(2,1)}, u32[]{:S(2)}, u32[]{:S(2)}) %collective-permute-start) | collective-permute-done | bytes 6291488 | tf_op jit(solution)/shard_map/ppermute | solution.py:9
  609.6 8.2 %convolution_multiply_fusion.2 = f32[384,384]{1,0:T(8,128)S(1)} fusion(bf16[384,8192]{1,0:T(8,128)(2,1)} %bitcast.9, bf16[384,8192]{1,0:T(8,128)(2,1)} %collective-permute-done, f32[]{:T(128)} %bitcast.12), kind=kOutput, calls=%fused_computation.8 | convolution fusion | flops 2416066560 | bytes 13172740 | tf_op jit(solution)/shard_map/dot_general | solution.py:61
  617.8 1.1 copy.16
  618.9 1.9 constant_dynamic-update-slice_fusion.2
  621.6 0.9 constant_dynamic-update-slice_fusion
  625.1 163.2 %reduce-scatter.2.cloned.1.call-done = f32[6,384,192]{1,2,0:T(8,128)} async-done(((f32[6,384,384]{1,2,0:T(8,128)}), f32[6,384,192]{1,2,0:T(8,128)}) %reduce-scatter.2.cloned.1.call-update) | async-done | bytes 1769488 | tf_op jit(solution)/shard_map/reduce_scatter | solution.py:64
  788.4 1.6 convert_element_type.33
  790.0 1.3 collective-permute-start.3
  791.3 2.1 collective-permute-start.5
  793.4 1.2 collective-permute-start.4
  794.9 11.8 %all_to_all.16 = bf16[8,1,48]{2,1,0:T(2,128)(2,1)S(1)} all-to-all(bf16[8,1,48]{2,1,0:T(2,128)(2,1)S(1)} %all_to_all.12), channel_id=1, replica_groups=mesh['groups'=2,'blk'=8,'dim'=2] {'blk'}, dimensions={0} | all-to-all | bytes 1536 | tf_op jit(solution)/shard_map/all_to_all | solution.py:48
  807.4 1.1 pad_maximum_fusion
  (38 shorter events, 9.5 us)
Async XLA Ops:
  7.2 28.9 %copy-start = (bf16[128,128]{1,0:T(8,128)(2,1)S(1)}, bf16[128,128]{1,0:T(8,128)(2,1)}, u32[]{:S(2)}) copy-start(bf16[128,128]{1,0:T(8,128)(2,1)} %param.9) | copy-start | bytes 98308
  7.2 24.2 %all-gather.2.cloned.1.call-start = ((), (), s32[]{:S(2)}) async-start(), calls=%async_computation.3 | async-start | bytes 12582912 | tf_op jit(solution)/shard_map/all_gather | solution.py:18
  7.9 780.4 %reduce-scatter.2.cloned.1.call-start = ((), (), s32[]{:S(2)}) async-start(), calls=%async_computation.4 | async-start | bytes 5308416 | tf_op jit(solution)/shard_map/reduce_scatter | solution.py:64
  58.6 145.2 %copy-start.2 = (s32[8,3]{0,1:T(4,128)S(1)}, s32[8,3]{0,1:T(4,128)}, u32[]{:S(2)}) copy-start(s32[8,3]{0,1:T(4,128)} %param.7) | copy-start | bytes 292
  201.2 273.4 %collective-permute-start.2 = (bf16[384,8192]{1,0:T(8,128)(2,1)}, bf16[384,8192]{1,0:T(8,128)(2,1)}, u32[]{:S(2)}, u32[]{:S(2)}) collective-permute-start(bf16[384,8192]{1,0:T(8,128)(2,1)} %bitcast.9), channel_id=1, source_target_pairs={{0,10},{2,12},{4,14},{6,0},{8,2},{10,4},{12,6},{14,8},{1,11},{3,13... | collective-permute-start | bytes 18874376 | tf_op jit(solution)/shard_map/ppermute | solution.py:9
  202.7 280.4 %collective-permute-start.1 = (bf16[384,8192]{1,0:T(8,128)(2,1)}, bf16[384,8192]{1,0:T(8,128)(2,1)}, u32[]{:S(2)}, u32[]{:S(2)}) collective-permute-start(bf16[384,8192]{1,0:T(8,128)(2,1)} %bitcast.9), channel_id=1, source_target_pairs={{0,12},{2,14},{4,0},{6,2},{8,4},{10,6},{12,8},{14,10},{1,13},{3,15... | collective-permute-start | bytes 18874376 | tf_op jit(solution)/shard_map/ppermute | solution.py:9
  203.8 405.8 %collective-permute-start = (bf16[384,8192]{1,0:T(8,128)(2,1)}, bf16[384,8192]{1,0:T(8,128)(2,1)}, u32[]{:S(2)}, u32[]{:S(2)}) collective-permute-start(bf16[384,8192]{1,0:T(8,128)(2,1)} %bitcast.9), channel_id=1, source_target_pairs={{0,14},{2,0},{4,2},{6,4},{8,6},{10,8},{12,10},{14,12},{1,15},{3,1}... | collective-permute-start | bytes 18874376 | tf_op jit(solution)/shard_map/ppermute | solution.py:9
  622.5 186.0 %copy-start.1 = (bf16[128,128]{1,0:T(8,128)(2,1)S(1)}, bf16[128,128]{1,0:T(8,128)(2,1)}, u32[]{:S(2)}) copy-start(bf16[128,128]{1,0:T(8,128)(2,1)} %param.9) | copy-start | bytes 98308
  790.0 17.4 %collective-permute-start.3 = (bf16[384,192]{0,1:T(8,128)(2,1)S(1)}, bf16[384,192]{0,1:T(8,128)(2,1)S(1)}, u32[]{:S(2)}, u32[]{:S(2)}) collective-permute-start(bf16[384,192]{0,1:T(8,128)(2,1)S(1)} %get-tuple-element.2), channel_id=1, source_target_pairs={{0,2},{2,4},{4,6},{6,8},{8,10},{10,12},{12,14},{14,0},{1,3},{3,5},... | collective-permute-start | bytes 442376 | tf_op jit(solution)/shard_map/ppermute | solution.py:9
  791.3 16.1 %collective-permute-start.5 = (bf16[384,192]{0,1:T(8,128)(2,1)S(1)}, bf16[384,192]{0,1:T(8,128)(2,1)S(1)}, u32[]{:S(2)}, u32[]{:S(2)}) collective-permute-start(bf16[384,192]{0,1:T(8,128)(2,1)S(1)} %get-tuple-element.3), channel_id=1, source_target_pairs={{0,6},{2,8},{4,10},{6,12},{8,14},{10,0},{12,2},{14,4},{1,7},{3,9},... | collective-permute-start | bytes 442376 | tf_op jit(solution)/shard_map/ppermute | solution.py:9
  793.4 14.0 %collective-permute-start.4 = (bf16[384,192]{0,1:T(8,128)(2,1)S(1)}, bf16[384,192]{0,1:T(8,128)(2,1)S(1)}, u32[]{:S(2)}, u32[]{:S(2)}) collective-permute-start(bf16[384,192]{0,1:T(8,128)(2,1)S(1)} %get-tuple-element.4), channel_id=1, source_target_pairs={{0,4},{2,6},{4,8},{6,10},{8,12},{10,14},{12,0},{14,2},{1,5},{3,7},... | collective-permute-start | bytes 442376 | tf_op jit(solution)/shard_map/ppermute | solution.py:9
Sparse Core Ops, SparseCore 0:
  9.6 21.7 all-gather.1
  625.2 163.0 reduce-scatter.1
where the time goes:
time: 818 us; the launch traced here: 815 us
  waiting for transfers between devices  571 us (70%)
  blocking collectives  157 us (19%)
  matrix products  45.2 us (6%)
  between operations  16 us (2%)
  other arithmetic  9.9 us (1%)
  local copies, waits for them, and re-layouts  9.41 us (1%)
    ppermute x6, waiting for transfers between devices, from_behind(): lax.ppermute(shard, axis, [(i, (i + by) % peers) for i in range(peers)])  386 us
    reduce_scatter x1, waiting for transfers between devices, per_device(): lax.psum_scatter(jnp.stack(partials), 'dim', scatter_dimension=2, tiled=T...  163 us
    all_to_all x1, blocking collectives, per_device(): lax.all_to_all(outgoing, 'blk', split_axis=0, concat_axis=0, tiled=True)  143 us
    dot_general x3, matrix products, per_device(): product = jnp.dot(own, ahead.T, preferred_element_type=jnp.float32)  24.6 us
    all_gather x1, waiting for transfers between devices, per_device(): whole = lax.all_gather(gradients, 'dim', axis=1, tiled=True)  20.4 us
  transfers between devices with their start and end apart: 8, of which 4 were waited for; matrix products, arithmetic and copies ran while one was open for 3% of the time, Pallas kernels for 0%

commit v1 on v0

--- a/solution.py
+++ b/solution.py
@@ -1,7 +1,17 @@
+import functools
+
 import jax
 import jax.numpy as jnp
 from jax import lax
+from jax.experimental import pallas as pl
+from jax.experimental.pallas import tpu as pltpu
 from jax.sharding import PartitionSpec as P
+
+PARTIAL_BYTES = 16 * 2**20
+CHUNKS = (1, 1, 1, 1)
+GROUP = 8
+STEP = 32
+VMEM_BYTES = 56 * 2**20
 
 
 def from_behind(shard, axis, by):
@@ -9,7 +19,17 @@
     return lax.ppermute(shard, axis, [(i, (i + by) % peers) for i in range(peers)])
 
 
-def per_device(gradients, owner_of, pair_flags, left_factor, right_factor):
+def slot_targets(owner_of, owners_count, slots):
+    owners = owner_of[:, 0]
+    onehot = (owners[:, None] == jnp.arange(owners_count, dtype=jnp.int32)[None, :]).astype(
+        jnp.int32
+    )
+    earlier = jnp.cumsum(onehot, axis=0) - onehot
+    rank = jnp.sum(earlier * onehot, axis=1)
+    return owners * slots + rank
+
+
+def ring_plan(gradients, owner_of, pair_flags, left_factor, right_factor):
     count, half, width = gradients.shape
     halves = lax.axis_size("dim")
     position = lax.axis_index("dim")
@@ -29,13 +49,7 @@
     owners_count = lax.axis_size("blk")
     slots = 3 * count // (2 * owners_count)
     block = owners_count * slots
-    owners = owner_of[:, 0]
-    onehot = (owners[:, None] == jnp.arange(owners_count, dtype=jnp.int32)[None, :]).astype(
-        jnp.int32
-    )
-    earlier = jnp.cumsum(onehot, axis=0) - onehot
-    rank = jnp.sum(earlier * onehot, axis=1)
-    target = owners * slots + rank
+    target = slot_targets(owner_of, owners_count, slots)
     placing = (jnp.arange(block, dtype=jnp.int32)[:, None] == target[None, :]).astype(jnp.bfloat16)
     outgoing = jnp.dot(placing, normed, preferred_element_type=jnp.float32).astype(jnp.bfloat16)
     outgoing = outgoing.reshape(owners_count, slots, half * width)
@@ -69,7 +83,257 @@
     return (summed, self_influence)
 
 
+def precondition_kernel(rows, spot, own, other, left, right, *rest):
+    outs, mean_sq, full, sums, parts = rest[:-4], rest[-4], rest[-3], rest[-2], rest[-1]
+    here = spot[0]
+    batch, half, width = own.shape
+    side = 2 * half
+    for first in range(0, batch, GROUP):
+        for e in range(first, first + GROUP, 2):
+            pair = [jnp.concatenate([own[i], other[i]], axis=0) for i in (e, e + 1)]
+            sides = jnp.dot(
+                left[...], jnp.concatenate(pair, axis=1), preferred_element_type=jnp.float32
+            )
+            for i in range(2):
+                term = sides[:, i * width : (i + 1) * width]
+                high = term.astype(jnp.bfloat16)
+                term = term - high.astype(jnp.float32)
+                mid = term.astype(jnp.bfloat16)
+                low = (term - mid.astype(jnp.float32)).astype(jnp.bfloat16)
+                parts[pl.ds((e - first + i) * side, side), :] = jnp.concatenate(
+                    [high, mid, low], axis=1
+                )
+        product = jnp.dot(parts[...], right[...], preferred_element_type=jnp.float32)
+        full[pl.ds(first * side, GROUP * side), :] = product
+        squares = (product * product).reshape(GROUP, side // 8, 8, width)
+        sums[pl.ds(first * 8, GROUP * 8), :] = jnp.sum(squares, axis=1).reshape(GROUP * 8, width)
+    total = sums[pl.ds(0, batch, stride=8), :]
+    for s in range(1, 8):
+        total = total + sums[pl.ds(s, batch, stride=8), :]
+    mean = jnp.sum(total, axis=1, keepdims=True) / (side * width)
+    mean_sq[...] = jnp.broadcast_to(mean, (batch, width))
+    scale = jnp.broadcast_to(lax.rsqrt(mean + 1e-06), (batch, width))
+    for k in range(len(outs)):
+        base = lax.bitwise_xor(here, k) * rows
+        for r in range(rows):
+            values = full[pl.ds(base + r, batch, stride=side), :]
+            outs[k][:, r * width : (r + 1) * width] = (values * scale).astype(jnp.bfloat16)
+
+
+def precondition(spot, own, other, left, right, quads):
+    count, half, width = own.shape
+    side = 2 * half
+    rows = half // quads
+    batch = min(STEP, count)
+    gradient_spec = pl.BlockSpec((batch, half, width), lambda i, s: (i, 0, 0))
+    return pl.pallas_call(
+        functools.partial(precondition_kernel, rows),
+        grid_spec=pltpu.PrefetchScalarGridSpec(
+            num_scalar_prefetch=1,
+            grid=(count // batch,),
+            in_specs=[
+                gradient_spec,
+                gradient_spec,
+                pl.BlockSpec((side, side), lambda i, s: (0, 0)),
+                pl.BlockSpec((3 * width, width), lambda i, s: (0, 0)),
+            ],
+            out_specs=[pl.BlockSpec((batch, rows * width), lambda i, s: (i, 0))] * quads
+            + [pl.BlockSpec((batch, width), lambda i, s: (i, 0))],
+            scratch_shapes=[
+                pltpu.VMEM((batch * side, width), jnp.float32),
+                pltpu.VMEM((batch * 8, width), jnp.float32),
+                pltpu.VMEM((GROUP * side, 3 * width), jnp.bfloat16),
+            ],
+        ),
+        out_shape=[jax.ShapeDtypeStruct((count, rows * width), jnp.bfloat16)] * quads
+        + [jax.ShapeDtypeStruct((count, width), jnp.float32)],
+        compiler_params=pltpu.CompilerParams(vmem_limit_bytes=VMEM_BYTES),
+        cost_estimate=pl.CostEstimate(
+            flops=2 * count * side * side * width * 4,
+            bytes_accessed=count * half * width * 6,
+            transcendentals=0,
+        ),
+        name="precondition",
+    )(spot, own, other, left, right)
+
+
+def tiles_kernel(quads, reach, slots, spot, targets, *rest):
+    owners = 2 * quads
+    outs = quads * reach * 2
+    inputs, sums, (cluster,) = rest[: -outs - 1], rest[-outs - 1 : -1], rest[-1:]
+    pieces = len(inputs) // owners
+    here, side, core = spot[0], spot[1], spot[2]
+    block = owners * slots
+    count = targets.shape[2]
+    depth = inputs[0].shape[1]
+
+    @pl.when(pl.program_id(0) == 0)
+    def _():
+        for ref in sums:
+            ref[...] = jnp.zeros_like(ref)
+
+    slot_of = lax.broadcasted_iota(jnp.int32, (block, count), 0)
+    for source in range(owners):
+        k, m = source % quads, source // quads
+        producer = 2 * lax.bitwise_xor(here, k) + lax.bitwise_xor(side, m)
+        placing = (slot_of == targets[producer]).astype(jnp.bfloat16)
+        values = jnp.concatenate([r[...] for r in inputs[source * pieces : (source + 1) * pieces]])
+        placed = jnp.dot(placing, values, preferred_element_type=jnp.float32).astype(jnp.bfloat16)
+        cluster[:, producer] = placed.reshape(owners, slots, depth)
+    for k in range(quads):
+        owner = 2 * lax.bitwise_xor(here, k) + side
+        mine = cluster[owner].reshape(block, depth)
+        for j in range(reach):
+            ahead = cluster[lax.rem(owner + j + 1, owners)].reshape(block, depth)
+            product = lax.dot_general(
+                ahead, mine, (((1,), (1,)), ((), ())), preferred_element_type=jnp.float32
+            )
+            keep, send = sums[2 * (k * reach + j)], sums[2 * (k * reach + j) + 1]
+
+            @pl.when(core == 0)
+            def _():
+                keep[...] += product[: block // 2]
+                send[...] += product[block // 2 :]
+
+            @pl.when(core != 0)
+            def _():
+                send[...] += product[: block // 2]
+                keep[...] += product[block // 2 :]
+
+
+def partial_tiles(spot, targets, pieces, quads, reach, slots):
+    owners = 2 * quads
+    block = owners * slots
+    count = targets.shape[2]
+    features = pieces[0].shape[1]
+    depth = min(512, features)
+    in_specs = [pl.BlockSpec(targets.shape, lambda i, s: (0, 0, 0))]
+    in_specs += [pl.BlockSpec((p.shape[0], depth), lambda i, s: (0, i)) for p in pieces]
+    outs = quads * reach * 2
+    return pl.pallas_call(
+        functools.partial(tiles_kernel, quads, reach, slots),
+        grid_spec=pltpu.PrefetchScalarGridSpec(
+            num_scalar_prefetch=1,
+            grid=(features // depth,),
+            in_specs=in_specs,
+            out_specs=[pl.BlockSpec((block // 2, block), lambda i, s: (0, 0))] * outs,
+            scratch_shapes=[pltpu.VMEM((owners, owners, slots, depth), jnp.bfloat16)],
+        ),
+        out_shape=[jax.ShapeDtypeStruct((block // 2, block), jnp.float32)] * outs,
+        compiler_params=pltpu.CompilerParams(vmem_limit_bytes=VMEM_BYTES),
+        cost_estimate=pl.CostEstimate(
+            flops=2 * features * block * (owners * count + quads * reach * block),
+            bytes_accessed=owners * count * features * 2 + outs * block * block * 2,
+            transcendentals=0,
+        ),
+        name="partial_tiles",
+    )(spot, targets, *pieces)
+
+
+def split_plan(gradients, owner_of, pair_flags, left_factor, right_factor):
+    count, half, width = gradients.shape
+    feat = 2 * half * width
+    owners = lax.axis_size("blk")
+    quads = owners // 2
+    reach = pair_flags.shape[1]
+    slots = 3 * count // (2 * owners)
+    block = owners * slots
+    index = lax.axis_index("blk")
+    core = lax.axis_index("dim")
+    here, side = index // 2, index % 2
+    spot = jnp.stack([here, side, core]).astype(jnp.int32)
+
+    def across(x):
+        return lax.ppermute(x, "dim", [(0, 1), (1, 0)])
+
+    def along(x, k):
+        return lax.ppermute(x, "blk", [(i, i ^ (2 * k)) for i in range(owners)])
+
+    def beside(x):
+        return lax.ppermute(x, "blk", [(i, i ^ 1) for i in range(owners)])
+
+    swapped = jnp.concatenate([left_factor[half:], left_factor[:half]], axis=0)
+    swapped = jnp.concatenate([swapped[:, half:], swapped[:, :half]], axis=1)
+    left = jnp.where(core == 0, left_factor, swapped)
+    right = jnp.concatenate([right_factor] * 3, axis=0)
+
+    target = slot_targets(owner_of, owners, slots)
+    targets = lax.all_gather(target, "blk", axis=0, tiled=True).reshape(owners, 1, count)
+
+    bounds = [0]
+    for part in CHUNKS:
+        bounds.append(bounds[-1] + part * count // sum(CHUNKS))
+    chunks = [gradients[a:b] for a, b in zip(bounds[:-1], bounds[1:])]
+    others = [across(chunk) for chunk in chunks]
+    pieces = [[] for _ in range(owners)]
+    means = []
+    for chunk, other in zip(chunks, others):
+        *parts, mean_sq = precondition(spot, chunk, other, left, right, quads)
+        means.append(mean_sq[:, 0])
+        got = [parts[0]] + [None] * (quads - 1)
+        for k in reversed(range(1, quads)):
+            got[k] = along(parts[k], k)
+        for k in range(quads):
+            pieces[k].append(got[k])
+            pieces[quads + k].append(beside(got[k]))
+
+    influence = jnp.log1p(jnp.concatenate(means)).astype(jnp.bfloat16)
+    influences = lax.all_gather(influence, "blk", axis=0, tiled=True).reshape(owners, count)
+    local = targets[:, 0] - index * slots
+    chosen = local[:, None, :] == jnp.arange(slots, dtype=jnp.int32)[None, :, None]
+    self_influence = jnp.sum(
+        jnp.where(chosen, influences[:, None, :].astype(jnp.float32), 0.0), axis=2
+    ).astype(jnp.bfloat16)
+
+    sums = partial_tiles(
+        spot, targets, [p for group in pieces for p in group], quads, reach, slots
+    )
+    flags = lax.dynamic_index_in_dim(pair_flags, index, 0, keepdims=False).astype(jnp.float32)
+    ahead, behind = [], []
+    for j in range(reach):
+        total = [None] * quads
+        for k in reversed(range(quads)):
+            at = 2 * (k * reach + j)
+            total[k] = sums[at] + across(sums[at + 1])
+        bit = 1
+        while bit < quads:
+            for k in range(0, quads, 2 * bit):
+                total[k] = total[k] + along(total[k + bit], bit)
+            bit *= 2
+        tile = (total[0] * (flags[j] * feat ** (-0.5))).astype(jnp.bfloat16)
+        ahead.append(tile)
+        turned = tile.T.reshape(2, block // 2, block // 2)
+        straight = lax.dynamic_index_in_dim(turned, core, 0, keepdims=False)
+        crossed = lax.dynamic_index_in_dim(turned, 1 - core, 0, keepdims=False)
+        by = j + 1
+        straight = from_behind(straight, "blk", by)
+        crossed = lax.ppermute(
+            crossed,
+            ("blk", "dim"),
+            [(2 * i + c, 2 * ((i + by) % owners) + 1 - c) for i in range(owners) for c in range(2)],
+        )
+        behind.append(
+            jnp.where(
+                core == 0,
+                jnp.concatenate([straight, crossed], axis=1),
+                jnp.concatenate([crossed, straight], axis=1),
+            )
+        )
+    tiles = jnp.stack(ahead + behind).swapaxes(1, 2)
+    return (tiles, self_influence.reshape(block))
+
+
 def solution(mesh):
+    owners = mesh.shape["blk"]
+
+    def per_device(gradients, owner_of, pair_flags, left_factor, right_factor):
+        block = 3 * gradients.shape[0] // 2
+        partial_bytes = 4 * owners * pair_flags.shape[1] * block * block // 2
+        quads = owners // 2
+        fits = partial_bytes <= PARTIAL_BYTES and quads & (quads - 1) == 0
+        plan = split_plan if fits and gradients.shape[1] % quads == 0 else ring_plan
+        return plan(gradients, owner_of, pair_flags, left_factor, right_factor)
+
     return jax.shard_map(
         per_device,
         mesh=mesh,

time: 818 us -> 329 us (0.40)
  waiting for transfers between devices: 571 us -> 80.9 us
  blocking collectives: 157 us -> 64.4 us
  starting transfers between devices: 7.27 us -> 96.8 us
  Pallas kernels: 0 us -> 59.8 us
  matrix products: 45.2 us -> 0 us
  between operations: 16 us -> 3.08 us
    ppermute x6 -> x3, waiting for transfers between devices: 386 us -> 11.2 us  [from_behind(): lax.ppermute(shard, axis, [(i, (i + by) % peers) for i in range(peers)])]
    reduce_scatter x1 -> x0, waiting for transfers between devices: 163 us -> none  [per_device(): lax.psum_scatter(jnp.stack(partials), 'dim', scatter_dimension=2, tiled=T...]
    all_to_all x2 -> x0, blocking collectives: 154 us -> none  [the longest x1 143 us: per_device(): lax.all_to_all(outgoing, 'blk', split_axis=0, concat_axis=0, tiled=True)]
    ppermute x0 -> x56, starting transfers between devices: none -> 89.7 us  [the longest x21 52.8 us: along(): return lax.ppermute(x, 'blk', [(i, i ^ 2 * k) for i in range(owners)])]
    ppermute x0 -> x56, waiting for transfers between devices: none -> 69.7 us  [the longest x21 50.2 us: along(): return lax.ppermute(x, 'blk', [(i, i ^ 2 * k) for i in range(owners)])]
    all_gather x0 -> x2, blocking collectives: none -> 64.4 us  [the longest x1 47.8 us: split_plan(): lax.all_gather(target, 'blk', axis=0, tiled=True).reshape(owners, 1, count)]
    pallas_call x0 -> x5, Pallas kernels: none -> 59.8 us  [the longest x1 31.5 us: partial_tiles(): pl.pallas_call(functools.partial(tiles_kernel, quads, reach, slots), grid...]
    dot_general x8 -> x0, matrix products: 45.2 us -> none  [the longest x3 24.6 us: per_device(): product = jnp.dot(own, ahead.T, preferred_element_type=jnp.float32)]
  transfers between devices with their start and end apart: 8 -> 59, of which waited for: 4 -> 17; matrix products, arithmetic and copies ran while one was open for 3% -> 6% of each run, Pallas kernels for 0% -> 9%
where the time goes in v1:
time: 329 us
  starting transfers between devices  96.8 us (29%)
  waiting for transfers between devices  80.9 us (25%)
  blocking collectives  64.4 us (20%)
  Pallas kernels  59.8 us (18%)
  other arithmetic  15.3 us (5%)
  local copies, waits for them, and re-layouts  8.29 us (3%)
    ppermute x21, starting transfers between devices, along(): return lax.ppermute(x, 'blk', [(i, i ^ 2 * k) for i in range(owners)])  52.8 us
    ppermute x21, waiting for transfers between devices, along(): return lax.ppermute(x, 'blk', [(i, i ^ 2 * k) for i in range(owners)])  50.2 us
    all_gather x1, blocking collectives, split_plan(): lax.all_gather(target, 'blk', axis=0, tiled=True).reshape(owners, 1, count)  47.8 us
    pallas_call x1, Pallas kernels, partial_tiles(): pl.pallas_call(functools.partial(tiles_kernel, quads, reach, slots), grid...  31.5 us
    pallas_call x4, Pallas kernels, precondition(): pl.pallas_call(functools.partial(precondition_kernel, rows), grid_spec=pl...  28.2 us
    ppermute x16, starting transfers between devices, across(): return lax.ppermute(x, 'dim', [(0, 1), (1, 0)])  18.9 us
    all_gather x1, blocking collectives, split_plan(): lax.all_gather(influence, 'blk', axis=0, tiled=True).reshape(owners, count)  16.5 us
    ppermute x16, starting transfers between devices, beside(): return lax.ppermute(x, 'blk', [(i, i ^ 1) for i in range(owners)])  14.9 us
  transfers between devices with their start and end apart: 59, of which 17 were waited for; matrix products, arithmetic and copies ran while one was open for 6% of the time, Pallas kernels for 9%

profile of v1, /device:TPU:5, one launch (start us, length us, event | category | flops | bytes accessed | tf_op | source)
XLA Modules:
  0.0 328.5 jit_solution(15944736714045371702)
XLA Ops:
  0.6 4.1 %fusion.9 = (bf16[64,64,128]{2,1,0:T(8,128)(2,1)}, bf16[64,64,128]{2,1,0:T(8,128)(2,1)S(1)}, bf16[64,64,128]{2,1,0:T(8,128)(2,1)S(1)}, bf16[64,64,128]{2,1,0:T(8,128)(2,1)S(1)}) fusion(bf16[256,64,128]{2,1,0:T(8,128)(2,1)} %param.5), kind=kLoop, calls=%fused_computation.49 | loop fusion | bytes 8388608 | tf_op jit(solution)/shard_map/slice | solution.py:266
  8.9 7.0 %precondition.7 = (bf16[64,2048]{1,0:T(8,128)(2,1)}, bf16[64,2048]{1,0:T(8,128)(2,1)}, bf16[64,2048]{1,0:T(8,128)(2,1)}, bf16[64,2048]{1,0:T(8,128)(2,1)}, f32[64,128]{1,0:T(8,128)}) custom-call(s32[3]{0:T(128)} %pad_add_fusion.spot, bf16[64,64,128]{2,1,0:T(8,128)(2,1)} %get-tuple-element.96.own, bf16[64,64,128]{2,1,0:T(8,128)(2,1)} %collective-permute-done.3.other, ...), custom_call_target="tpu_custom_call" | custom-call | flops 1073741824 | bytes 3145728 | tf_op jit(solution)/shard_map/precondition/pallas_call | solution.py:129
  19.6 7.1 %precondition.5 = (bf16[64,2048]{1,0:T(8,128)(2,1)}, bf16[64,2048]{1,0:T(8,128)(2,1)}, bf16[64,2048]{1,0:T(8,128)(2,1)}, bf16[64,2048]{1,0:T(8,128)(2,1)}, f32[64,128]{1,0:T(8,128)}) custom-call(s32[3]{0:T(128)} %pad_add_fusion.spot, bf16[64,64,128]{2,1,0:T(8,128)(2,1)} %copy-done.2, bf16[64,64,128]{2,1,0:T(8,128)(2,1)} %collective-permute-done.1.other, ...), custom_call_target="tpu_custom_call" | custom-call | flops 1073741824 | bytes 3145728 | tf_op jit(solution)/shard_map/precondition/pallas_call | solution.py:129
  30.5 8.1 %collective-permute-start.13 = (bf16[64,2048]{1,0:T(8,128)(2,1)}, bf16[64,2048]{1,0:T(8,128)(2,1)S(1)}, u32[]{:S(2)}, u32[]{:S(2)}) collective-permute-start(bf16[64,2048]{1,0:T(8,128)(2,1)} %get-tuple-element.59), channel_id=1, source_target_pairs={{0,12},{2,14},{4,8},{6,10},{8,4},{10,6},{12,0},{14,2},{1,13},{3,15... | collective-permute-start | bytes 786440 | tf_op jit(solution)/shard_map/ppermute | solution.py:250
  38.9 7.0 %precondition.4 = (bf16[64,2048]{1,0:T(8,128)(2,1)}, bf16[64,2048]{1,0:T(8,128)(2,1)}, bf16[64,2048]{1,0:T(8,128)(2,1)}, bf16[64,2048]{1,0:T(8,128)(2,1)}, f32[64,128]{1,0:T(8,128)}) custom-call(s32[3]{0:T(128)} %pad_add_fusion.spot, bf16[64,64,128]{2,1,0:T(8,128)(2,1)} %copy-done.1, bf16[64,64,128]{2,1,0:T(8,128)(2,1)} %collective-permute-done.other, ...), custom_call_target="tpu_custom_call" | custom-call | flops 1073741824 | bytes 3145728 | tf_op jit(solution)/shard_map/precondition/pallas_call | solution.py:129
  45.9 7.1 %precondition.6 = (bf16[64,2048]{1,0:T(8,128)(2,1)}, bf16[64,2048]{1,0:T(8,128)(2,1)}, bf16[64,2048]{1,0:T(8,128)(2,1)}, bf16[64,2048]{1,0:T(8,128)(2,1)}, f32[64,128]{1,0:T(8,128)}) custom-call(s32[3]{0:T(128)} %pad_add_fusion.spot, bf16[64,64,128]{2,1,0:T(8,128)(2,1)} %copy-done, bf16[64,64,128]{2,1,0:T(8,128)(2,1)} %collective-permute-done.2.other, ...), custom_call_target="tpu_custom_call" | custom-call | flops 1073741824 | bytes 3145728 | tf_op jit(solution)/shard_map/precondition/pallas_call | solution.py:129
  53.0 4.3 %collective-permute-start.4 = (bf16[64,2048]{1,0:T(8,128)(2,1)}, bf16[64,2048]{1,0:T(8,128)(2,1)S(1)}, u32[]{:S(2)}, u32[]{:S(2)}) collective-permute-start(bf16[64,2048]{1,0:T(8,128)(2,1)} %get-tuple-element.50), channel_id=1, source_target_pairs={{0,4},{2,6},{4,0},{6,2},{8,12},{10,14},{12,8},{14,10},{1,5},{3,7},... | collective-permute-start | bytes 786440 | tf_op jit(solution)/shard_map/ppermute | solution.py:250
  57.2 12.3 %collective-permute-start.8 = (bf16[64,2048]{1,0:T(8,128)(2,1)}, bf16[64,2048]{1,0:T(8,128)(2,1)S(1)}, u32[]{:S(2)}, u32[]{:S(2)}) collective-permute-start(bf16[64,2048]{1,0:T(8,128)(2,1)} %get-tuple-element.54), channel_id=1, source_target_pairs={{0,8},{2,10},{4,12},{6,14},{8,0},{10,2},{12,4},{14,6},{1,9},{3,11}... | collective-permute-start | bytes 786440 | tf_op jit(solution)/shard_map/ppermute | solution.py:250
  74.9 12.3 %collective-permute-start.14 = (bf16[64,2048]{1,0:T(8,128)(2,1)}, bf16[64,2048]{1,0:T(8,128)(2,1)}, u32[]{:S(2)}, u32[]{:S(2)}) collective-permute-start(bf16[64,2048]{1,0:T(8,128)(2,1)} %get-tuple-element.60), channel_id=1, source_target_pairs={{0,12},{2,14},{4,8},{6,10},{8,4},{10,6},{12,0},{14,2},{1,13},{3,15... | collective-permute-start | bytes 786440 | tf_op jit(solution)/shard_map/ppermute | solution.py:250
  90.9 15.0 %collective-permute-done.10.rest_10_ = bf16[64,2048]{1,0:T(8,128)(2,1)S(1)} collective-permute-done((bf16[64,2048]{1,0:T(8,128)(2,1)}, bf16[64,2048]{1,0:T(8,128)(2,1)S(1)}, u32[]{:S(2)}, u32[]{:S(2)}) %collective-permute-start.10) | collective-permute-done | bytes 262176 | tf_op jit(solution)/shard_map/ppermute | solution.py:250
  118.8 4.3 %collective-permute-done.29.rest_29_ = bf16[64,2048]{1,0:T(8,128)(2,1)S(1)} collective-permute-done((bf16[64,2048]{1,0:T(8,128)(2,1)S(1)}, bf16[64,2048]{1,0:T(8,128)(2,1)S(1)}, u32[]{:S(2)}, u32[]{:S(2)}) %collective-permute-start.29) | collective-permute-done | bytes 262176 | tf_op jit(solution)/shard_map/ppermute | solution.py:253
  124.4 4.4 %collective-permute-done.20.rest_20_ = bf16[64,2048]{1,0:T(8,128)(2,1)S(1)} collective-permute-done((bf16[64,2048]{1,0:T(8,128)(2,1)S(1)}, bf16[64,2048]{1,0:T(8,128)(2,1)S(1)}, u32[]{:S(2)}, u32[]{:S(2)}) %collective-permute-start.20) | collective-permute-done | bytes 262176 | tf_op jit(solution)/shard_map/ppermute | solution.py:253
  132.4 47.8 %all-gather.targets = s32[8,1,256]{2,1,0:T(1,128)S(1)} all-gather(s32[1,1,256]{2,1,0:T(1,128)S(1)} %bitcast.76), channel_id=1, replica_groups=mesh['groups'=2,'blk'=8,'dim'=2] {'blk'}, dimensions={0}, use_global_device_ids=true | all-gather | bytes 9216 | tf_op jit(solution)/shard_map/all_gather | solution.py:261
  180.8 31.5 %partial_tiles.1 = (f32[192,384]{1,0:T(8,128)}, f32[192,384]{1,0:T(8,128)}, f32[192,384]{1,0:T(8,128)}, f32[192,384]{1,0:T(8,128)}, f32[192,384]{1,0:T(8,128)}, ...) custom-call(s32[3]{0:T(128)} %pad_add_fusion.spot, ...), custom_call_target="tpu_custom_call" | custom-call | flops 10468982784 | bytes 15466496 | tf_op jit(solution)/shard_map/partial_tiles/pallas_call | solution.py:213
  212.4 8.4 %collective-permute-start.33 = (f32[192,384]{1,0:T(8,128)}, f32[192,384]{1,0:T(8,128)S(1)}, u32[]{:S(2)}, u32[]{:S(2)}) collective-permute-start(f32[192,384]{1,0:T(8,128)} %get-tuple-element.65), channel_id=1, source_target_pairs={{0,1},{1,0},{2,3},{3,2},{4,5},{5,4},{6,7},{7,6},{8,9},{9,8},{10,11... | collective-permute-start | bytes 884744 | tf_op jit(solution)/shard_map/ppermute | solution.py:247
  226.5 16.5 %all-gather.1 = bf16[8,1,256]{2,1,0:T(2,128)(2,1)S(1)} all-gather(bf16[1,1,256]{2,1,0:T(2,128)(2,1)S(1)} %reshape.243), channel_id=1, replica_groups=mesh['groups'=2,'blk'=8,'dim'=2] {'blk'}, dimensions={0}, use_global_device_ids=true | all-gather | bytes 4608 | tf_op jit(solution)/shard_map/all_gather | solution.py:281
  244.1 4.2 %collective-permute-start.42 = (f32[192,384]{1,0:T(8,128)}, f32[192,384]{1,0:T(8,128)}, u32[]{:S(2)}, u32[]{:S(2)}) collective-permute-start(f32[192,384]{1,0:T(8,128)} %get-tuple-element.75), channel_id=1, source_target_pairs={{0,1},{1,0},{2,3},{3,2},{4,5},{5,4},{6,7},{7,6},{8,9},{9,8},{10,11... | collective-permute-start | bytes 884744 | tf_op jit(solution)/shard_map/ppermute | solution.py:247
  259.5 10.0 %collective-permute-done.51 = f32[192,384]{1,0:T(8,128)S(1)} collective-permute-done((f32[192,384]{1,0:T(8,128)S(1)}, f32[192,384]{1,0:T(8,128)S(1)}, u32[]{:S(2)}, u32[]{:S(2)}) %collective-permute-start.51) | collective-permute-done | bytes 294944 | tf_op jit(solution)/shard_map/ppermute | solution.py:250
  271.0 4.9 %collective-permute-done.34 = f32[192,384]{1,0:T(8,128)S(1)} collective-permute-done((f32[192,384]{1,0:T(8,128)S(1)}, f32[192,384]{1,0:T(8,128)S(1)}, u32[]{:S(2)}, u32[]{:S(2)}) %collective-permute-start.34) | collective-permute-done | bytes 294944 | tf_op jit(solution)/shard_map/ppermute | solution.py:250
  279.7 10.9 %collective-permute-done.41 = f32[192,384]{1,0:T(8,128)} collective-permute-done((f32[192,384]{1,0:T(8,128)S(1)}, f32[192,384]{1,0:T(8,128)}, u32[]{:S(2)}, u32[]{:S(2)}) %collective-permute-start.41) | collective-permute-done | bytes 294944 | tf_op jit(solution)/shard_map/ppermute | solution.py:250
  297.5 6.2 %collective-permute-start.55 = (bf16[192,192]{1,0:T(8,128)(2,1)S(1)}, bf16[192,192]{1,0:T(8,128)(2,1)S(1)}, u32[]{:S(2)}, u32[]{:S(2)}) collective-permute-start(bf16[192,192]{1,0:T(8,128)(2,1)S(1)} %get-tuple-element.102), channel_id=1, source_target_pairs={{0,4},{2,6},{4,8},{6,10},{8,12},{10,14},{12,0},{14,2},{1,5},{3,7},... | collective-permute-start | bytes 221192 | tf_op jit(solution)/shard_map/ppermute | solution.py:19
  303.7 4.6 %collective-permute-done.52 = f32[192,384]{1,0:T(8,128)S(1)} collective-permute-done((f32[192,384]{1,0:T(8,128)S(1)}, f32[192,384]{1,0:T(8,128)S(1)}, u32[]{:S(2)}, u32[]{:S(2)}) %collective-permute-start.52) | collective-permute-done | bytes 294944 | tf_op jit(solution)/shard_map/ppermute | solution.py:250
  312.4 4.2 %collective-permute-done.58 = bf16[192,192]{1,0:T(8,128)(2,1)S(1)} collective-permute-done((bf16[192,192]{1,0:T(8,128)(2,1)S(1)}, bf16[192,192]{1,0:T(8,128)(2,1)S(1)}, u32[]{:S(2)}, u32[]{:S(2)}) %collective-permute-start.58) | collective-permute-done | bytes 73760 | tf_op jit(solution)/shard_map/ppermute | solution.py:310
  316.6 11.2 %collective-permute-done.57 = bf16[192,192]{1,0:T(8,128)(2,1)S(1)} collective-permute-done((bf16[192,192]{1,0:T(8,128)(2,1)S(1)}, bf16[192,192]{1,0:T(8,128)(2,1)S(1)}, u32[]{:S(2)}, u32[]{:S(2)}) %collective-permute-start.57) | collective-permute-done | bytes 73760 | tf_op jit(solution)/shard_map/ppermute | solution.py:19
  (227 shorter events, 72.1 us)
Async XLA Ops:
  5.6 21.1 %collective-permute-start = (bf16[64,64,128]{2,1,0:T(8,128)(2,1)S(1)}, bf16[64,64,128]{2,1,0:T(8,128)(2,1)}, u32[]{:S(2)}, u32[]{:S(2)}) collective-permute-start(bf16[64,64,128]{2,1,0:T(8,128)(2,1)S(1)} %get-tuple-element.98.own), channel_id=1, source_target_pairs={{0,1},{1,0},{2,3},{3,2},{4,5},{5,4},{6,7},{7,6},{8,9},{9,8},{10,11... | collective-permute-start | bytes 3145736 | tf_op jit(solution)/shard_map/ppermute | solution.py:247
  6.0 21.0 %collective-permute-start.2 = (bf16[64,64,128]{2,1,0:T(8,128)(2,1)S(1)}, bf16[64,64,128]{2,1,0:T(8,128)(2,1)}, u32[]{:S(2)}, u32[]{:S(2)}) collective-permute-start(bf16[64,64,128]{2,1,0:T(8,128)(2,1)S(1)} %get-tuple-element.99.own), channel_id=1, source_target_pairs={{0,1},{1,0},{2,3},{3,2},{4,5},{5,4},{6,7},{7,6},{8,9},{9,8},{10,11... | collective-permute-start | bytes 3145736 | tf_op jit(solution)/shard_map/ppermute | solution.py:247
  26.7 26.3 %collective-permute-start.19 = (bf16[64,2048]{1,0:T(8,128)(2,1)}, bf16[64,2048]{1,0:T(8,128)(2,1)S(1)}, u32[]{:S(2)}, u32[]{:S(2)}) collective-permute-start(bf16[64,2048]{1,0:T(8,128)(2,1)} %get-tuple-element.49.rest_3_), channel_id=1, source_target_pairs={{0,2},{2,0},{4,6},{6,4},{8,10},{10,8},{12,14},{14,12},{1,3},{3,1},... | collective-permute-start | bytes 786440 | tf_op jit(solution)/shard_map/ppermute | solution.py:253
  27.0 30.2 %collective-permute-start.5 = (bf16[64,2048]{1,0:T(8,128)(2,1)}, bf16[64,2048]{1,0:T(8,128)(2,1)S(1)}, u32[]{:S(2)}, u32[]{:S(2)}) collective-permute-start(bf16[64,2048]{1,0:T(8,128)(2,1)} %get-tuple-element.51), channel_id=1, source_target_pairs={{0,4},{2,6},{4,0},{6,2},{8,12},{10,14},{12,8},{14,10},{1,5},{3,7},... | collective-permute-start | bytes 786440 | tf_op jit(solution)/shard_map/ppermute | solution.py:250
  28.8 40.7 %collective-permute-start.9 = (bf16[64,2048]{1,0:T(8,128)(2,1)}, bf16[64,2048]{1,0:T(8,128)(2,1)S(1)}, u32[]{:S(2)}, u32[]{:S(2)}) collective-permute-start(bf16[64,2048]{1,0:T(8,128)(2,1)} %get-tuple-element.55), channel_id=1, source_target_pairs={{0,8},{2,10},{4,12},{6,14},{8,0},{10,2},{12,4},{14,6},{1,9},{3,11}... | collective-permute-start | bytes 786440 | tf_op jit(solution)/shard_map/ppermute | solution.py:250
  30.5 40.2 %collective-permute-start.13 = (bf16[64,2048]{1,0:T(8,128)(2,1)}, bf16[64,2048]{1,0:T(8,128)(2,1)S(1)}, u32[]{:S(2)}, u32[]{:S(2)}) collective-permute-start(bf16[64,2048]{1,0:T(8,128)(2,1)} %get-tuple-element.59), channel_id=1, source_target_pairs={{0,12},{2,14},{4,8},{6,10},{8,4},{10,6},{12,0},{14,2},{1,13},{3,15... | collective-permute-start | bytes 786440 | tf_op jit(solution)/shard_map/ppermute | solution.py:250
  38.6 33.4 %collective-permute-start.17 = (bf16[64,2048]{1,0:T(8,128)(2,1)}, bf16[64,2048]{1,0:T(8,128)(2,1)S(1)}, u32[]{:S(2)}, u32[]{:S(2)}) collective-permute-start(bf16[64,2048]{1,0:T(8,128)(2,1)} %get-tuple-element.47.rest_1_), channel_id=1, source_target_pairs={{0,2},{2,0},{4,6},{6,4},{8,10},{10,8},{12,14},{14,12},{1,3},{3,1},... | collective-permute-start | bytes 786440 | tf_op jit(solution)/shard_map/ppermute | solution.py:253
  72.3 33.6 %collective-permute-start.10 = (bf16[64,2048]{1,0:T(8,128)(2,1)}, bf16[64,2048]{1,0:T(8,128)(2,1)S(1)}, u32[]{:S(2)}, u32[]{:S(2)}) collective-permute-start(bf16[64,2048]{1,0:T(8,128)(2,1)} %get-tuple-element.56), channel_id=1, source_target_pairs={{0,8},{2,10},{4,12},{6,14},{8,0},{10,2},{12,4},{14,6},{1,9},{3,11}... | collective-permute-start | bytes 786440 | tf_op jit(solution)/shard_map/ppermute | solution.py:250
  74.9 32.3 %collective-permute-start.14 = (bf16[64,2048]{1,0:T(8,128)(2,1)}, bf16[64,2048]{1,0:T(8,128)(2,1)}, u32[]{:S(2)}, u32[]{:S(2)}) collective-permute-start(bf16[64,2048]{1,0:T(8,128)(2,1)} %get-tuple-element.60), channel_id=1, source_target_pairs={{0,12},{2,14},{4,8},{6,10},{8,4},{10,6},{12,0},{14,2},{1,13},{3,15... | collective-permute-start | bytes 786440 | tf_op jit(solution)/shard_map/ppermute | solution.py:250
  87.2 20.2 %collective-permute-start.18 = (bf16[64,2048]{1,0:T(8,128)(2,1)}, bf16[64,2048]{1,0:T(8,128)(2,1)}, u32[]{:S(2)}, u32[]{:S(2)}) collective-permute-start(bf16[64,2048]{1,0:T(8,128)(2,1)} %get-tuple-element.48.rest_2_), channel_id=1, source_target_pairs={{0,2},{2,0},{4,6},{6,4},{8,10},{10,8},{12,14},{14,12},{1,3},{3,1},... | collective-permute-start | bytes 786440 | tf_op jit(solution)/shard_map/ppermute | solution.py:253
  111.7 68.6 %collective-permute-start.24 = (bf16[64,2048]{1,0:T(8,128)(2,1)S(1)}, bf16[64,2048]{1,0:T(8,128)(2,1)}, u32[]{:S(2)}, u32[]{:S(2)}) collective-permute-start(bf16[64,2048]{1,0:T(8,128)(2,1)S(1)} %collective-permute-done.8.rest_8_), channel_id=1, source_target_pairs={{0,2},{2,0},{4,6},{6,4},{8,10},{10,8},{12,14},{14,12},{1,3},{3,1},... | collective-permute-start | bytes 786440 | tf_op jit(solution)/shard_map/ppermute | solution.py:253
  114.2 66.1 %collective-permute-start.28 = (bf16[64,2048]{1,0:T(8,128)(2,1)S(1)}, bf16[64,2048]{1,0:T(8,128)(2,1)}, u32[]{:S(2)}, u32[]{:S(2)}) collective-permute-start(bf16[64,2048]{1,0:T(8,128)(2,1)S(1)} %collective-permute-done.12.rest_12_), channel_id=1, source_target_pairs={{0,2},{2,0},{4,6},{6,4},{8,10},{10,8},{12,14},{14,12},{1,3},{3,1},... | collective-permute-start | bytes 786440 | tf_op jit(solution)/shard_map/ppermute | solution.py:253
  117.5 62.8 %collective-permute-start.22 = (bf16[64,2048]{1,0:T(8,128)(2,1)S(1)}, bf16[64,2048]{1,0:T(8,128)(2,1)}, u32[]{:S(2)}, u32[]{:S(2)}) collective-permute-start(bf16[64,2048]{1,0:T(8,128)(2,1)S(1)} %collective-permute-done.6.rest_6_), channel_id=1, source_target_pairs={{0,2},{2,0},{4,6},{6,4},{8,10},{10,8},{12,14},{14,12},{1,3},{3,1},... | collective-permute-start | bytes 786440 | tf_op jit(solution)/shard_map/ppermute | solution.py:253
  123.1 57.2 %collective-permute-start.26 = (bf16[64,2048]{1,0:T(8,128)(2,1)S(1)}, bf16[64,2048]{1,0:T(8,128)(2,1)}, u32[]{:S(2)}, u32[]{:S(2)}) collective-permute-start(bf16[64,2048]{1,0:T(8,128)(2,1)S(1)} %collective-permute-done.10.rest_10_), channel_id=1, source_target_pairs={{0,2},{2,0},{4,6},{6,4},{8,10},{10,8},{12,14},{14,12},{1,3},{3,1},... | collective-permute-start | bytes 786440 | tf_op jit(solution)/shard_map/ppermute | solution.py:253
  128.8 51.6 %collective-permute-start.30 = (bf16[64,2048]{1,0:T(8,128)(2,1)}, bf16[64,2048]{1,0:T(8,128)(2,1)}, u32[]{:S(2)}, u32[]{:S(2)}) collective-permute-start(bf16[64,2048]{1,0:T(8,128)(2,1)} %collective-permute-done.14.rest_14_), channel_id=1, source_target_pairs={{0,2},{2,0},{4,6},{6,4},{8,10},{10,8},{12,14},{14,12},{1,3},{3,1},... | collective-permute-start | bytes 786440 | tf_op jit(solution)/shard_map/ppermute | solution.py:253
  221.5 22.5 %collective-permute-start.40 = (f32[192,384]{1,0:T(8,128)}, f32[192,384]{1,0:T(8,128)S(1)}, u32[]{:S(2)}, u32[]{:S(2)}) collective-permute-start(f32[192,384]{1,0:T(8,128)} %get-tuple-element.73), channel_id=1, source_target_pairs={{0,1},{1,0},{2,3},{3,2},{4,5},{5,4},{6,7},{7,6},{8,9},{9,8},{10,11... | collective-permute-start | bytes 884744 | tf_op jit(solution)/shard_map/ppermute | solution.py:247
  221.7 26.6 %collective-permute-start.47 = (f32[192,384]{1,0:T(8,128)}, f32[192,384]{1,0:T(8,128)S(1)}, u32[]{:S(2)}, u32[]{:S(2)}) collective-permute-start(f32[192,384]{1,0:T(8,128)} %get-tuple-element.81), channel_id=1, source_target_pairs={{0,1},{1,0},{2,3},{3,2},{4,5},{5,4},{6,7},{7,6},{8,9},{9,8},{10,11... | collective-permute-start | bytes 884744 | tf_op jit(solution)/shard_map/ppermute | solution.py:247
  222.6 29.7 %collective-permute-start.35 = (f32[192,384]{1,0:T(8,128)}, f32[192,384]{1,0:T(8,128)}, u32[]{:S(2)}, u32[]{:S(2)}) collective-permute-start(f32[192,384]{1,0:T(8,128)} %get-tuple-element.67), channel_id=1, source_target_pairs={{0,1},{1,0},{2,3},{3,2},{4,5},{5,4},{6,7},{7,6},{8,9},{9,8},{10,11... | collective-permute-start | bytes 884744 | tf_op jit(solution)/shard_map/ppermute | solution.py:247
  224.0 28.1 %collective-permute-start.50 = (f32[192,384]{1,0:T(8,128)}, f32[192,384]{1,0:T(8,128)S(1)}, u32[]{:S(2)}, u32[]{:S(2)}) collective-permute-start(f32[192,384]{1,0:T(8,128)} %get-tuple-element.85), channel_id=1, source_target_pairs={{0,1},{1,0},{2,3},{3,2},{4,5},{5,4},{6,7},{7,6},{8,9},{9,8},{10,11... | collective-permute-start | bytes 884744 | tf_op jit(solution)/shard_map/ppermute | solution.py:247
  224.2 28.6 %collective-permute-start.37 = (f32[192,384]{1,0:T(8,128)S(1)}, f32[192,384]{1,0:T(8,128)}, u32[]{:S(2)}, u32[]{:S(2)}) collective-permute-start(f32[192,384]{1,0:T(8,128)S(1)} %add.93), channel_id=1, source_target_pairs={{0,4},{2,6},{4,0},{6,2},{8,12},{10,14},{12,8},{14,10},{1,5},{3,7},... | collective-permute-start | bytes 884744 | tf_op jit(solution)/shard_map/ppermute | solution.py:250
  255.5 20.3 %collective-permute-start.34 = (f32[192,384]{1,0:T(8,128)S(1)}, f32[192,384]{1,0:T(8,128)S(1)}, u32[]{:S(2)}, u32[]{:S(2)}) collective-permute-start(f32[192,384]{1,0:T(8,128)S(1)} %add.90), channel_id=1, source_target_pairs={{0,4},{2,6},{4,0},{6,2},{8,12},{10,14},{12,8},{14,10},{1,5},{3,7},... | collective-permute-start | bytes 884744 | tf_op jit(solution)/shard_map/ppermute | solution.py:250
  269.5 28.0 %collective-permute-start.46 = (f32[192,384]{1,0:T(8,128)}, f32[192,384]{1,0:T(8,128)S(1)}, u32[]{:S(2)}, u32[]{:S(2)}) collective-permute-start(f32[192,384]{1,0:T(8,128)} %get-tuple-element.79), channel_id=1, source_target_pairs={{0,1},{1,0},{2,3},{3,2},{4,5},{5,4},{6,7},{7,6},{8,9},{9,8},{10,11... | collective-permute-start | bytes 884744 | tf_op jit(solution)/shard_map/ppermute | solution.py:247
  275.8 27.8 %collective-permute-start.48 = (f32[192,384]{1,0:T(8,128)S(1)}, f32[192,384]{1,0:T(8,128)S(1)}, u32[]{:S(2)}, u32[]{:S(2)}) collective-permute-start(f32[192,384]{1,0:T(8,128)S(1)} %add.105), channel_id=1, source_target_pairs={{0,4},{2,6},{4,0},{6,2},{8,12},{10,14},{12,8},{14,10},{1,5},{3,7},... | collective-permute-start | bytes 884744 | tf_op jit(solution)/shard_map/ppermute | solution.py:250
  278.2 30.1 %collective-permute-start.52 = (f32[192,384]{1,0:T(8,128)S(1)}, f32[192,384]{1,0:T(8,128)S(1)}, u32[]{:S(2)}, u32[]{:S(2)}) collective-permute-start(f32[192,384]{1,0:T(8,128)S(1)} %add_add_fusion), channel_id=1, source_target_pairs={{0,8},{2,10},{4,12},{6,14},{8,0},{10,2},{12,4},{14,6},{1,9},{3,11}... | collective-permute-start | bytes 884744 | tf_op jit(solution)/shard_map/ppermute | solution.py:250
  (73 other events, 2579.3 us)

commit v2 on v1

--- a/solution.py
+++ b/solution.py
@@ -8,7 +8,9 @@
 from jax.sharding import PartitionSpec as P
 
 PARTIAL_BYTES = 16 * 2**20
-CHUNKS = (1, 1, 1, 1)
+FIRST = 64
+SLICES = (3, 3, 2)
+PLACE_WIDTH = 256
 GROUP = 8
 STEP = 32
 VMEM_BYTES = 56 * 2**20
@@ -83,7 +85,12 @@
     return (summed, self_influence)
 
 
-def precondition_kernel(rows, spot, own, other, left, right, *rest):
+def after(values, *deps):
+    return list(lax.optimization_barrier((tuple(values), deps))[0])
+
+
+def precondition_kernel(widths, spot, own, other, left, right, *rest):
+    quads = len(rest[:-4]) // len(widths)
     outs, mean_sq, full, sums, parts = rest[:-4], rest[-4], rest[-3], rest[-2], rest[-1]
     here = spot[0]
     batch, half, width = own.shape
@@ -113,21 +120,25 @@
     mean = jnp.sum(total, axis=1, keepdims=True) / (side * width)
     mean_sq[...] = jnp.broadcast_to(mean, (batch, width))
     scale = jnp.broadcast_to(lax.rsqrt(mean + 1e-06), (batch, width))
-    for k in range(len(outs)):
-        base = lax.bitwise_xor(here, k) * rows
-        for r in range(rows):
-            values = full[pl.ds(base + r, batch, stride=side), :]
-            outs[k][:, r * width : (r + 1) * width] = (values * scale).astype(jnp.bfloat16)
-
-
-def precondition(spot, own, other, left, right, quads):
-    count, half, width = own.shape
+    for k in range(quads):
+        base = lax.bitwise_xor(here, k) * (half // quads)
+        row = 0
+        for f, wide in enumerate(widths):
+            out = outs[k * len(widths) + f]
+            for r in range(wide // width):
+                values = full[pl.ds(base + row, batch, stride=side), :]
+                out[:, r * width : (r + 1) * width] = (values * scale).astype(jnp.bfloat16)
+                row += 1
+
+
+def precondition(spot, own, other, left, right, span, widths, quads):
+    _, half, width = own.shape
     side = 2 * half
-    rows = half // quads
-    batch = min(STEP, count)
-    gradient_spec = pl.BlockSpec((batch, half, width), lambda i, s: (i, 0, 0))
+    first, count, batch = span
+    gradient_spec = pl.BlockSpec((batch, half, width), lambda i, s: (first // batch + i, 0, 0))
+    widths_all = list(widths) * quads
     return pl.pallas_call(
-        functools.partial(precondition_kernel, rows),
+        functools.partial(precondition_kernel, widths),
         grid_spec=pltpu.PrefetchScalarGridSpec(
             num_scalar_prefetch=1,
             grid=(count // batch,),
@@ -137,7 +148,9 @@
                 pl.BlockSpec((side, side), lambda i, s: (0, 0)),
                 pl.BlockSpec((3 * width, width), lambda i, s: (0, 0)),
             ],
-            out_specs=[pl.BlockSpec((batch, rows * width), lambda i, s: (i, 0))] * quads
+            out_specs=[
+                pl.BlockSpec((batch, wide), lambda i, s: (i, 0)) for wide in widths_all
+            ]
             + [pl.BlockSpec((batch, width), lambda i, s: (i, 0))],
             scratch_shapes=[
                 pltpu.VMEM((batch * side, width), jnp.float32),
@@ -145,7 +158,7 @@
                 pltpu.VMEM((GROUP * side, 3 * width), jnp.bfloat16),
             ],
         ),
-        out_shape=[jax.ShapeDtypeStruct((count, rows * width), jnp.bfloat16)] * quads
+        out_shape=[jax.ShapeDtypeStruct((count, wide), jnp.bfloat16) for wide in widths_all]
         + [jax.ShapeDtypeStruct((count, width), jnp.float32)],
         compiler_params=pltpu.CompilerParams(vmem_limit_bytes=VMEM_BYTES),
         cost_estimate=pl.CostEstimate(
@@ -157,77 +170,118 @@
     )(spot, own, other, left, right)
 
 
-def tiles_kernel(quads, reach, slots, spot, targets, *rest):
-    owners = 2 * quads
-    outs = quads * reach * 2
-    inputs, sums, (cluster,) = rest[: -outs - 1], rest[-outs - 1 : -1], rest[-1:]
-    pieces = len(inputs) // owners
-    here, side, core = spot[0], spot[1], spot[2]
+def place_kernel(owners, slots, spot, targets, *rest):
+    inputs, cluster = rest[:-1], rest[-1]
+    quads = owners // 2
+    here, side = spot[0], spot[1]
     block = owners * slots
-    count = targets.shape[2]
-    depth = inputs[0].shape[1]
-
-    @pl.when(pl.program_id(0) == 0)
-    def _():
-        for ref in sums:
-            ref[...] = jnp.zeros_like(ref)
-
-    slot_of = lax.broadcasted_iota(jnp.int32, (block, count), 0)
+    depth = cluster.shape[3]
     for source in range(owners):
+        early, late = inputs[2 * source : 2 * source + 2]
+        values = jnp.concatenate([early[...], late[...]], axis=0)
+        count = values.shape[0]
         k, m = source % quads, source // quads
         producer = 2 * lax.bitwise_xor(here, k) + lax.bitwise_xor(side, m)
-        placing = (slot_of == targets[producer]).astype(jnp.bfloat16)
-        values = jnp.concatenate([r[...] for r in inputs[source * pieces : (source + 1) * pieces]])
+        slot_of = lax.broadcasted_iota(jnp.int32, (block, count), 0)
+        placing = (slot_of == targets[source]).astype(jnp.bfloat16)
         placed = jnp.dot(placing, values, preferred_element_type=jnp.float32).astype(jnp.bfloat16)
         cluster[:, producer] = placed.reshape(owners, slots, depth)
-    for k in range(quads):
-        owner = 2 * lax.bitwise_xor(here, k) + side
-        mine = cluster[owner].reshape(block, depth)
-        for j in range(reach):
-            ahead = cluster[lax.rem(owner + j + 1, owners)].reshape(block, depth)
-            product = lax.dot_general(
-                ahead, mine, (((1,), (1,)), ((), ())), preferred_element_type=jnp.float32
-            )
-            keep, send = sums[2 * (k * reach + j)], sums[2 * (k * reach + j) + 1]
-
-            @pl.when(core == 0)
-            def _():
-                keep[...] += product[: block // 2]
-                send[...] += product[block // 2 :]
-
-            @pl.when(core != 0)
-            def _():
-                send[...] += product[: block // 2]
-                keep[...] += product[block // 2 :]
-
-
-def partial_tiles(spot, targets, pieces, quads, reach, slots):
-    owners = 2 * quads
-    block = owners * slots
-    count = targets.shape[2]
-    features = pieces[0].shape[1]
-    depth = min(512, features)
-    in_specs = [pl.BlockSpec(targets.shape, lambda i, s: (0, 0, 0))]
-    in_specs += [pl.BlockSpec((p.shape[0], depth), lambda i, s: (0, i)) for p in pieces]
-    outs = quads * reach * 2
+
+
+def place(spot, targets, early, late, offset, slots):
+    owners = len(early)
+    first = early[0].shape[0]
+    rest, features = late[0].shape
+    depth = PLACE_WIDTH
+    in_specs, operands = [pl.BlockSpec(targets.shape, lambda i, s: (0, 0, 0))], [targets]
+    for a, b in zip(early, late):
+        in_specs += [
+            pl.BlockSpec((first, depth), lambda i, s: (0, offset // depth + i)),
+            pl.BlockSpec((rest, depth), lambda i, s: (0, i)),
+        ]
+        operands += [a, b]
     return pl.pallas_call(
-        functools.partial(tiles_kernel, quads, reach, slots),
+        functools.partial(place_kernel, owners, slots),
         grid_spec=pltpu.PrefetchScalarGridSpec(
             num_scalar_prefetch=1,
             grid=(features // depth,),
             in_specs=in_specs,
-            out_specs=[pl.BlockSpec((block // 2, block), lambda i, s: (0, 0))] * outs,
-            scratch_shapes=[pltpu.VMEM((owners, owners, slots, depth), jnp.bfloat16)],
-        ),
-        out_shape=[jax.ShapeDtypeStruct((block // 2, block), jnp.float32)] * outs,
+            out_specs=pl.BlockSpec((owners, owners, slots, depth), lambda i, s: (0, 0, 0, i)),
+        ),
+        out_shape=jax.ShapeDtypeStruct((owners, owners, slots, features), jnp.bfloat16),
         compiler_params=pltpu.CompilerParams(vmem_limit_bytes=VMEM_BYTES),
         cost_estimate=pl.CostEstimate(
-            flops=2 * features * block * (owners * count + quads * reach * block),
-            bytes_accessed=owners * count * features * 2 + outs * block * block * 2,
+            flops=2 * features * owners * slots * owners * (first + rest),
+            bytes_accessed=owners * features * 2 * (first + rest + owners * slots),
             transcendentals=0,
         ),
+        name="place",
+    )(spot, *operands)
+
+
+def tiles_kernel(count, spot, *rest):
+    inputs, (keep, send) = rest[: 2 * count], rest[2 * count :]
+    core = spot[2]
+    owners, slots = inputs[0].shape[1:3]
+    half = owners // 2
+    rows = half * slots
+    total = None
+    for f in range(count):
+        mine, ahead = inputs[2 * f], inputs[2 * f + 1]
+        depth = mine.shape[3]
+        halves = [
+            ahead[0, pl.ds(lax.bitwise_xor(core, h) * half, half)].reshape(rows, depth)
+            for h in range(2)
+        ]
+        product = lax.dot_general(
+            jnp.concatenate(halves, axis=0),
+            mine[0].reshape(owners * slots, depth),
+            (((1,), (1,)), ((), ())),
+            preferred_element_type=jnp.float32,
+        )
+        total = product if total is None else total + product
+    keep[0] = total[:rows]
+    send[0] = total[rows:]
+
+
+def partial_tiles(spot, slices, order, j):
+    owners, _, slots, _ = slices[0].shape
+    block = owners * slots
+    features = sum(s.shape[3] for s in slices)
+
+    def owner_at(i, s):
+        k = functools.reduce(lambda v, n: jnp.where(i == n, order[n], v), range(len(order)), 0)
+        return 2 * lax.bitwise_xor(s[0], k) + s[1]
+
+    def mine(i, s):
+        return (owner_at(i, s), 0, 0, 0)
+
+    def ahead(i, s):
+        return (lax.rem(owner_at(i, s) + j + 1, owners), 0, 0, 0)
+
+    in_specs, operands = [], []
+    for part in slices:
+        shape = (1,) + part.shape[1:]
+        in_specs += [pl.BlockSpec(shape, mine), pl.BlockSpec(shape, ahead)]
+        operands += [part, part]
+    out = (len(order), block // 2, block)
+    return pl.pallas_call(
+        functools.partial(tiles_kernel, len(slices)),
+        grid_spec=pltpu.PrefetchScalarGridSpec(
+            num_scalar_prefetch=1,
+            grid=(len(order),),
+            in_specs=in_specs,
+            out_specs=[pl.BlockSpec((1,) + out[1:], lambda i, s: (i, 0, 0))] * 2,
+        ),
+        out_shape=[jax.ShapeDtypeStruct(out, jnp.float32)] * 2,
+        compiler_params=pltpu.CompilerParams(vmem_limit_bytes=VMEM_BYTES),
+        cost_estimate=pl.CostEstimate(
+            flops=2 * features * block * block * len(order),
+            bytes_accessed=len(order) * block * (features * 4 + block * 4),
+            transcendentals=0,
+        ),
         name="partial_tiles",
-    )(spot, targets, *pieces)
+    )(spot, *operands)
 
 
 def split_plan(gradients, owner_of, pair_flags, left_factor, right_factor):
@@ -252,54 +306,82 @@
     def beside(x):
         return lax.ppermute(x, "blk", [(i, i ^ 1) for i in range(owners)])
 
+    def send(parts):
+        got = [parts[0]] + [None] * (quads - 1)
+        for k in reversed(range(1, quads)):
+            got[k] = along(parts[k], k)
+        return got
+
     swapped = jnp.concatenate([left_factor[half:], left_factor[:half]], axis=0)
     swapped = jnp.concatenate([swapped[:, half:], swapped[:, :half]], axis=1)
     left = jnp.where(core == 0, left_factor, swapped)
     right = jnp.concatenate([right_factor] * 3, axis=0)
 
-    target = slot_targets(owner_of, owners, slots)
-    targets = lax.all_gather(target, "blk", axis=0, tiled=True).reshape(owners, 1, count)
-
-    bounds = [0]
-    for part in CHUNKS:
-        bounds.append(bounds[-1] + part * count // sum(CHUNKS))
-    chunks = [gradients[a:b] for a, b in zip(bounds[:-1], bounds[1:])]
-    others = [across(chunk) for chunk in chunks]
-    pieces = [[] for _ in range(owners)]
-    means = []
-    for chunk, other in zip(chunks, others):
-        *parts, mean_sq = precondition(spot, chunk, other, left, right, quads)
-        means.append(mean_sq[:, 0])
-        got = [parts[0]] + [None] * (quads - 1)
-        for k in reversed(range(1, quads)):
-            got[k] = along(parts[k], k)
-        for k in range(quads):
-            pieces[k].append(got[k])
-            pieces[quads + k].append(beside(got[k]))
-
-    influence = jnp.log1p(jnp.concatenate(means)).astype(jnp.bfloat16)
-    influences = lax.all_gather(influence, "blk", axis=0, tiled=True).reshape(owners, count)
-    local = targets[:, 0] - index * slots
-    chosen = local[:, None, :] == jnp.arange(slots, dtype=jnp.int32)[None, :, None]
-    self_influence = jnp.sum(
-        jnp.where(chosen, influences[:, None, :].astype(jnp.float32), 0.0), axis=2
-    ).astype(jnp.bfloat16)
-
-    sums = partial_tiles(
-        spot, targets, [p for group in pieces for p in group], quads, reach, slots
-    )
+    first = FIRST
+    own_features = half * width // quads
+    widths = [own_features * n // sum(SLICES) for n in SLICES]
+    other_first = across(gradients[:first])
+    other = across(gradients)
+    *parts, mean_early = precondition(
+        spot, gradients, other_first, left, right, (0, first, first), [own_features], quads
+    )
+    early = send(parts)
+    *parts, mean_late = precondition(
+        spot, gradients, other, left, right, (first, count - first, STEP), widths, quads
+    )
+    early_came = early[:1] + after(early[1:], parts[0])
+    arrived = [early_came]
+    besides = [[beside(part) for part in early_came]]
+
+    means = jnp.concatenate([mean_early[:, 0], mean_late[:, 0]])
+    told = jnp.stack([owner_of[:, 0].astype(jnp.float32), jnp.log1p(means)])
+    told = jnp.stack(send([told] * quads))
+    told = jnp.stack([told, beside(told)], axis=1)
+    owners_all, influences = told[:, :, 0].astype(jnp.int32), told[:, :, 1]
+    same = owners_all[..., :, None] == owners_all[..., None, :]
+    before = jnp.arange(count)[:, None] > jnp.arange(count)[None, :]
+    rank = jnp.sum((same & before).astype(jnp.int32), axis=-1)
+    targets = owners_all * slots + rank
+
+    slices = []
+    offset = 0
+    for f, wide in enumerate(widths):
+        message = parts[f :: len(widths)]
+        if f >= 1:
+            message = after(message, *besides[f - 1])
+        if f >= 2:
+            message = after(message, slices[f - 2])
+        late = send(message)
+        if f == len(widths) - 1:
+            late = late[:1] + after(late[1:], slices[f - 1])
+        besides.append([beside(part) for part in late])
+        slices.append(
+            place(
+                spot,
+                targets.swapaxes(0, 1).reshape(owners, 1, count),
+                early_came + besides[0],
+                late + besides[-1],
+                offset,
+                slots,
+            )
+        )
+        offset += wide
+
     flags = lax.dynamic_index_in_dim(pair_flags, index, 0, keepdims=False).astype(jnp.float32)
     ahead, behind = [], []
+    pair = [list(reversed(range(1, quads, 2))), list(reversed(range(0, quads, 2)))]
+    operands = slices
     for j in range(reach):
-        total = [None] * quads
-        for k in reversed(range(quads)):
-            at = 2 * (k * reach + j)
-            total[k] = sums[at] + across(sums[at + 1])
-        bit = 1
-        while bit < quads:
-            for k in range(0, quads, 2 * bit):
-                total[k] = total[k] + along(total[k + bit], bit)
-            bit *= 2
+        keep_odd, send_odd = partial_tiles(spot, operands, pair[0], j)
+        odd = keep_odd + across(send_odd)
+        keep_even, send_even = partial_tiles(spot, operands, pair[1], j)
+        came = along(odd, 1)
+        if j + 1 < reach:
+            operands = after(slices, odd, send_even)
+        total = keep_even + across(send_even) + came
+        while total.shape[0] > 1:
+            rows = total.shape[0] // 2
+            total = total[rows:] + along(total[:rows], 2 * rows)
         tile = (total[0] * (flags[j] * feat ** (-0.5))).astype(jnp.bfloat16)
         ahead.append(tile)
         turned = tile.T.reshape(2, block // 2, block // 2)
@@ -320,6 +402,24 @@
             )
         )
     tiles = jnp.stack(ahead + behind).swapaxes(1, 2)
+
+    (influences,) = after([influences], ahead[-1])
+    wanted = index * slots + jnp.arange(slots, dtype=jnp.int32)
+    chosen = targets[:, :, None, :] == wanted[:, None]
+    self_influence = jnp.sum(jnp.where(chosen, influences[:, :, None, :], 0.0), axis=3)
+    self_influence = lax.switch(
+        index,
+        [
+            functools.partial(
+                lambda i, x: jnp.stack(
+                    [x[(p ^ i) // 2, (p ^ i) % 2] for p in range(owners)]
+                ).astype(jnp.bfloat16),
+                i,
+            )
+            for i in range(owners)
+        ],
+        self_influence,
+    )
     return (tiles, self_influence.reshape(block))
 
 
@@ -331,7 +431,7 @@
         partial_bytes = 4 * owners * pair_flags.shape[1] * block * block // 2
         quads = owners // 2
         fits = partial_bytes <= PARTIAL_BYTES and quads & (quads - 1) == 0
-        plan = split_plan if fits and gradients.shape[1] % quads == 0 else ring_plan
+        plan = split_plan if fits and gradients.shape[0] % FIRST == 0 else ring_plan
         return plan(gradients, owner_of, pair_flags, left_factor, right_factor)
 
     return jax.shard_map(

time: 329 us -> 272 us (0.83)
  blocking collectives: 64.4 us -> 0 us
  starting transfers between devices: 96.8 us -> 78.3 us
  Pallas kernels: 59.8 us -> 77.2 us
  waiting for transfers between devices: 80.9 us -> 87.5 us
    all_gather x2 -> x0, blocking collectives: 64.4 us -> none  [the longest x1 47.8 us: split_plan(): lax.all_gather(target, 'blk', axis=0, tiled=True).reshape(owners, 1, count)]
    pallas_call x5 -> x11, Pallas kernels: 59.8 us -> 77.2 us  [the longest x6 32.7 us: partial_tiles(): pl.pallas_call(functools.partial(tiles_kernel, len(slices)), grid_spec=pl...]
    ppermute x21, waiting for transfers between devices: 50.2 us -> 62.1 us  [along(): return lax.ppermute(x, 'blk', [(i, i ^ 2 * k) for i in range(owners)])]
    ppermute x21, starting transfers between devices: 52.8 us -> 44.5 us  [along(): return lax.ppermute(x, 'blk', [(i, i ^ 2 * k) for i in range(owners)])]
    ppermute x3, waiting for transfers between devices: 11.2 us -> 4.87 us  [from_behind(): lax.ppermute(shard, axis, [(i, (i + by) % peers) for i in range(peers)])]
    ppermute x16 -> x8, starting transfers between devices: 18.9 us -> 12.8 us  [across(): return lax.ppermute(x, 'dim', [(0, 1), (1, 0)])]
    ppermute x3, starting transfers between devices: 7.13 us -> 2.03 us  [from_behind(): lax.ppermute(shard, axis, [(i, (i + by) % peers) for i in range(peers)])]
    add x10 -> x6, other arithmetic: 7.34 us -> 4.04 us  [the longest x3 3.85 us: split_plan(): total = keep_even + across(send_even) + came]
  transfers between devices with their start and end apart: 59 -> 52, of which waited for: 17 -> 18; matrix products, arithmetic and copies ran while one was open for 6% -> 8% of each run, Pallas kernels for 9% -> 23%
where the time goes in v2:
time: 272 us; the launch traced here: 271 us
  waiting for transfers between devices  87.5 us (32%)
  starting transfers between devices  78.3 us (29%)
  Pallas kernels  77.2 us (28%)
  other arithmetic  13.6 us (5%)
  local copies, waits for them, and re-layouts  10.8 us (4%)
  between operations  3.12 us (1%)
    ppermute x21, waiting for transfers between devices, along(): return lax.ppermute(x, 'blk', [(i, i ^ 2 * k) for i in range(owners)])  62.1 us
    ppermute x21, starting transfers between devices, along(): return lax.ppermute(x, 'blk', [(i, i ^ 2 * k) for i in range(owners)])  44.5 us
    pallas_call x6, Pallas kernels, partial_tiles(): pl.pallas_call(functools.partial(tiles_kernel, len(slices)), grid_spec=pl...  32.7 us
    pallas_call x2, Pallas kernels, precondition(): pl.pallas_call(functools.partial(precondition_kernel, widths), grid_spec=...  25.9 us
    pallas_call x3, Pallas kernels, place(): pl.pallas_call(functools.partial(place_kernel, owners, slots), grid_spec=...  18.6 us
    ppermute x17, waiting for transfers between devices, beside(): return lax.ppermute(x, 'blk', [(i, i ^ 1) for i in range(owners)])  15.9 us
    ppermute x17, starting transfers between devices, beside(): return lax.ppermute(x, 'blk', [(i, i ^ 1) for i in range(owners)])  13.8 us
    ppermute x8, starting transfers between devices, across(): return lax.ppermute(x, 'dim', [(0, 1), (1, 0)])  12.8 us
  transfers between devices with their start and end apart: 52, of which 18 were waited for; matrix products, arithmetic and copies ran while one was open for 8% of the time, Pallas kernels for 23%

profile of v2, /device:TPU:5, one launch (start us, length us, event | category | flops | bytes accessed | tf_op | source)
XLA Modules:
  0.0 270.7 jit_solution(17270722576838456993)
XLA Ops:
  10.7 7.2 %precondition.2 = (bf16[64,2048]{1,0:T(8,128)(2,1)}, bf16[64,2048]{1,0:T(8,128)(2,1)}, bf16[64,2048]{1,0:T(8,128)(2,1)}, bf16[64,2048]{1,0:T(8,128)(2,1)}, f32[64,128]{1,0:T(8,128)}) custom-call(s32[3]{0:T(128)} %pad_add_fusion.spot, bf16[256,64,128]{2,1,0:T(8,128)(2,1)} %own.3, bf16[64,64,128]{2,1,0:T(8,128)(2,1)} %copy-done.7, ...), custom_call_target="tpu_custom_call" | custom-call | flops 1073741824 | bytes 3145728 | tf_op jit(solution)/shard_map/precondition/pallas_call | solution.py:140
  22.5 18.7 %precondition.3 = (bf16[192,768]{1,0:T(8,128)(2,1)}, bf16[192,768]{1,0:T(8,128)(2,1)}, bf16[192,512]{1,0:T(8,128)(2,1)}, bf16[192,768]{1,0:T(8,128)(2,1)}, bf16[...) custom-call(s32[3]{0:T(128)} %pad_add_fusion.spot, ...), custom_call_target="tpu_custom_call" | custom-call | flops 3221225472 | bytes 9437184 | tf_op jit(solution)/shard_map/precondition/pallas_call | solution.py:140
  45.2 3.4 %collective-permute-start.3 = (f32[2,256]{1,0:T(2,128)S(1)}, f32[2,256]{1,0:T(2,128)S(1)}, u32[]{:S(2)}, u32[]{:S(2)}) collective-permute-start(f32[2,256]{1,0:T(2,128)S(1)} %get-tuple-element.805), channel_id=1, source_target_pairs={{0,8},{2,10},{4,12},{6,14},{8,0},{10,2},{12,4},{14,6},{1,9},{3,11}... | collective-permute-start | bytes 6152 | tf_op jit(solution)/shard_map/ppermute | solution.py:304
  60.1 4.0 %collective-permute-done.5 = f32[4,2,256]{2,0,1:T(4,128)S(1)} collective-permute-done((f32[4,2,256]{2,0,1:T(4,128)S(1)}, f32[4,2,256]{2,0,1:T(4,128)S(1)}, u32[]{:S(2)}, u32[]{:S(2)}) %collective-permute-start.5) | collective-permute-done | bytes 8224 | tf_op jit(solution)/shard_map/ppermute | solution.py:307
  64.2 4.6 %collective-permute-start.20 = (bf16[192,768]{1,0:T(8,128)(2,1)}, bf16[192,768]{1,0:T(8,128)(2,1)S(1)}, u32[]{:S(2)}, u32[]{:S(2)}) collective-permute-start(bf16[192,768]{1,0:T(8,128)(2,1)} %get-tuple-element.602), channel_id=1, source_target_pairs={{0,4},{2,6},{4,0},{6,2},{8,12},{10,14},{12,8},{14,10},{1,5},{3,7},... | collective-permute-start | bytes 884744 | tf_op jit(solution)/shard_map/ppermute | solution.py:304
  69.8 4.0 %collective-permute-done.10.rest_5_ = bf16[192,768]{1,0:T(8,128)(2,1)S(1)} collective-permute-done((bf16[192,768]{1,0:T(8,128)(2,1)}, bf16[192,768]{1,0:T(8,128)(2,1)S(1)}, u32[]{:S(2)}, u32[]{:S(2)}) %collective-permute-start.10) | collective-permute-done | bytes 294944 | tf_op jit(solution)/shard_map/ppermute | solution.py:304
  76.9 5.0 %collective-permute-done.20.rest_3_ = bf16[192,768]{1,0:T(8,128)(2,1)S(1)} collective-permute-done((bf16[192,768]{1,0:T(8,128)(2,1)}, bf16[192,768]{1,0:T(8,128)(2,1)S(1)}, u32[]{:S(2)}, u32[]{:S(2)}) %collective-permute-start.20) | collective-permute-done | bytes 294944 | tf_op jit(solution)/shard_map/ppermute | solution.py:304
  82.7 17.1 %collective-permute-done.21.rest_5_ = bf16[192,768]{1,0:T(8,128)(2,1)} collective-permute-done((bf16[192,768]{1,0:T(8,128)(2,1)}, bf16[192,768]{1,0:T(8,128)(2,1)}, u32[]{:S(2)}, u32[]{:S(2)}) %collective-permute-start.21) | collective-permute-done | bytes 294944 | tf_op jit(solution)/shard_map/ppermute | solution.py:304
  104.2 7.1 %place.3.rest_0_.rest_1_ = bf16[8,8,48,768]{3,2,1,0:T(8,128)(2,1)} custom-call(s32[3]{0:T(128)} %pad_add_fusion.spot, s32[8,1,256]{2,1,0:T(1,128)} %reshape.331.targets, bf16[64,2048]{1,0:T(8,128)(2,1)} %get-tuple-element.586.rest_0_, bf16[192,768]{1,0:T(8,128)(2,1)} %get-tuple-element.587.rest_1_, bf16[64,2048]{1,0:T(8,128)(2,1)} %copy-done, ...), custom_call_target="tpu_custom_call" | custom-call | flops 1207959552 | bytes 7864320 | tf_op jit(solution)/shard_map/place/pallas_call | solution.py:203
  111.2 6.1 %collective-permute-start.27 = (bf16[192,512]{1,0:T(8,128)(2,1)S(1)}, bf16[192,512]{1,0:T(8,128)(2,1)S(1)}, u32[]{:S(2)}, u32[]{:S(2)}) collective-permute-start(bf16[192,512]{1,0:T(8,128)(2,1)S(1)} %copy-done.34), channel_id=1, source_target_pairs={{0,4},{2,6},{4,0},{6,2},{8,12},{10,14},{12,8},{14,10},{1,5},{3,7},... | collective-permute-start | bytes 589832 | tf_op jit(solution)/shard_map/ppermute | solution.py:304
  122.9 7.0 %place.4.rest_2_.rest_3_ = bf16[8,8,48,768]{3,2,1,0:T(8,128)(2,1)} custom-call(s32[3]{0:T(128)} %pad_add_fusion.spot, s32[8,1,256]{2,1,0:T(1,128)} %reshape.331.targets, bf16[64,2048]{1,0:T(8,128)(2,1)} %get-tuple-element.586.rest_0_, bf16[192,768]{1,0:T(8,128)(2,1)} %get-tuple-element.601.rest_1_, bf16[64,2048]{1,0:T(8,128)(2,1)} %copy-done, ...), custom_call_target="tpu_custom_call" | custom-call | flops 1207959552 | bytes 7864320 | tf_op jit(solution)/shard_map/place/pallas_call | solution.py:203
  134.9 4.1 %collective-permute-done.32.rest_13_ = bf16[192,512]{1,0:T(8,128)(2,1)S(1)} collective-permute-done((bf16[192,512]{1,0:T(8,128)(2,1)S(1)}, bf16[192,512]{1,0:T(8,128)(2,1)S(1)}, u32[]{:S(2)}, u32[]{:S(2)}) %collective-permute-start.32) | collective-permute-done | bytes 196640 | tf_op jit(solution)/shard_map/ppermute | solution.py:307
  141.6 4.5 %place.5.rest_4_.rest_5_ = bf16[8,8,48,512]{3,2,1,0:T(8,128)(2,1)} custom-call(s32[3]{0:T(128)} %pad_add_fusion.spot, s32[8,1,256]{2,1,0:T(1,128)} %reshape.331.targets, bf16[64,2048]{1,0:T(8,128)(2,1)} %get-tuple-element.586.rest_0_, bf16[192,512]{1,0:T(8,128)(2,1)} %get-tuple-element.613.rest_1_, bf16[64,2048]{1,0:T(8,128)(2,1)} %copy-done, ...), custom_call_target="tpu_custom_call" | custom-call | flops 805306368 | bytes 5242880 | tf_op jit(solution)/shard_map/place/pallas_call | solution.py:203
  146.1 5.4 %partial_tiles.7 = (f32[2,192,384]{2,1,0:T(8,128)}, f32[2,192,384]{2,1,0:T(8,128)}) custom-call(s32[3]{0:T(128)} %pad_add_fusion.spot, bf16[8,8,48,768]{3,2,1,0:T(8,128)(2,1)} %place.3.rest_0_.rest_1_, bf16[8,8,48,768]{3,2,1,0:T(8,128)(2,1)} %place.3.rest_0_.rest_1_, bf16[8,8,48,768]{3,2,1,0:T(8,128)(2,1)} %place.4.rest_2_.rest_3_, ...), custom_call_target="tpu_custom_call" | custom-call | flops 1207959552 | bytes 7471104 | tf_op jit(solution)/shard_map/partial_tiles/pallas_call | solution.py:268
  151.5 9.0 %collective-permute-start.35 = (f32[2,192,384]{2,1,0:T(8,128)}, f32[2,192,384]{2,1,0:T(8,128)S(1)}, u32[]{:S(2)}, u32[]{:S(2)}) collective-permute-start(f32[2,192,384]{2,1,0:T(8,128)} %get-tuple-element.623), channel_id=1, source_target_pairs={{0,1},{1,0},{2,3},{3,2},{4,5},{5,4},{6,7},{7,6},{8,9},{9,8},{10,11... | collective-permute-start | bytes 1769480 | tf_op jit(solution)/shard_map/ppermute | solution.py:301
  160.5 5.4 %partial_tiles.6 = (f32[2,192,384]{2,1,0:T(8,128)}, f32[2,192,384]{2,1,0:T(8,128)}) custom-call(s32[3]{0:T(128)} %pad_add_fusion.spot, bf16[8,8,48,768]{3,2,1,0:T(8,128)(2,1)} %place.3.rest_0_.rest_1_, bf16[8,8,48,768]{3,2,1,0:T(8,128)(2,1)} %place.3.rest_0_.rest_1_, bf16[8,8,48,768]{3,2,1,0:T(8,128)(2,1)} %place.4.rest_2_.rest_3_, ...), custom_call_target="tpu_custom_call" | custom-call | flops 1207959552 | bytes 7471104 | tf_op jit(solution)/shard_map/partial_tiles/pallas_call | solution.py:268
  165.9 5.4 %partial_tiles.9 = (f32[2,192,384]{2,1,0:T(8,128)}, f32[2,192,384]{2,1,0:T(8,128)}) custom-call(s32[3]{0:T(128)} %pad_add_fusion.spot, bf16[8,8,48,768]{3,2,1,0:T(8,128)(2,1)} %place.3.rest_0_.rest_1_, bf16[8,8,48,768]{3,2,1,0:T(8,128)(2,1)} %place.3.rest_0_.rest_1_, bf16[8,8,48,768]{3,2,1,0:T(8,128)(2,1)} %place.4.rest_2_.rest_3_, ...), custom_call_target="tpu_custom_call" | custom-call | flops 1207959552 | bytes 7471104 | tf_op jit(solution)/shard_map/partial_tiles/pallas_call | solution.py:268
  171.8 10.6 %collective-permute-start.36 = (f32[2,192,384]{2,1,0:T(8,128)S(1)}, f32[2,192,384]{2,1,0:T(8,128)}, u32[]{:S(2)}, u32[]{:S(2)}) collective-permute-start(f32[2,192,384]{2,1,0:T(8,128)S(1)} %add.163), channel_id=1, source_target_pairs={{0,4},{2,6},{4,0},{6,2},{8,12},{10,14},{12,8},{14,10},{1,5},{3,7},... | collective-permute-start | bytes 1769480 | tf_op jit(solution)/shard_map/ppermute | solution.py:304
  182.4 5.5 %partial_tiles.8 = (f32[2,192,384]{2,1,0:T(8,128)}, f32[2,192,384]{2,1,0:T(8,128)}) custom-call(s32[3]{0:T(128)} %pad_add_fusion.spot, bf16[8,8,48,768]{3,2,1,0:T(8,128)(2,1)} %place.3.rest_0_.rest_1_, bf16[8,8,48,768]{3,2,1,0:T(8,128)(2,1)} %place.3.rest_0_.rest_1_, bf16[8,8,48,768]{3,2,1,0:T(8,128)(2,1)} %place.4.rest_2_.rest_3_, ...), custom_call_target="tpu_custom_call" | custom-call | flops 1207959552 | bytes 7471104 | tf_op jit(solution)/shard_map/partial_tiles/pallas_call | solution.py:268
  188.5 5.5 %partial_tiles.11 = (f32[2,192,384]{2,1,0:T(8,128)}, f32[2,192,384]{2,1,0:T(8,128)}) custom-call(s32[3]{0:T(128)} %pad_add_fusion.spot, bf16[8,8,48,768]{3,2,1,0:T(8,128)(2,1)} %place.3.rest_0_.rest_1_, bf16[8,8,48,768]{3,2,1,0:T(8,128)(2,1)} %place.3.rest_0_.rest_1_, bf16[8,8,48,768]{3,2,1,0:T(8,128)(2,1)} %place.4.rest_2_.rest_3_, ...), custom_call_target="tpu_custom_call" | custom-call | flops 1207959552 | bytes 7471104 | tf_op jit(solution)/shard_map/partial_tiles/pallas_call | solution.py:268
  203.7 5.5 %partial_tiles.10 = (f32[2,192,384]{2,1,0:T(8,128)}, f32[2,192,384]{2,1,0:T(8,128)}) custom-call(s32[3]{0:T(128)} %pad_add_fusion.spot, bf16[8,8,48,768]{3,2,1,0:T(8,128)(2,1)} %place.3.rest_0_.rest_1_, bf16[8,8,48,768]{3,2,1,0:T(8,128)(2,1)} %place.3.rest_0_.rest_1_, bf16[8,8,48,768]{3,2,1,0:T(8,128)(2,1)} %place.4.rest_2_.rest_3_, ...), custom_call_target="tpu_custom_call" | custom-call | flops 1207959552 | bytes 7471104 | tf_op jit(solution)/shard_map/partial_tiles/pallas_call | solution.py:268
  224.4 9.5 %collective-permute-done.44 = f32[2,192,384]{2,1,0:T(8,128)} collective-permute-done((f32[2,192,384]{2,1,0:T(8,128)S(1)}, f32[2,192,384]{2,1,0:T(8,128)}, u32[]{:S(2)}, u32[]{:S(2)}) %collective-permute-start.44) | collective-permute-done | bytes 589856 | tf_op jit(solution)/shard_map/ppermute | solution.py:304
  240.1 19.5 %collective-permute-done.45 = f32[1,192,384]{2,1,0:T(8,128)S(1)} collective-permute-done((f32[1,192,384]{2,1,0:T(8,128)S(1)}, f32[1,192,384]{2,1,0:T(8,128)S(1)}, u32[]{:S(2)}, u32[]{:S(2)}) %collective-permute-start.45) | collective-permute-done | bytes 294944 | tf_op jit(solution)/shard_map/ppermute | solution.py:304
  262.3 4.9 %collective-permute-done.50 = bf16[192,192]{1,0:T(8,128)(2,1)S(1)} collective-permute-done((bf16[192,192]{1,0:T(8,128)(2,1)S(1)}, bf16[192,192]{1,0:T(8,128)(2,1)S(1)}, u32[]{:S(2)}, u32[]{:S(2)}) %collective-permute-start.50) | collective-permute-done | bytes 73760 | tf_op jit(solution)/shard_map/ppermute | solution.py:21
  (217 shorter events, 88.9 us)
Async XLA Ops:
  0.6 21.9 %collective-permute-start.1 = (bf16[256,64,128]{2,1,0:T(8,128)(2,1)}, bf16[256,64,128]{2,1,0:T(8,128)(2,1)}, u32[]{:S(2)}, u32[]{:S(2)}) collective-permute-start(bf16[256,64,128]{2,1,0:T(8,128)(2,1)} %own.3), channel_id=1, source_target_pairs={{0,1},{1,0},{2,3},{3,2},{4,5},{5,4},{6,7},{7,6},{8,9},{9,8},{10,11... | collective-permute-start | bytes 12582920 | tf_op jit(solution)/shard_map/ppermute | solution.py:301
  17.8 23.4 %collective-permute-start.6 = (bf16[64,2048]{1,0:T(8,128)(2,1)}, bf16[64,2048]{1,0:T(8,128)(2,1)S(1)}, u32[]{:S(2)}, u32[]{:S(2)}) collective-permute-start(bf16[64,2048]{1,0:T(8,128)(2,1)} %get-tuple-element.588), channel_id=1, source_target_pairs={{0,4},{2,6},{4,0},{6,2},{8,12},{10,14},{12,8},{14,10},{1,5},{3,7},... | collective-permute-start | bytes 786440 | tf_op jit(solution)/shard_map/ppermute | solution.py:304
  19.1 22.1 %collective-permute-start.7 = (bf16[64,2048]{1,0:T(8,128)(2,1)}, bf16[64,2048]{1,0:T(8,128)(2,1)S(1)}, u32[]{:S(2)}, u32[]{:S(2)}) collective-permute-start(bf16[64,2048]{1,0:T(8,128)(2,1)} %get-tuple-element.589), channel_id=1, source_target_pairs={{0,8},{2,10},{4,12},{6,14},{8,0},{10,2},{12,4},{14,6},{1,9},{3,11}... | collective-permute-start | bytes 786440 | tf_op jit(solution)/shard_map/ppermute | solution.py:304
  21.4 19.8 %collective-permute-start.8 = (bf16[64,2048]{1,0:T(8,128)(2,1)}, bf16[64,2048]{1,0:T(8,128)(2,1)S(1)}, u32[]{:S(2)}, u32[]{:S(2)}) collective-permute-start(bf16[64,2048]{1,0:T(8,128)(2,1)} %get-tuple-element.590), channel_id=1, source_target_pairs={{0,12},{2,14},{4,8},{6,10},{8,4},{10,6},{12,0},{14,2},{1,13},{3,15... | collective-permute-start | bytes 786440 | tf_op jit(solution)/shard_map/ppermute | solution.py:304
  21.4 27.1 %collective-permute-start.12 = (bf16[64,2048]{1,0:T(8,128)(2,1)}, bf16[64,2048]{1,0:T(8,128)(2,1)S(1)}, u32[]{:S(2)}, u32[]{:S(2)}) collective-permute-start(bf16[64,2048]{1,0:T(8,128)(2,1)} %get-tuple-element.586.rest_0_), channel_id=1, source_target_pairs={{0,2},{2,0},{4,6},{6,4},{8,10},{10,8},{12,14},{14,12},{1,3},{3,1},... | collective-permute-start | bytes 786440 | tf_op jit(solution)/shard_map/ppermute | solution.py:307
  53.8 20.1 %collective-permute-start.10 = (bf16[192,768]{1,0:T(8,128)(2,1)}, bf16[192,768]{1,0:T(8,128)(2,1)S(1)}, u32[]{:S(2)}, u32[]{:S(2)}) collective-permute-start(bf16[192,768]{1,0:T(8,128)(2,1)} %get-tuple-element.594), channel_id=1, source_target_pairs={{0,8},{2,10},{4,12},{6,14},{8,0},{10,2},{12,4},{14,6},{1,9},{3,11}... | collective-permute-start | bytes 884744 | tf_op jit(solution)/shard_map/ppermute | solution.py:304
  54.7 20.7 %collective-permute-start.11 = (bf16[192,768]{1,0:T(8,128)(2,1)}, bf16[192,768]{1,0:T(8,128)(2,1)S(1)}, u32[]{:S(2)}, u32[]{:S(2)}) collective-permute-start(bf16[192,768]{1,0:T(8,128)(2,1)} %get-tuple-element.596), channel_id=1, source_target_pairs={{0,12},{2,14},{4,8},{6,10},{8,4},{10,6},{12,0},{14,2},{1,13},{3,15... | collective-permute-start | bytes 884744 | tf_op jit(solution)/shard_map/ppermute | solution.py:304
  56.3 19.1 %collective-permute-start.13 = (bf16[192,768]{1,0:T(8,128)(2,1)}, bf16[192,768]{1,0:T(8,128)(2,1)S(1)}, u32[]{:S(2)}, u32[]{:S(2)}) collective-permute-start(bf16[192,768]{1,0:T(8,128)(2,1)} %get-tuple-element.587.rest_1_), channel_id=1, source_target_pairs={{0,2},{2,0},{4,6},{6,4},{8,10},{10,8},{12,14},{14,12},{1,3},{3,1},... | collective-permute-start | bytes 884744 | tf_op jit(solution)/shard_map/ppermute | solution.py:307
  68.7 31.1 %collective-permute-start.21 = (bf16[192,768]{1,0:T(8,128)(2,1)}, bf16[192,768]{1,0:T(8,128)(2,1)}, u32[]{:S(2)}, u32[]{:S(2)}) collective-permute-start(bf16[192,768]{1,0:T(8,128)(2,1)} %get-tuple-element.603), channel_id=1, source_target_pairs={{0,8},{2,10},{4,12},{6,14},{8,0},{10,2},{12,4},{14,6},{1,9},{3,11}... | collective-permute-start | bytes 884744 | tf_op jit(solution)/shard_map/ppermute | solution.py:304
  73.9 27.3 %collective-permute-start.22 = (bf16[192,768]{1,0:T(8,128)(2,1)}, bf16[192,768]{1,0:T(8,128)(2,1)}, u32[]{:S(2)}, u32[]{:S(2)}) collective-permute-start(bf16[192,768]{1,0:T(8,128)(2,1)} %get-tuple-element.604), channel_id=1, source_target_pairs={{0,12},{2,14},{4,8},{6,10},{8,4},{10,6},{12,0},{14,2},{1,13},{3,15... | collective-permute-start | bytes 884744 | tf_op jit(solution)/shard_map/ppermute | solution.py:304
  75.4 26.0 %collective-permute-start.15 = (bf16[192,768]{1,0:T(8,128)(2,1)S(1)}, bf16[192,768]{1,0:T(8,128)(2,1)S(1)}, u32[]{:S(2)}, u32[]{:S(2)}) collective-permute-start(bf16[192,768]{1,0:T(8,128)(2,1)S(1)} %collective-permute-done.9.rest_3_), channel_id=1, source_target_pairs={{0,2},{2,0},{4,6},{6,4},{8,10},{10,8},{12,14},{14,12},{1,3},{3,1},... | collective-permute-start | bytes 884744 | tf_op jit(solution)/shard_map/ppermute | solution.py:307
  75.4 27.3 %collective-permute-start.17 = (bf16[192,768]{1,0:T(8,128)(2,1)S(1)}, bf16[192,768]{1,0:T(8,128)(2,1)S(1)}, u32[]{:S(2)}, u32[]{:S(2)}) collective-permute-start(bf16[192,768]{1,0:T(8,128)(2,1)S(1)} %collective-permute-done.10.rest_5_), channel_id=1, source_target_pairs={{0,2},{2,0},{4,6},{6,4},{8,10},{10,8},{12,14},{14,12},{1,3},{3,1},... | collective-permute-start | bytes 884744 | tf_op jit(solution)/shard_map/ppermute | solution.py:307
  82.0 22.1 %collective-permute-start.19 = (bf16[192,768]{1,0:T(8,128)(2,1)S(1)}, bf16[192,768]{1,0:T(8,128)(2,1)}, u32[]{:S(2)}, u32[]{:S(2)}) collective-permute-start(bf16[192,768]{1,0:T(8,128)(2,1)S(1)} %collective-permute-done.11.rest_7_), channel_id=1, source_target_pairs={{0,2},{2,0},{4,6},{6,4},{8,10},{10,8},{12,14},{14,12},{1,3},{3,1},... | collective-permute-start | bytes 884744 | tf_op jit(solution)/shard_map/ppermute | solution.py:307
  102.7 20.2 %collective-permute-start.26 = (bf16[192,768]{1,0:T(8,128)(2,1)}, bf16[192,768]{1,0:T(8,128)(2,1)}, u32[]{:S(2)}, u32[]{:S(2)}) collective-permute-start(bf16[192,768]{1,0:T(8,128)(2,1)} %collective-permute-done.22.rest_7_), channel_id=1, source_target_pairs={{0,2},{2,0},{4,6},{6,4},{8,10},{10,8},{12,14},{14,12},{1,3},{3,1},... | collective-permute-start | bytes 884744 | tf_op jit(solution)/shard_map/ppermute | solution.py:307
  171.5 22.8 %collective-permute-start.34 = (f32[2,192,384]{2,1,0:T(8,128)}, f32[2,192,384]{2,1,0:T(8,128)}, u32[]{:S(2)}, u32[]{:S(2)}) collective-permute-start(f32[2,192,384]{2,1,0:T(8,128)} %get-tuple-element.621), channel_id=1, source_target_pairs={{0,1},{1,0},{2,3},{3,2},{4,5},{5,4},{6,7},{7,6},{8,9},{9,8},{10,11... | collective-permute-start | bytes 1769480 | tf_op jit(solution)/shard_map/ppermute | solution.py:301
  171.8 24.2 %collective-permute-start.36 = (f32[2,192,384]{2,1,0:T(8,128)S(1)}, f32[2,192,384]{2,1,0:T(8,128)}, u32[]{:S(2)}, u32[]{:S(2)}) collective-permute-start(f32[2,192,384]{2,1,0:T(8,128)S(1)} %add.163), channel_id=1, source_target_pairs={{0,4},{2,6},{4,0},{6,2},{8,12},{10,14},{12,8},{14,10},{1,5},{3,7},... | collective-permute-start | bytes 1769480 | tf_op jit(solution)/shard_map/ppermute | solution.py:304
  187.9 28.9 %collective-permute-start.38 = (f32[2,192,384]{2,1,0:T(8,128)}, f32[2,192,384]{2,1,0:T(8,128)S(1)}, u32[]{:S(2)}, u32[]{:S(2)}) collective-permute-start(f32[2,192,384]{2,1,0:T(8,128)} %get-tuple-element.628), channel_id=1, source_target_pairs={{0,1},{1,0},{2,3},{3,2},{4,5},{5,4},{6,7},{7,6},{8,9},{9,8},{10,11... | collective-permute-start | bytes 1769480 | tf_op jit(solution)/shard_map/ppermute | solution.py:301
  188.5 28.3 %collective-permute-start.40 = (f32[2,192,384]{2,1,0:T(8,128)S(1)}, f32[2,192,384]{2,1,0:T(8,128)}, u32[]{:S(2)}, u32[]{:S(2)}) collective-permute-start(f32[2,192,384]{2,1,0:T(8,128)S(1)} %add.168), channel_id=1, source_target_pairs={{0,4},{2,6},{4,0},{6,2},{8,12},{10,14},{12,8},{14,10},{1,5},{3,7},... | collective-permute-start | bytes 1769480 | tf_op jit(solution)/shard_map/ppermute | solution.py:304
  211.2 22.8 %collective-permute-start.44 = (f32[2,192,384]{2,1,0:T(8,128)S(1)}, f32[2,192,384]{2,1,0:T(8,128)}, u32[]{:S(2)}, u32[]{:S(2)}) collective-permute-start(f32[2,192,384]{2,1,0:T(8,128)S(1)} %add.172), channel_id=1, source_target_pairs={{0,4},{2,6},{4,0},{6,2},{8,12},{10,14},{12,8},{14,10},{1,5},{3,7},... | collective-permute-start | bytes 1769480 | tf_op jit(solution)/shard_map/ppermute | solution.py:304
  221.2 39.4 %collective-permute-start.46 = (bf16[192,192]{1,0:T(8,128)(2,1)S(1)}, bf16[192,192]{1,0:T(8,128)(2,1)S(1)}, u32[]{:S(2)}, u32[]{:S(2)}) collective-permute-start(bf16[192,192]{1,0:T(8,128)(2,1)S(1)} %get-tuple-element.793), channel_id=1, source_target_pairs={{0,2},{2,4},{4,6},{6,8},{8,10},{10,12},{12,14},{14,0},{1,3},{3,5},... | collective-permute-start | bytes 221192 | tf_op jit(solution)/shard_map/ppermute | solution.py:21
  221.3 39.4 %collective-permute-start.47 = (bf16[192,192]{1,0:T(8,128)(2,1)S(1)}, bf16[192,192]{1,0:T(8,128)(2,1)S(1)}, u32[]{:S(2)}, u32[]{:S(2)}) collective-permute-start(bf16[192,192]{1,0:T(8,128)(2,1)S(1)} %get-tuple-element.794), channel_id=1, source_target_pairs={{0,3},{1,2},{2,5},{3,4},{4,7},{5,6},{6,9},{7,8},{8,11},{9,10},{10,... | collective-permute-start | bytes 221192 | tf_op jit(solution)/shard_map/ppermute | solution.py:392
  235.3 24.3 %collective-permute-start.45 = (f32[1,192,384]{2,1,0:T(8,128)S(1)}, f32[1,192,384]{2,1,0:T(8,128)S(1)}, u32[]{:S(2)}, u32[]{:S(2)}) collective-permute-start(f32[1,192,384]{2,1,0:T(8,128)S(1)} %slice.468), channel_id=1, source_target_pairs={{0,8},{2,10},{4,12},{6,14},{8,0},{10,2},{12,4},{14,6},{1,9},{3,11}... | collective-permute-start | bytes 884744 | tf_op jit(solution)/shard_map/ppermute | solution.py:304
  236.3 25.2 %collective-permute-start.48 = (bf16[192,192]{1,0:T(8,128)(2,1)S(1)}, bf16[192,192]{1,0:T(8,128)(2,1)S(1)}, u32[]{:S(2)}, u32[]{:S(2)}) collective-permute-start(bf16[192,192]{1,0:T(8,128)(2,1)S(1)} %get-tuple-element.791), channel_id=1, source_target_pairs={{0,4},{2,6},{4,8},{6,10},{8,12},{10,14},{12,0},{14,2},{1,5},{3,7},... | collective-permute-start | bytes 221192 | tf_op jit(solution)/shard_map/ppermute | solution.py:21
  238.2 23.3 %collective-permute-start.49 = (bf16[192,192]{1,0:T(8,128)(2,1)S(1)}, bf16[192,192]{1,0:T(8,128)(2,1)S(1)}, u32[]{:S(2)}, u32[]{:S(2)}) collective-permute-start(bf16[192,192]{1,0:T(8,128)(2,1)S(1)} %get-tuple-element.792), channel_id=1, source_target_pairs={{0,5},{1,4},{2,7},{3,6},{4,9},{5,8},{6,11},{7,10},{8,13},{9,12},{1... | collective-permute-start | bytes 221192 | tf_op jit(solution)/shard_map/ppermute | solution.py:392
  (63 other events, 1076.5 us)

commit v3 on v0

--- a/solution.py
+++ b/solution.py
@@ -1,7 +1,21 @@
+import functools
+
 import jax
 import jax.numpy as jnp
 from jax import lax
+from jax.experimental import pallas as pl
+from jax.experimental.pallas import tpu as pltpu
 from jax.sharding import PartitionSpec as P
+
+PARTIAL_BYTES = 16 * 2**20
+FIRST = 64
+SLICES = (3, 3, 2)
+NOTE = 16
+NOTE_BASE = 256
+GROUP = 8
+STEP = 32
+VMEM_BYTES = 56 * 2**20
+SMALL_COST = pl.CostEstimate(flops=2**20, bytes_accessed=2**16, transcendentals=0)
 
 
 def from_behind(shard, axis, by):
@@ -9,7 +23,17 @@
     return lax.ppermute(shard, axis, [(i, (i + by) % peers) for i in range(peers)])
 
 
-def per_device(gradients, owner_of, pair_flags, left_factor, right_factor):
+def slot_targets(owner_of, owners_count, slots):
+    owners = owner_of[:, 0]
+    onehot = (owners[:, None] == jnp.arange(owners_count, dtype=jnp.int32)[None, :]).astype(
+        jnp.int32
+    )
+    earlier = jnp.cumsum(onehot, axis=0) - onehot
+    rank = jnp.sum(earlier * onehot, axis=1)
+    return owners * slots + rank
+
+
+def ring_plan(gradients, owner_of, pair_flags, left_factor, right_factor):
     count, half, width = gradients.shape
     halves = lax.axis_size("dim")
     position = lax.axis_index("dim")
@@ -29,13 +53,7 @@
     owners_count = lax.axis_size("blk")
     slots = 3 * count // (2 * owners_count)
     block = owners_count * slots
-    owners = owner_of[:, 0]
-    onehot = (owners[:, None] == jnp.arange(owners_count, dtype=jnp.int32)[None, :]).astype(
-        jnp.int32
-    )
-    earlier = jnp.cumsum(onehot, axis=0) - onehot
-    rank = jnp.sum(earlier * onehot, axis=1)
-    target = owners * slots + rank
+    target = slot_targets(owner_of, owners_count, slots)
     placing = (jnp.arange(block, dtype=jnp.int32)[:, None] == target[None, :]).astype(jnp.bfloat16)
     outgoing = jnp.dot(placing, normed, preferred_element_type=jnp.float32).astype(jnp.bfloat16)
     outgoing = outgoing.reshape(owners_count, slots, half * width)
@@ -69,7 +87,405 @@
     return (summed, self_influence)
 
 
+def after(values, *deps):
+    return list(lax.optimization_barrier((tuple(values), deps))[0])
+
+
+def precondition_kernel(plan, notes, spot, own, other, left, right, *rest):
+    full, sums, parts = rest[-3:]
+    if notes:
+        slot_note, means_before, *outs, means, mean_sq = rest[:-3]
+    else:
+        *outs, mean_sq = rest[:-3]
+    here, core = spot[0], spot[2]
+    batch, half, width = own.shape
+    side = 2 * half
+    quads = len(plan)
+    straight = left[...]
+    turned = jnp.concatenate([straight[half:], straight[:half]], axis=0)
+    turned = jnp.concatenate([turned[:, half:], turned[:, :half]], axis=1)
+    factor = jnp.where(core == 0, straight, turned)
+    right_twice = jnp.concatenate([right[...]] * 2, axis=0)
+    for first in range(0, batch, GROUP):
+        for e in range(first, first + GROUP, 2):
+            pair = [jnp.concatenate([own[i], other[i]], axis=0) for i in (e, e + 1)]
+            sides = jnp.dot(
+                factor, jnp.concatenate(pair, axis=1), preferred_element_type=jnp.float32
+            )
+            for i in range(2):
+                term = sides[:, i * width : (i + 1) * width]
+                high = term.astype(jnp.bfloat16)
+                low = (term - high.astype(jnp.float32)).astype(jnp.bfloat16)
+                parts[pl.ds((e - first + i) * side, side), :] = jnp.concatenate(
+                    [high, low], axis=1
+                )
+        product = jnp.dot(parts[...], right_twice, preferred_element_type=jnp.float32)
+        full[pl.ds(first * side, GROUP * side), :] = product
+        squares = (product * product).reshape(GROUP, side // 8, 8, width)
+        sums[pl.ds(first * 8, GROUP * 8), :] = jnp.sum(squares, axis=1).reshape(GROUP * 8, width)
+    total = sums[pl.ds(0, batch, stride=8), :]
+    for s in range(1, 8):
+        total = total + sums[pl.ds(s, batch, stride=8), :]
+    mean = jnp.sum(total, axis=1, keepdims=True) / (side * width)
+    spread_mean = jnp.broadcast_to(mean, (batch, width))
+    step, steps = pl.program_id(0), pl.num_programs(0)
+    at = pl.ds(pl.multiple_of(step * batch, batch), batch)
+    mean_sq[at] = spread_mean
+    scale = lax.rsqrt(spread_mean + 1e-06)
+    slices = iter(outs)
+    for k in range(quads):
+        base = lax.bitwise_xor(here, k) * (half // quads)
+        row = 0
+        for wide in plan[k]:
+            out = next(slices)
+            for r in range(wide // width):
+                values = full[pl.ds(base + row, batch, stride=side), :]
+                out[at, r * width : (r + 1) * width] = (values * scale).astype(jnp.bfloat16)
+                row += 1
+    if notes:
+
+        @pl.when(step == steps - 1)
+        def _():
+            every = jnp.concatenate([means_before[...], mean_sq[...]], axis=0)
+            means[...] = every
+            eye = lax.broadcasted_iota(jnp.int32, (width, width), 0) == lax.broadcasted_iota(
+                jnp.int32, (width, width), 1
+            )
+            lanes = [
+                jnp.sum(jnp.where(eye, every[i : i + width], 0.0), axis=0, keepdims=True)
+                for i in range(0, every.shape[0], width)
+            ]
+            term = jnp.concatenate(lanes, axis=1)
+            terms = []
+            for _ in range(3):
+                terms.append(term.astype(jnp.bfloat16).astype(jnp.float32))
+                term = term - terms[-1]
+            number = lax.broadcasted_iota(jnp.int32, (NOTE, every.shape[0]), 0)
+            note = slot_note[...].astype(jnp.float32)
+            for i in range(3):
+                note = jnp.where(number == 2 + i, terms[i], note)
+            slices = iter(outs)
+            for k in range(quads):
+                out = next(slices)
+                rows = out.shape[0] - NOTE
+                out[rows:, :] = jnp.zeros((NOTE, out.shape[1]), jnp.bfloat16)
+                out[rows:, : every.shape[0]] = note.astype(jnp.bfloat16)
+                for _ in plan[k][1:]:
+                    next(slices)
+
+
+def precondition(spot, own, other, left, right, span, plan, slot_note=None, means_before=None):
+    _, half, width = own.shape
+    side = 2 * half
+    first, count, batch = span
+    notes = slot_note is not None
+    gradient_spec = pl.BlockSpec((batch, half, width), lambda i, s: (first // batch + i, 0, 0))
+    whole = lambda shape: pl.BlockSpec(shape, lambda i, s: (0, 0))
+    in_specs = [gradient_spec, gradient_spec, whole((side, side)), whole((width, width))]
+    operands = [own, other, left, right]
+    if notes:
+        in_specs += [whole(slot_note.shape), whole(means_before.shape)]
+        operands += [slot_note, means_before]
+    out_shape = [
+        jax.ShapeDtypeStruct((count + (NOTE if notes and f == 0 else 0), wide), jnp.bfloat16)
+        for widths in plan
+        for f, wide in enumerate(widths)
+    ]
+    if notes:
+        out_shape.append(jax.ShapeDtypeStruct((first + count, width), jnp.float32))
+    out_shape.append(jax.ShapeDtypeStruct((count, width), jnp.float32))
+    return pl.pallas_call(
+        functools.partial(precondition_kernel, plan, notes),
+        grid_spec=pltpu.PrefetchScalarGridSpec(
+            num_scalar_prefetch=1,
+            grid=(count // batch,),
+            in_specs=in_specs,
+            out_specs=[whole(out.shape) for out in out_shape],
+            scratch_shapes=[
+                pltpu.VMEM((batch * side, width), jnp.float32),
+                pltpu.VMEM((batch * 8, width), jnp.float32),
+                pltpu.VMEM((GROUP * side, 2 * width), jnp.bfloat16),
+            ],
+        ),
+        out_shape=out_shape,
+        compiler_params=pltpu.CompilerParams(vmem_limit_bytes=VMEM_BYTES),
+        cost_estimate=SMALL_COST,
+        name="precondition",
+    )(spot, *operands)
+
+
+def tiles_kernel(order, reach, shapes, based, spot, *rest):
+    owners, slots, early_rows, late_rows = shapes
+    quads = owners // 2
+    block = owners * slots
+    notes, inputs = rest[:owners], rest[owners : 3 * owners]
+    bases = rest[3 * owners : 3 * owners + 2 * reach] if based else ()
+    outs, cluster = rest[-2 * reach - 1 : -1], rest[-1]
+    here, side, core = spot[0], spot[1], spot[2]
+    count = early_rows + late_rows
+    depth = cluster.shape[3]
+    step = pl.program_id(0)
+
+    @pl.when(step == 0)
+    def _():
+        for source in range(owners):
+            note = notes[source][:, :count].astype(jnp.float32).astype(jnp.int32)
+            target = note[0:1] + note[1:2] * NOTE_BASE
+            slot_of = lax.broadcasted_iota(jnp.int32, (block, count), 0)
+            placing = (slot_of == target).astype(jnp.bfloat16)
+            early, late = inputs[2 * source : 2 * source + 2]
+            values = jnp.concatenate([early[...], late[:late_rows]], axis=0)
+            k, m = source % quads, source // quads
+            producer = 2 * lax.bitwise_xor(here, k) + lax.bitwise_xor(side, m)
+            placed = jnp.dot(placing, values, preferred_element_type=jnp.float32)
+            cluster[:, producer] = placed.astype(jnp.bfloat16).reshape(owners, slots, depth)
+
+    half = owners // 2
+    rows = half * slots
+
+    @pl.when(step > 0)
+    def _():
+        k = functools.reduce(lambda v, n: jnp.where(step == n + 1, order[n], v), range(quads), 0)
+        owner = 2 * lax.bitwise_xor(here, k) + side
+        ahead = [
+            cluster[
+                lax.rem(owner + j + 1, owners), pl.ds(lax.bitwise_xor(core, h) * half, half)
+            ].reshape(rows, depth)
+            for h in range(2)
+            for j in range(reach)
+        ]
+        product = lax.dot_general(
+            jnp.concatenate(ahead, axis=0),
+            cluster[owner].reshape(block, depth),
+            (((1,), (1,)), ((), ())),
+            preferred_element_type=jnp.float32,
+        )
+        for i in range(2 * reach):
+            part = product[i * rows : (i + 1) * rows]
+            outs[i][0] = part + bases[i][0] if based else part
+
+
+def partial_tiles(spot, notes, pieces, width, order, reach, slots, bases=()):
+    owners = len(pieces)
+    block = owners * slots
+    early_rows, late_rows = pieces[0][0][1][1], pieces[0][1][1][1]
+    in_specs, operands = [], []
+    for array, row in notes:
+        in_specs.append(
+            pl.BlockSpec((NOTE, 2 * NOTE_BASE), functools.partial(lambda r, i, s: (r, 0), row // NOTE))
+        )
+        operands.append(array)
+    for piece in pieces:
+        for array, (row, rows), column in piece:
+            if column % width or row % rows:
+                array, column, row = array[row : row + rows, column : column + width], 0, 0
+            in_specs.append(
+                pl.BlockSpec(
+                    (rows, width),
+                    functools.partial(lambda r, c, i, s: (r, c), row // rows, column // width),
+                )
+            )
+            operands.append(array)
+    shape = (len(order), block // 2, block)
+    tile_specs = [
+        pl.BlockSpec((1,) + shape[1:], lambda i, s: (jnp.maximum(i - 1, 0), 0, 0))
+    ] * (2 * reach)
+    return pl.pallas_call(
+        functools.partial(
+            tiles_kernel, order, reach, (owners, slots, early_rows, late_rows), bool(bases)
+        ),
+        grid_spec=pltpu.PrefetchScalarGridSpec(
+            num_scalar_prefetch=1,
+            grid=(1 + len(order),),
+            in_specs=in_specs + (tile_specs if bases else []),
+            out_specs=tile_specs,
+            scratch_shapes=[pltpu.VMEM((owners, owners, slots, width), jnp.bfloat16)],
+        ),
+        out_shape=[jax.ShapeDtypeStruct(shape, jnp.float32)] * (2 * reach),
+        compiler_params=pltpu.CompilerParams(vmem_limit_bytes=VMEM_BYTES),
+        cost_estimate=SMALL_COST,
+        name="partial_tiles",
+    )(spot, *operands, *bases)
+
+
+def split_plan(gradients, owner_of, pair_flags, left_factor, right_factor):
+    count, half, width = gradients.shape
+    feat = 2 * half * width
+    owners = lax.axis_size("blk")
+    quads = owners // 2
+    reach = pair_flags.shape[1]
+    slots = 3 * count // (2 * owners)
+    block = owners * slots
+    index = lax.axis_index("blk")
+    core = lax.axis_index("dim")
+    here, side = index // 2, index % 2
+    spot = jnp.stack([here, side, core]).astype(jnp.int32)
+
+    def across(x):
+        return lax.ppermute(x, "dim", [(0, 1), (1, 0)])
+
+    def along(x, k):
+        return lax.ppermute(x, "blk", [(i, i ^ (2 * k)) for i in range(owners)])
+
+    def beside(x):
+        return lax.ppermute(x, "blk", [(i, i ^ 1) for i in range(owners)])
+
+    def send(parts):
+        return [parts[0]] + [along(parts[k], k) for k in range(1, quads)]
+
+    first = FIRST
+    rest_count = count - first
+    features = half * width // quads
+    widths = [features * n // sum(SLICES) for n in SLICES]
+    other_first = across(gradients[:first])
+    (whole,) = after([gradients], other_first)
+    other = across(whole)
+
+    *parts, mean_early = precondition(
+        spot,
+        gradients,
+        other_first,
+        left_factor,
+        right_factor,
+        (0, first, first),
+        [[features]] * quads,
+    )
+    target = slot_targets(owner_of, owners, slots)
+    slot_note = jnp.stack([target % NOTE_BASE, target // NOTE_BASE] + [target] * (NOTE - 2))
+    slot_note = slot_note.astype(jnp.bfloat16)
+
+    *parts, mean_early, other, slot_note = after([*parts, mean_early, other, slot_note])
+    early = send(parts)
+    early.append(beside(early[0]))
+    own, *parts, means, _ = precondition(
+        spot,
+        gradients,
+        other,
+        left_factor,
+        right_factor,
+        (first, rest_count, STEP),
+        [[features]] + [widths] * (quads - 1),
+        slot_note,
+        mean_early,
+    )
+    *early, own = after([*early, own])
+    parts = after(parts, own)
+    early.append(beside(jnp.concatenate(early[1:quads], axis=0)))
+    order = [3, 1, 2, 0] if quads == 4 else list(reversed(range(quads)))
+    sums, notes, came, crossed = (), [], [], None
+    offset = 0
+    late = [None] * owners
+    for f in range(len(widths) + 1):
+        wide = widths[f] if f < len(widths) else 0
+        next_came, ready, next_crossed = [], [], None
+        if f < len(widths):
+            next_came = [along(parts[(k - 1) * len(widths) + f], k) for k in range(1, quads)]
+        if f == 0:
+            next_crossed = beside(own)
+        elif f < len(widths):
+            next_crossed = beside(jnp.concatenate(came, axis=0))
+        else:
+            next_crossed = [beside(part) for part in came]
+        if f >= 2:
+            sums = partial_tiles(spot, notes, pieces, widths[f - 2], order, reach, slots, sums)
+        tied = jax.tree.leaves((next_came, next_crossed, early, own, parts, sums))
+        held = after(tied)
+        structure = jax.tree.structure((next_came, next_crossed, early, own, parts, sums))
+        next_came, next_crossed, early, own, parts, sums = jax.tree.unflatten(structure, held)
+        if f == 0:
+            own_beside = next_crossed
+        else:
+            rows = came[0].shape[0]
+            if f < len(widths):
+                far = [(next_crossed, rows * k) for k in range(quads - 1)]
+            else:
+                far = [(part, 0) for part in next_crossed]
+            start = sum(widths[: f - 1])
+            late = [(own, 0)] + [(part, 0) for part in came] + [(own_beside, 0)] + far
+            first_rows = [(part, 0) for part in early[: quads + 1]]
+            first_rows += [(early[quads + 1], first * k) for k in range(quads - 1)]
+            if f == 1:
+                notes = [(array, row + rest_count) for array, row in late]
+            pieces = [
+                (
+                    (first_rows[s][0], (first_rows[s][1], first), start),
+                    (late[s][0], (late[s][1], rest_count), 0 if s % quads else start),
+                )
+                for s in range(owners)
+            ]
+        came = next_came
+    sums = partial_tiles(spot, notes, pieces, widths[-1], order, reach, slots, sums)
+
+    flags = lax.dynamic_index_in_dim(pair_flags, index, 0, keepdims=False).astype(jnp.float32)
+    ahead, behind = [], []
+    gathered = [across(sums[reach + j]) for j in range(reach)]
+    for j in range(reach):
+        total = {}
+        keep, got = sums[j], gathered[j]
+        if j < reach:
+            odd = keep[: quads // 2] + got[: quads // 2]
+            odd = along(odd, 1)
+            for n, k in enumerate(order[quads // 2 :]):
+                total[k] = keep[quads // 2 + n] + got[quads // 2 + n] + odd[n]
+            total = total[0] + along(total[2], 2)
+        else:
+            for n, k in enumerate(order):
+                total[k] = keep[n] + got[n]
+            total = sum([along(total[k], k) for k in order[:-1]], total[0])
+        tile = (total * (flags[j] * feat ** (-0.5))).astype(jnp.bfloat16)
+        ahead.append(tile)
+        turned = tile.T.reshape(2, block // 2, block // 2)
+        straight = lax.dynamic_index_in_dim(turned, core, 0, keepdims=False)
+        crossed = lax.dynamic_index_in_dim(turned, 1 - core, 0, keepdims=False)
+        by = j + 1
+        straight = from_behind(straight, "blk", by)
+        crossed = lax.ppermute(
+            crossed,
+            ("blk", "dim"),
+            [(2 * i + c, 2 * ((i + by) % owners) + 1 - c) for i in range(owners) for c in range(2)],
+        )
+        behind.append(
+            jnp.where(
+                core == 0,
+                jnp.concatenate([straight, crossed], axis=1),
+                jnp.concatenate([crossed, straight], axis=1),
+            )
+        )
+    tiles = jnp.stack(ahead + behind).swapaxes(1, 2)
+
+    note = jnp.stack([array[row : row + 5, :count] for array, row in notes]).astype(jnp.float32)
+    targets = note[:, 0:1].astype(jnp.int32) + note[:, 1:2].astype(jnp.int32) * NOTE_BASE
+    influences = jnp.log1p(note[:, 2:3] + note[:, 3:4] + note[:, 4:5])
+    wanted = index * slots + jnp.arange(slots, dtype=jnp.int32)
+    chosen = targets == wanted[None, :, None]
+    self_influence = jnp.sum(jnp.where(chosen, influences, 0.0), axis=2)
+    self_influence = lax.switch(
+        index,
+        [
+            functools.partial(
+                lambda i, x: jnp.stack(
+                    [x[(p ^ i) // 2 + (p ^ i) % 2 * quads] for p in range(owners)]
+                ).astype(jnp.bfloat16),
+                i,
+            )
+            for i in range(owners)
+        ],
+        self_influence,
+    )
+    return (tiles, self_influence.reshape(block))
+
+
 def solution(mesh):
+    owners = mesh.shape["blk"]
+
+    def per_device(gradients, owner_of, pair_flags, left_factor, right_factor):
+        block = 3 * gradients.shape[0] // 2
+        partial_bytes = 4 * owners * pair_flags.shape[1] * block * block // 2
+        quads = owners // 2
+        fits = partial_bytes <= PARTIAL_BYTES and quads == 4
+        plan = split_plan if fits and gradients.shape[0] % FIRST == 0 else ring_plan
+        return plan(gradients, owner_of, pair_flags, left_factor, right_factor)
+
     return jax.shard_map(
         per_device,
         mesh=mesh,

time: 818 us -> 262 us (0.32)
  the two profiles are of different devices: /device:TPU:5 before, /device:TPU:0 now
where the time goes in v3:
time: 262 us; the launch traced here: 261 us
  waiting for transfers between devices  108 us (41%)
  starting transfers between devices  55.1 us (21%)
  Pallas kernels  52.9 us (20%)
  other arithmetic  22.9 us (9%)
  local copies, waits for them, and re-layouts  19.6 us (7%)
  between operations  2.94 us (1%)
    ppermute x18, waiting for transfers between devices, along(): return lax.ppermute(x, 'blk', [(i, i ^ 2 * k) for i in range(owners)])  91.3 us
    ppermute x18, starting transfers between devices, along(): return lax.ppermute(x, 'blk', [(i, i ^ 2 * k) for i in range(owners)])  37.2 us
    pallas_call x3, Pallas kernels, partial_tiles(): pl.pallas_call(functools.partial(tiles_kernel, order, reach, (owners, slo...  32.4 us
    pallas_call x2, Pallas kernels, precondition(): pl.pallas_call(functools.partial(precondition_kernel, plan, notes), grid_...  20.5 us
    ppermute x8, starting transfers between devices, beside(): return lax.ppermute(x, 'blk', [(i, i ^ 1) for i in range(owners)])  9.67 us
    unnamed x5, other arithmetic  8.21 us
    ppermute x3, waiting for transfers between devices, from_behind(): lax.ppermute(shard, axis, [(i, (i + by) % peers) for i in range(peers)])  7.8 us
    unnamed x75, local copies, waits for them, and re-layouts  7.4 us
  transfers between devices with their start and end apart: 37, of which 14 were waited for; matrix products, arithmetic and copies ran while one was open for 14% of the time, Pallas kernels for 16%

profile of v3, /device:TPU:0, one launch (start us, length us, event | category | flops | bytes accessed | tf_op | source)
XLA Modules:
  0.0 261.0 jit_solution(6251443364882977635)
XLA Ops:
  8.0 6.2 %precondition.2 = (bf16[64,2048]{1,0:T(8,128)(2,1)}, bf16[64,2048]{1,0:T(8,128)(2,1)}, bf16[64,2048]{1,0:T(8,128)(2,1)}, bf16[64,2048]{1,0:T(8,128)(2,1)}, f32[64,128]{1,0:T(8,128)}) custom-call(s32[3]{0:T(128)} %pad_add_fusion.spot, bf16[256,64,128]{2,1,0:T(8,128)(2,1)} %own.3, bf16[64,64,128]{2,1,0:T(8,128)(2,1)} %copy-done.17, bf16[128,128]{1,0:T(8,128)(2,1)} %left.3, ...), custom_call_target="tpu_custom_call" | custom-call | flops 1048576 | bytes 65536 | tf_op jit(solution)/shard_map/precondition/pallas_call | solution.py:197
  14.2 2.7 %collective-permute-start.2 = (bf16[64,2048]{1,0:T(8,128)(2,1)}, bf16[64,2048]{1,0:T(8,128)(2,1)S(1)}, u32[]{:S(2)}, u32[]{:S(2)}) collective-permute-start(bf16[64,2048]{1,0:T(8,128)(2,1)} %get-tuple-element.644), channel_id=1, source_target_pairs={{0,4},{2,6},{4,0},{6,2},{8,12},{10,14},{12,8},{14,10},{1,5},{3,7},... | collective-permute-start | bytes 786440 | tf_op jit(solution)/shard_map/ppermute | solution.py:328
  21.3 14.3 %precondition.3 = (bf16[208,2048]{1,0:T(8,128)(2,1)}, bf16[208,768]{1,0:T(8,128)(2,1)}, bf16[192,768]{1,0:T(8,128)(2,1)}, bf16[192,512]{1,0:T(8,128)(2,1)}, bf16...) custom-call(s32[3]{0:T(128)} %pad_add_fusion.spot, ...), custom_call_target="tpu_custom_call" | custom-call | flops 1048576 | bytes 65536 | tf_op jit(solution)/shard_map/precondition/pallas_call | solution.py:197
  35.6 2.9 %collective-permute-done.3.rest_12_ = bf16[64,2048]{1,0:T(8,128)(2,1)S(1)} collective-permute-done((bf16[64,2048]{1,0:T(8,128)(2,1)}, bf16[64,2048]{1,0:T(8,128)(2,1)S(1)}, u32[]{:S(2)}, u32[]{:S(2)}) %collective-permute-start.3) | collective-permute-done | bytes 262176 | tf_op jit(solution)/shard_map/ppermute | solution.py:328
  40.8 5.3 %collective-permute-start.6 = (bf16[208,768]{1,0:T(8,128)(2,1)S(1)}, bf16[208,768]{1,0:T(8,128)(2,1)S(1)}, u32[]{:S(2)}, u32[]{:S(2)}) collective-permute-start(bf16[208,768]{1,0:T(8,128)(2,1)S(1)} %copy-done.29), channel_id=1, source_target_pairs={{0,4},{2,6},{4,0},{6,2},{8,12},{10,14},{12,8},{14,10},{1,5},{3,7},... | collective-permute-start | bytes 958472 | tf_op jit(solution)/shard_map/ppermute | solution.py:328
  48.6 9.3 %collective-permute-done.6.rest_1_.rest_11_ = bf16[208,768]{1,0:T(8,128)(2,1)S(1)} collective-permute-done((bf16[208,768]{1,0:T(8,128)(2,1)S(1)}, bf16[208,768]{1,0:T(8,128)(2,1)S(1)}, u32[]{:S(2)}, u32[]{:S(2)}) %collective-permute-start.6) | collective-permute-done | bytes 319520 | tf_op jit(solution)/shard_map/ppermute | solution.py:328
  57.9 13.2 %collective-permute-done.7.rest_2_.rest_13_ = bf16[208,768]{1,0:T(8,128)(2,1)S(1)} collective-permute-done((bf16[208,768]{1,0:T(8,128)(2,1)S(1)}, bf16[208,768]{1,0:T(8,128)(2,1)S(1)}, u32[]{:S(2)}, u32[]{:S(2)}) %collective-permute-start.7) | collective-permute-done | bytes 319520 | tf_op jit(solution)/shard_map/ppermute | solution.py:328
  71.1 3.8 %collective-permute-done.10.rest_18_.rest_20_.rest_22_ = bf16[192,2048]{1,0:T(8,128)(2,1)S(1)} collective-permute-done((bf16[192,2048]{1,0:T(8,128)(2,1)S(1)}, bf16[192,2048]{1,0:T(8,128)(2,1)S(1)}, u32[]{:S(2)}, u32[]{:S(2)}) %collective-permute-start.10) | collective-permute-done | bytes 786464 | tf_op jit(solution)/shard_map/ppermute | solution.py:331
  76.7 6.0 %collective-permute-start.11 = (bf16[192,768]{1,0:T(8,128)(2,1)S(1)}, bf16[192,768]{1,0:T(8,128)(2,1)S(1)}, u32[]{:S(2)}, u32[]{:S(2)}) collective-permute-start(bf16[192,768]{1,0:T(8,128)(2,1)S(1)} %copy-done.32), channel_id=1, source_target_pairs={{0,4},{2,6},{4,0},{6,2},{8,12},{10,14},{12,8},{14,10},{1,5},{3,7},... | collective-permute-start | bytes 884744 | tf_op jit(solution)/shard_map/ppermute | solution.py:328
  85.3 7.1 %collective-permute-done.11.rest_11_ = bf16[192,768]{1,0:T(8,128)(2,1)S(1)} collective-permute-done((bf16[192,768]{1,0:T(8,128)(2,1)S(1)}, bf16[192,768]{1,0:T(8,128)(2,1)S(1)}, u32[]{:S(2)}, u32[]{:S(2)}) %collective-permute-start.11) | collective-permute-done | bytes 294944 | tf_op jit(solution)/shard_map/ppermute | solution.py:328
  92.4 13.8 %collective-permute-done.12.rest_13_ = bf16[192,768]{1,0:T(8,128)(2,1)S(1)} collective-permute-done((bf16[192,768]{1,0:T(8,128)(2,1)S(1)}, bf16[192,768]{1,0:T(8,128)(2,1)S(1)}, u32[]{:S(2)}, u32[]{:S(2)}) %collective-permute-start.12) | collective-permute-done | bytes 294944 | tf_op jit(solution)/shard_map/ppermute | solution.py:328
  111.1 3.1 %collective-permute-start.15 = (bf16[192,512]{1,0:T(8,128)(2,1)}, bf16[192,512]{1,0:T(8,128)(2,1)S(1)}, u32[]{:S(2)}, u32[]{:S(2)}) collective-permute-start(bf16[192,512]{1,0:T(8,128)(2,1)} %get-tuple-element.682), channel_id=1, source_target_pairs={{0,4},{2,6},{4,0},{6,2},{8,12},{10,14},{12,8},{14,10},{1,5},{3,7},... | collective-permute-start | bytes 589832 | tf_op jit(solution)/shard_map/ppermute | solution.py:328
  117.5 10.2 %partial_tiles.3 = (f32[4,192,384]{2,1,0:T(8,128)}, f32[4,192,384]{2,1,0:T(8,128)}, f32[4,192,384]{2,1,0:T(8,128)}, f32[4,192,384]{2,1,0:T(8,128)}, f32[4,192,384]{2,1,0:T(8,128)}, /*index=5*/f32[4,192,384]{2,1,0:T(8,128)}) custom-call(s32[3]{0:T(128)} %pad_add_fusion.spot, bf16[208,2048]{1,0:T(8,128)(2,1)} %get-tuple-element.724.rest_0_.rest_9_, ...), custom_call_target="tpu_custom_call" | custom-call | flops 1048576 | bytes 65536 | tf_op jit(solution)/shard_map/partial_tiles/pallas_call | solution.py:293
  133.0 11.9 %partial_tiles.4 = (f32[4,192,384]{2,1,0:T(8,128)}, f32[4,192,384]{2,1,0:T(8,128)}, f32[4,192,384]{2,1,0:T(8,128)}, f32[4,192,384]{2,1,0:T(8,128)}, f32[4,192,384]{2,1,0:T(8,128)}, /*index=5*/f32[4,192,384]{2,1,0:T(8,128)}) custom-call(s32[3]{0:T(128)} %pad_add_fusion.spot, bf16[208,2048]{1,0:T(8,128)(2,1)} %get-tuple-element.724.rest_0_.rest_9_, ...), custom_call_target="tpu_custom_call" | custom-call | flops 1048576 | bytes 65536 | tf_op jit(solution)/shard_map/partial_tiles/pallas_call | solution.py:293
  145.8 10.3 %partial_tiles.5 = (f32[4,192,384]{2,1,0:T(8,128)}, f32[4,192,384]{2,1,0:T(8,128)}, f32[4,192,384]{2,1,0:T(8,128)}, f32[4,192,384]{2,1,0:T(8,128)}, f32[4,192,384]{2,1,0:T(8,128)}, /*index=5*/f32[4,192,384]{2,1,0:T(8,128)}) custom-call(s32[3]{0:T(128)} %pad_add_fusion.spot, bf16[208,2048]{1,0:T(8,128)(2,1)} %get-tuple-element.724.rest_0_.rest_9_, ...), custom_call_target="tpu_custom_call" | custom-call | flops 1048576 | bytes 65536 | tf_op jit(solution)/shard_map/partial_tiles/pallas_call | solution.py:293
  163.8 2.6 collective-permute-start.23
  170.9 4.2 %conditional.3 = (bf16[384]{0:T(512)(128)(2,1)S(1)}) conditional(s32[]{:T(128)} %clamp.3, (s32[8,1,256]{2,1,0:T(1,128)S(1)}, s32[8,1,256]{2,1,0:T(1,128)S(1)}, s32[]{:T(128)}, s32[1,48,1]{1,2,0:T(1,128)}, f32[8,5,256]{2,1,0:T(8,128)S(1)}) %tuple.111, (s32[8,1,256]{2,1,0:T(1,128)S(1)}, s32[8,1,256]{2,1,0:T(1,128)S(1)}, ...), branch_computations={%region_3.5_spmd, %region_5.7_spmd, %region_7.9_spmd, %region_9.11... | conditional | flops 302769 | bytes 161624
  175.1 5.8 %collective-permute-done.23 = f32[2,192,384]{2,1,0:T(8,128)} collective-permute-done((f32[2,192,384]{2,1,0:T(8,128)}, f32[2,192,384]{2,1,0:T(8,128)}, u32[]{:S(2)}, u32[]{:S(2)}) %collective-permute-start.23) | collective-permute-done | bytes 589856 | tf_op jit(solution)/shard_map/ppermute | solution.py:328
  182.1 3.9 %collective-permute-start.24 = (f32[192,384]{1,0:T(8,128)S(1)}, f32[192,384]{1,0:T(8,128)S(1)}, u32[]{:S(2)}, u32[]{:S(2)}) collective-permute-start(f32[192,384]{1,0:T(8,128)S(1)} %fusion.34), channel_id=1, source_target_pairs={{0,8},{2,10},{4,12},{6,14},{8,0},{10,2},{12,4},{14,6},{1,9},{3,11}... | collective-permute-start | bytes 884744 | tf_op jit(solution)/shard_map/ppermute | solution.py:328
  186.0 13.9 %collective-permute-done.29 = f32[2,192,384]{2,1,0:T(8,128)} collective-permute-done((f32[2,192,384]{2,1,0:T(8,128)}, f32[2,192,384]{2,1,0:T(8,128)}, u32[]{:S(2)}, u32[]{:S(2)}) %collective-permute-start.29) | collective-permute-done | bytes 589856 | tf_op jit(solution)/shard_map/ppermute | solution.py:328
  203.0 13.3 %collective-permute-done.26 = f32[2,192,384]{2,1,0:T(8,128)} collective-permute-done((f32[2,192,384]{2,1,0:T(8,128)}, f32[2,192,384]{2,1,0:T(8,128)}, u32[]{:S(2)}, u32[]{:S(2)}) %collective-permute-start.26) | collective-permute-done | bytes 589856 | tf_op jit(solution)/shard_map/ppermute | solution.py:328
  224.9 11.8 %collective-permute-done.27 = f32[192,384]{1,0:T(8,128)} collective-permute-done((f32[192,384]{1,0:T(8,128)}, f32[192,384]{1,0:T(8,128)}, u32[]{:S(2)}, u32[]{:S(2)}) %collective-permute-start.27) | collective-permute-done | bytes 294944 | tf_op jit(solution)/shard_map/ppermute | solution.py:328
  242.6 3.8 %collective-permute-start.35 = (bf16[192,192]{1,0:T(8,128)(2,1)S(1)}, bf16[192,192]{1,0:T(8,128)(2,1)S(1)}, u32[]{:S(2)}, u32[]{:S(2)}) collective-permute-start(bf16[192,192]{1,0:T(8,128)(2,1)S(1)} %bitcast.161), channel_id=1, source_target_pairs={{0,6},{2,8},{4,10},{6,12},{8,14},{10,0},{12,2},{14,4},{1,7},{3,9},... | collective-permute-start | bytes 221192 | tf_op jit(solution)/shard_map/ppermute | solution.py:23
  250.2 7.8 %collective-permute-done.35 = bf16[192,192]{1,0:T(8,128)(2,1)S(1)} collective-permute-done((bf16[192,192]{1,0:T(8,128)(2,1)S(1)}, bf16[192,192]{1,0:T(8,128)(2,1)S(1)}, u32[]{:S(2)}, u32[]{:S(2)}) %collective-permute-start.35) | collective-permute-done | bytes 73760 | tf_op jit(solution)/shard_map/ppermute | solution.py:23
  (180 shorter events, 75.0 us)
Async XLA Ops:
  14.2 21.4 %collective-permute-start.2 = (bf16[64,2048]{1,0:T(8,128)(2,1)}, bf16[64,2048]{1,0:T(8,128)(2,1)S(1)}, u32[]{:S(2)}, u32[]{:S(2)}) collective-permute-start(bf16[64,2048]{1,0:T(8,128)(2,1)} %get-tuple-element.644), channel_id=1, source_target_pairs={{0,4},{2,6},{4,0},{6,2},{8,12},{10,14},{12,8},{14,10},{1,5},{3,7},... | collective-permute-start | bytes 786440 | tf_op jit(solution)/shard_map/ppermute | solution.py:328
  17.0 21.6 %collective-permute-start.3 = (bf16[64,2048]{1,0:T(8,128)(2,1)}, bf16[64,2048]{1,0:T(8,128)(2,1)S(1)}, u32[]{:S(2)}, u32[]{:S(2)}) collective-permute-start(bf16[64,2048]{1,0:T(8,128)(2,1)} %get-tuple-element.645), channel_id=1, source_target_pairs={{0,8},{2,10},{4,12},{6,14},{8,0},{10,2},{12,4},{14,6},{1,9},{3,11}... | collective-permute-start | bytes 786440 | tf_op jit(solution)/shard_map/ppermute | solution.py:328
  19.5 19.0 %collective-permute-start.4 = (bf16[64,2048]{1,0:T(8,128)(2,1)}, bf16[64,2048]{1,0:T(8,128)(2,1)S(1)}, u32[]{:S(2)}, u32[]{:S(2)}) collective-permute-start(bf16[64,2048]{1,0:T(8,128)(2,1)} %get-tuple-element.646), channel_id=1, source_target_pairs={{0,12},{2,14},{4,8},{6,10},{8,4},{10,6},{12,0},{14,2},{1,13},{3,15... | collective-permute-start | bytes 786440 | tf_op jit(solution)/shard_map/ppermute | solution.py:328
  19.5 19.0 %collective-permute-start.5 = (bf16[64,2048]{1,0:T(8,128)(2,1)}, bf16[64,2048]{1,0:T(8,128)(2,1)S(1)}, u32[]{:S(2)}, u32[]{:S(2)}) collective-permute-start(bf16[64,2048]{1,0:T(8,128)(2,1)} %get-tuple-element.723.rest_8_), channel_id=1, source_target_pairs={{0,2},{2,0},{4,6},{6,4},{8,10},{10,8},{12,14},{14,12},{1,3},{3,1},... | collective-permute-start | bytes 786440 | tf_op jit(solution)/shard_map/ppermute | solution.py:331
  38.5 36.5 %collective-permute-start.9 = (bf16[208,2048]{1,0:T(8,128)(2,1)}, bf16[208,2048]{1,0:T(8,128)(2,1)S(1)}, u32[]{:S(2)}, u32[]{:S(2)}) collective-permute-start(bf16[208,2048]{1,0:T(8,128)(2,1)} %get-tuple-element.724.rest_0_.rest_9_), channel_id=1, source_target_pairs={{0,2},{2,0},{4,6},{6,4},{8,10},{10,8},{12,14},{14,12},{1,3},{3,1},... | collective-permute-start | bytes 2555912 | tf_op jit(solution)/shard_map/ppermute | solution.py:331
  40.2 34.8 %collective-permute-start.10 = (bf16[192,2048]{1,0:T(8,128)(2,1)S(1)}, bf16[192,2048]{1,0:T(8,128)(2,1)S(1)}, u32[]{:S(2)}, u32[]{:S(2)}) collective-permute-start(bf16[192,2048]{1,0:T(8,128)(2,1)S(1)} %pad_maximum_fusion.2), channel_id=1, source_target_pairs={{0,2},{2,0},{4,6},{6,4},{8,10},{10,8},{12,14},{14,12},{1,3},{3,1},... | collective-permute-start | bytes 2359304 | tf_op jit(solution)/shard_map/ppermute | solution.py:331
  40.8 17.1 %collective-permute-start.6 = (bf16[208,768]{1,0:T(8,128)(2,1)S(1)}, bf16[208,768]{1,0:T(8,128)(2,1)S(1)}, u32[]{:S(2)}, u32[]{:S(2)}) collective-permute-start(bf16[208,768]{1,0:T(8,128)(2,1)S(1)} %copy-done.29), channel_id=1, source_target_pairs={{0,4},{2,6},{4,0},{6,2},{8,12},{10,14},{12,8},{14,10},{1,5},{3,7},... | collective-permute-start | bytes 958472 | tf_op jit(solution)/shard_map/ppermute | solution.py:328
  46.1 25.1 %collective-permute-start.7 = (bf16[208,768]{1,0:T(8,128)(2,1)S(1)}, bf16[208,768]{1,0:T(8,128)(2,1)S(1)}, u32[]{:S(2)}, u32[]{:S(2)}) collective-permute-start(bf16[208,768]{1,0:T(8,128)(2,1)S(1)} %copy-done.28), channel_id=1, source_target_pairs={{0,8},{2,10},{4,12},{6,14},{8,0},{10,2},{12,4},{14,6},{1,9},{3,11}... | collective-permute-start | bytes 958472 | tf_op jit(solution)/shard_map/ppermute | solution.py:328
  47.1 24.0 %collective-permute-start.8 = (bf16[208,768]{1,0:T(8,128)(2,1)S(1)}, bf16[208,768]{1,0:T(8,128)(2,1)S(1)}, u32[]{:S(2)}, u32[]{:S(2)}) collective-permute-start(bf16[208,768]{1,0:T(8,128)(2,1)S(1)} %copy-done.27), channel_id=1, source_target_pairs={{0,12},{2,14},{4,8},{6,10},{8,4},{10,6},{12,0},{14,2},{1,13},{3,15... | collective-permute-start | bytes 958472 | tf_op jit(solution)/shard_map/ppermute | solution.py:328
  75.1 31.1 %collective-permute-start.14 = (bf16[624,768]{1,0:T(8,128)(2,1)S(1)}, bf16[624,768]{1,0:T(8,128)(2,1)S(1)}, u32[]{:S(2)}, u32[]{:S(2)}) collective-permute-start(bf16[624,768]{1,0:T(8,128)(2,1)S(1)} %pad_maximum_fusion), channel_id=1, source_target_pairs={{0,2},{2,0},{4,6},{6,4},{8,10},{10,8},{12,14},{14,12},{1,3},{3,1},... | collective-permute-start | bytes 2875400 | tf_op jit(solution)/shard_map/ppermute | solution.py:331
  76.7 15.7 %collective-permute-start.11 = (bf16[192,768]{1,0:T(8,128)(2,1)S(1)}, bf16[192,768]{1,0:T(8,128)(2,1)S(1)}, u32[]{:S(2)}, u32[]{:S(2)}) collective-permute-start(bf16[192,768]{1,0:T(8,128)(2,1)S(1)} %copy-done.32), channel_id=1, source_target_pairs={{0,4},{2,6},{4,0},{6,2},{8,12},{10,14},{12,8},{14,10},{1,5},{3,7},... | collective-permute-start | bytes 884744 | tf_op jit(solution)/shard_map/ppermute | solution.py:328
  82.8 23.4 %collective-permute-start.12 = (bf16[192,768]{1,0:T(8,128)(2,1)S(1)}, bf16[192,768]{1,0:T(8,128)(2,1)S(1)}, u32[]{:S(2)}, u32[]{:S(2)}) collective-permute-start(bf16[192,768]{1,0:T(8,128)(2,1)S(1)} %copy-done.31), channel_id=1, source_target_pairs={{0,8},{2,10},{4,12},{6,14},{8,0},{10,2},{12,4},{14,6},{1,9},{3,11}... | collective-permute-start | bytes 884744 | tf_op jit(solution)/shard_map/ppermute | solution.py:328
  83.8 22.3 %collective-permute-start.13 = (bf16[192,768]{1,0:T(8,128)(2,1)S(1)}, bf16[192,768]{1,0:T(8,128)(2,1)S(1)}, u32[]{:S(2)}, u32[]{:S(2)}) collective-permute-start(bf16[192,768]{1,0:T(8,128)(2,1)S(1)} %copy-done.30), channel_id=1, source_target_pairs={{0,12},{2,14},{4,8},{6,10},{8,4},{10,6},{12,0},{14,2},{1,13},{3,15... | collective-permute-start | bytes 884744 | tf_op jit(solution)/shard_map/ppermute | solution.py:328
  108.0 20.7 %collective-permute-start.18 = (bf16[576,768]{1,0:T(8,128)(2,1)}, bf16[576,768]{1,0:T(8,128)(2,1)}, u32[]{:S(2)}, u32[]{:S(2)}) collective-permute-start(bf16[576,768]{1,0:T(8,128)(2,1)} %pad_maximum_fusion.1), channel_id=1, source_target_pairs={{0,2},{2,0},{4,6},{6,4},{8,10},{10,8},{12,14},{14,12},{1,3},{3,1},... | collective-permute-start | bytes 2654216 | tf_op jit(solution)/shard_map/ppermute | solution.py:331
  111.1 17.3 %collective-permute-start.15 = (bf16[192,512]{1,0:T(8,128)(2,1)}, bf16[192,512]{1,0:T(8,128)(2,1)S(1)}, u32[]{:S(2)}, u32[]{:S(2)}) collective-permute-start(bf16[192,512]{1,0:T(8,128)(2,1)} %get-tuple-element.682), channel_id=1, source_target_pairs={{0,4},{2,6},{4,0},{6,2},{8,12},{10,14},{12,8},{14,10},{1,5},{3,7},... | collective-permute-start | bytes 589832 | tf_op jit(solution)/shard_map/ppermute | solution.py:328
  128.7 16.3 %collective-permute-start.19 = (bf16[192,512]{1,0:T(8,128)(2,1)S(1)}, bf16[192,512]{1,0:T(8,128)(2,1)S(1)}, u32[]{:S(2)}, u32[]{:S(2)}) collective-permute-start(bf16[192,512]{1,0:T(8,128)(2,1)S(1)} %collective-permute-done.15.rest_11_), channel_id=1, source_target_pairs={{0,2},{2,0},{4,6},{6,4},{8,10},{10,8},{12,14},{14,12},{1,3},{3,1},... | collective-permute-start | bytes 589832 | tf_op jit(solution)/shard_map/ppermute | solution.py:331
  163.8 17.1 %collective-permute-start.23 = (f32[2,192,384]{2,1,0:T(8,128)}, f32[2,192,384]{2,1,0:T(8,128)}, u32[]{:S(2)}, u32[]{:S(2)}) collective-permute-start(f32[2,192,384]{2,1,0:T(8,128)} %slice_add_fusion.18), channel_id=1, source_target_pairs={{0,4},{2,6},{4,0},{6,2},{8,12},{10,14},{12,8},{14,10},{1,5},{3,7},... | collective-permute-start | bytes 1769480 | tf_op jit(solution)/shard_map/ppermute | solution.py:328
  167.3 32.6 %collective-permute-start.29 = (f32[2,192,384]{2,1,0:T(8,128)}, f32[2,192,384]{2,1,0:T(8,128)}, u32[]{:S(2)}, u32[]{:S(2)}) collective-permute-start(f32[2,192,384]{2,1,0:T(8,128)} %slice_add_fusion.16), channel_id=1, source_target_pairs={{0,4},{2,6},{4,0},{6,2},{8,12},{10,14},{12,8},{14,10},{1,5},{3,7},... | collective-permute-start | bytes 1769480 | tf_op jit(solution)/shard_map/ppermute | solution.py:328
  168.3 48.0 %collective-permute-start.26 = (f32[2,192,384]{2,1,0:T(8,128)}, f32[2,192,384]{2,1,0:T(8,128)}, u32[]{:S(2)}, u32[]{:S(2)}) collective-permute-start(f32[2,192,384]{2,1,0:T(8,128)} %slice_add_fusion.17), channel_id=1, source_target_pairs={{0,4},{2,6},{4,0},{6,2},{8,12},{10,14},{12,8},{14,10},{1,5},{3,7},... | collective-permute-start | bytes 1769480 | tf_op jit(solution)/shard_map/ppermute | solution.py:328
  182.1 36.0 %collective-permute-start.24 = (f32[192,384]{1,0:T(8,128)S(1)}, f32[192,384]{1,0:T(8,128)S(1)}, u32[]{:S(2)}, u32[]{:S(2)}) collective-permute-start(f32[192,384]{1,0:T(8,128)S(1)} %fusion.34), channel_id=1, source_target_pairs={{0,8},{2,10},{4,12},{6,14},{8,0},{10,2},{12,4},{14,6},{1,9},{3,11}... | collective-permute-start | bytes 884744 | tf_op jit(solution)/shard_map/ppermute | solution.py:328
  201.6 38.5 %collective-permute-start.30 = (f32[192,384]{1,0:T(8,128)}, f32[192,384]{1,0:T(8,128)}, u32[]{:S(2)}, u32[]{:S(2)}) collective-permute-start(f32[192,384]{1,0:T(8,128)} %fusion.24), channel_id=1, source_target_pairs={{0,8},{2,10},{4,12},{6,14},{8,0},{10,2},{12,4},{14,6},{1,9},{3,11}... | collective-permute-start | bytes 884744 | tf_op jit(solution)/shard_map/ppermute | solution.py:328
  218.1 18.5 %collective-permute-start.27 = (f32[192,384]{1,0:T(8,128)}, f32[192,384]{1,0:T(8,128)}, u32[]{:S(2)}, u32[]{:S(2)}) collective-permute-start(f32[192,384]{1,0:T(8,128)} %fusion.29), channel_id=1, source_target_pairs={{0,8},{2,10},{4,12},{6,14},{8,0},{10,2},{12,4},{14,6},{1,9},{3,11}... | collective-permute-start | bytes 884744 | tf_op jit(solution)/shard_map/ppermute | solution.py:328
  223.4 23.2 %collective-permute-start.31 = (bf16[192,192]{1,0:T(8,128)(2,1)}, bf16[192,192]{1,0:T(8,128)(2,1)}, u32[]{:S(2)}, u32[]{:S(2)}) collective-permute-start(bf16[192,192]{1,0:T(8,128)(2,1)} %get-tuple-element.861), channel_id=1, source_target_pairs={{0,2},{2,4},{4,6},{6,8},{8,10},{10,12},{12,14},{14,0},{1,3},{3,5},... | collective-permute-start | bytes 221192 | tf_op jit(solution)/shard_map/ppermute | solution.py:23
  223.9 23.7 %collective-permute-start.32 = (bf16[192,192]{1,0:T(8,128)(2,1)}, bf16[192,192]{1,0:T(8,128)(2,1)}, u32[]{:S(2)}, u32[]{:S(2)}) collective-permute-start(bf16[192,192]{1,0:T(8,128)(2,1)} %get-tuple-element.862), channel_id=1, source_target_pairs={{0,3},{1,2},{2,5},{3,4},{4,7},{5,6},{6,9},{7,8},{8,11},{9,10},{10,... | collective-permute-start | bytes 221192 | tf_op jit(solution)/shard_map/ppermute | solution.py:442
  (47 other events, 843.2 us)

commit v4 on v3

--- a/solution.py
+++ b/solution.py
@@ -14,7 +14,7 @@
 NOTE_BASE = 256
 GROUP = 8
 STEP = 32
-VMEM_BYTES = 56 * 2**20
+VMEM_BYTES = 30 * 2**20
 SMALL_COST = pl.CostEstimate(flops=2**20, bytes_accessed=2**16, transcendentals=0)
 
 
@@ -308,6 +308,38 @@
     )(spot, *operands, *bases)
 
 
+def finish_kernel(spot, flags, *rest):
+    *terms, tile, straight, crossed = rest
+    total = sum([term[...] for term in terms[1:]], terms[0][...])
+    done = (total * flags[0]).astype(tile.dtype)
+    tile[...] = done
+    turned = done.astype(jnp.float32).T.astype(tile.dtype)
+    half = turned.shape[0] // 2
+    core = spot[2]
+    first, second = turned[:half], turned[half:]
+    straight[...] = jnp.where(core == 0, first, second)
+    crossed[...] = jnp.where(core == 0, second, first)
+
+
+def finish(spot, factor, terms):
+    rows, block = terms[0].shape
+    spec = lambda shape: pl.BlockSpec(shape, lambda i, s, f: (0, 0))
+    out = [(rows, block), (rows, rows), (rows, rows)]
+    return pl.pallas_call(
+        finish_kernel,
+        grid_spec=pltpu.PrefetchScalarGridSpec(
+            num_scalar_prefetch=2,
+            grid=(1,),
+            in_specs=[spec(term.shape) for term in terms],
+            out_specs=[spec(shape) for shape in out],
+        ),
+        out_shape=[jax.ShapeDtypeStruct(shape, jnp.bfloat16) for shape in out],
+        compiler_params=pltpu.CompilerParams(vmem_limit_bytes=VMEM_BYTES),
+        cost_estimate=SMALL_COST,
+        name="finish",
+    )(spot, factor, *terms)
+
+
 def split_plan(gradients, owner_of, pair_flags, left_factor, right_factor):
     count, half, width = gradients.shape
     feat = 2 * half * width
@@ -337,13 +369,14 @@
     rest_count = count - first
     features = half * width // quads
     widths = [features * n // sum(SLICES) for n in SLICES]
-    other_first = across(gradients[:first])
+    own_first = gradients[:first]
+    other_first = across(own_first)
     (whole,) = after([gradients], other_first)
     other = across(whole)
 
     *parts, mean_early = precondition(
         spot,
-        gradients,
+        own_first,
         other_first,
         left_factor,
         right_factor,
@@ -354,7 +387,7 @@
     slot_note = jnp.stack([target % NOTE_BASE, target // NOTE_BASE] + [target] * (NOTE - 2))
     slot_note = slot_note.astype(jnp.bfloat16)
 
-    *parts, mean_early, other, slot_note = after([*parts, mean_early, other, slot_note])
+    *parts, mean_early, slot_note = after([*parts, mean_early, slot_note])
     early = send(parts)
     early.append(beside(early[0]))
     own, *parts, means, _ = precondition(
@@ -370,45 +403,42 @@
     )
     *early, own = after([*early, own])
     parts = after(parts, own)
-    early.append(beside(jnp.concatenate(early[1:quads], axis=0)))
-    order = [3, 1, 2, 0] if quads == 4 else list(reversed(range(quads)))
-    sums, notes, came, crossed = (), [], [], None
-    offset = 0
-    late = [None] * owners
+    order = [3, 1, 2, 0]
+    sums, notes, came = (), [], []
+    own_beside = None
+    start = 0
     for f in range(len(widths) + 1):
-        wide = widths[f] if f < len(widths) else 0
-        next_came, ready, next_crossed = [], [], None
+        next_came = []
         if f < len(widths):
             next_came = [along(parts[(k - 1) * len(widths) + f], k) for k in range(1, quads)]
         if f == 0:
-            next_crossed = beside(own)
-        elif f < len(widths):
-            next_crossed = beside(jnp.concatenate(came, axis=0))
+            own_beside = beside(own)
+            early.append(beside(jnp.concatenate(early[1 : quads - 1], axis=0)))
+        if f == 1:
+            early.append(beside(early[quads - 1]))
+        if f < len(widths):
+            crossed = [beside(jnp.concatenate(came, axis=0))] if came else []
         else:
-            next_crossed = [beside(part) for part in came]
+            crossed = [beside(part) for part in came]
         if f >= 2:
             sums = partial_tiles(spot, notes, pieces, widths[f - 2], order, reach, slots, sums)
-        tied = jax.tree.leaves((next_came, next_crossed, early, own, parts, sums))
-        held = after(tied)
-        structure = jax.tree.structure((next_came, next_crossed, early, own, parts, sums))
-        next_came, next_crossed, early, own, parts, sums = jax.tree.unflatten(structure, held)
-        if f == 0:
-            own_beside = next_crossed
-        else:
+        every = (next_came, came, crossed, early, own, own_beside, parts, list(sums))
+        leaves, structure = jax.tree.flatten(every)
+        every = jax.tree.unflatten(structure, after(leaves))
+        next_came, came, crossed, early, own, own_beside, parts, sums = every
+        if f:
             rows = came[0].shape[0]
-            if f < len(widths):
-                far = [(next_crossed, rows * k) for k in range(quads - 1)]
-            else:
-                far = [(part, 0) for part in next_crossed]
-            start = sum(widths[: f - 1])
-            late = [(own, 0)] + [(part, 0) for part in came] + [(own_beside, 0)] + far
-            first_rows = [(part, 0) for part in early[: quads + 1]]
-            first_rows += [(early[quads + 1], first * k) for k in range(quads - 1)]
+            late = [(own, 0)] + [(part, 0) for part in came] + [(own_beside, 0)]
+            late += [(crossed[0], rows * k) for k in range(quads - 1)][: len(came) * (f < len(widths))]
+            late += [(part, 0) for part in crossed][: len(came) * (f == len(widths))]
+            head = [(part, 0) for part in early[: quads + 1]]
+            head += [(early[quads + 1], first * k) for k in range(quads - 2)] + [(early[-1], 0)]
             if f == 1:
                 notes = [(array, row + rest_count) for array, row in late]
+            start = sum(widths[: f - 1])
             pieces = [
                 (
-                    (first_rows[s][0], (first_rows[s][1], first), start),
+                    (head[s][0], (head[s][1], first), start),
                     (late[s][0], (late[s][1], rest_count), 0 if s % quads else start),
                 )
                 for s in range(owners)
@@ -417,42 +447,52 @@
     sums = partial_tiles(spot, notes, pieces, widths[-1], order, reach, slots, sums)
 
     flags = lax.dynamic_index_in_dim(pair_flags, index, 0, keepdims=False).astype(jnp.float32)
-    ahead, behind = [], []
-    gathered = [across(sums[reach + j]) for j in range(reach)]
+    ahead, behind = [None] * reach, [None] * reach
+    gathered = [across(sums[reach + j]) for j in reversed(range(reach))][::-1]
+    def back(x, by, turn):
+        pairs = [
+            (2 * i + c, 2 * ((i + by) % owners) + (1 - c if turn else c))
+            for i in range(owners)
+            for c in range(2)
+        ]
+        return lax.ppermute(x, ("blk", "dim"), pairs)
+
+    spans = list(reversed(range(reach)))
+    odds, evens, nears, fars = {}, {}, {}, {}
+    for j in spans:
+        keep, got = sums[j], gathered[j]
+        odds[j] = along(keep[: quads // 2] + got[: quads // 2], 1)
+        evens[j] = [keep[2] + got[2], keep[3] + got[3]]
+
+    def halve(j):
+        nears[j] = evens[j][1] + odds[j][1]
+        fars[j] = along(evens[j][0] + odds[j][0], 2)
+
+    def complete(j):
+        factor = (flags[j] * feat ** (-0.5)).reshape(1)
+        ahead[j], straight, crossed = finish(spot, factor, [nears[j], fars[j]])
+        straight, crossed = back(straight, j + 1, False), back(crossed, j + 1, True)
+        behind[j] = [straight, crossed]
+
+    for n, j in enumerate(spans):
+        if n > 1:
+            complete(spans[n - 2])
+            (odds[j],) = after([odds[j]], ahead[spans[n - 2]], *behind[spans[n - 2]])
+        halve(j)
+    for n in range(max(0, reach - 2), reach):
+        j = spans[n]
+        complete(j)
     for j in range(reach):
-        total = {}
-        keep, got = sums[j], gathered[j]
-        if j < reach:
-            odd = keep[: quads // 2] + got[: quads // 2]
-            odd = along(odd, 1)
-            for n, k in enumerate(order[quads // 2 :]):
-                total[k] = keep[quads // 2 + n] + got[quads // 2 + n] + odd[n]
-            total = total[0] + along(total[2], 2)
-        else:
-            for n, k in enumerate(order):
-                total[k] = keep[n] + got[n]
-            total = sum([along(total[k], k) for k in order[:-1]], total[0])
-        tile = (total * (flags[j] * feat ** (-0.5))).astype(jnp.bfloat16)
-        ahead.append(tile)
-        turned = tile.T.reshape(2, block // 2, block // 2)
-        straight = lax.dynamic_index_in_dim(turned, core, 0, keepdims=False)
-        crossed = lax.dynamic_index_in_dim(turned, 1 - core, 0, keepdims=False)
-        by = j + 1
-        straight = from_behind(straight, "blk", by)
-        crossed = lax.ppermute(
-            crossed,
-            ("blk", "dim"),
-            [(2 * i + c, 2 * ((i + by) % owners) + 1 - c) for i in range(owners) for c in range(2)],
-        )
-        behind.append(
-            jnp.where(
-                core == 0,
-                jnp.concatenate([straight, crossed], axis=1),
-                jnp.concatenate([crossed, straight], axis=1),
-            )
+        straight, crossed = behind[j]
+        behind[j] = jnp.where(
+            core == 0,
+            jnp.concatenate([straight, crossed], axis=1),
+            jnp.concatenate([crossed, straight], axis=1),
         )
     tiles = jnp.stack(ahead + behind).swapaxes(1, 2)
 
+    held = after([array for array, _ in notes], ahead[-1])
+    notes = [(array, row) for array, (_, row) in zip(held, notes)]
     note = jnp.stack([array[row : row + 5, :count] for array, row in notes]).astype(jnp.float32)
     targets = note[:, 0:1].astype(jnp.int32) + note[:, 1:2].astype(jnp.int32) * NOTE_BASE
     influences = jnp.log1p(note[:, 2:3] + note[:, 3:4] + note[:, 4:5])
@@ -483,7 +523,7 @@
         partial_bytes = 4 * owners * pair_flags.shape[1] * block * block // 2
         quads = owners // 2
         fits = partial_bytes <= PARTIAL_BYTES and quads == 4
-        plan = split_plan if fits and gradients.shape[0] % FIRST == 0 else ring_plan
+        plan = split_plan if fits and (gradients.shape[0] - FIRST) % STEP == 0 and FIRST % STEP == 0 else ring_plan
         return plan(gradients, owner_of, pair_flags, left_factor, right_factor)
 
     return jax.shard_map(

time: 262 us -> 235 us (0.90)
  the two profiles are of different devices: /device:TPU:0 before, /device:TPU:5 now
where the time goes in v4:
time: 235 us; the launch traced here: 234 us
  waiting for transfers between devices  106 us (45%)
  starting transfers between devices  65.9 us (28%)
  Pallas kernels  38.5 us (16%)
  other arithmetic  11.5 us (5%)
  local copies, waits for them, and re-layouts  8.6 us (4%)
  between operations  2.81 us (1%)
    ppermute x18, waiting for transfers between devices, along(): return lax.ppermute(x, 'blk', [(i, i ^ 2 * k) for i in range(owners)])  76.8 us
    ppermute x18, starting transfers between devices, along(): return lax.ppermute(x, 'blk', [(i, i ^ 2 * k) for i in range(owners)])  41.9 us
    pallas_call x3, Pallas kernels, partial_tiles(): pl.pallas_call(functools.partial(tiles_kernel, order, reach, (owners, slo...  20.6 us
    pallas_call x2, Pallas kernels, precondition(): pl.pallas_call(functools.partial(precondition_kernel, plan, notes), grid_...  16.6 us
    ppermute x9, waiting for transfers between devices, beside(): return lax.ppermute(x, 'blk', [(i, i ^ 1) for i in range(owners)])  14 us
    ppermute x6, waiting for transfers between devices, back(): return lax.ppermute(x, ('blk', 'dim'), pairs)  9.61 us
    ppermute x6, starting transfers between devices, back(): return lax.ppermute(x, ('blk', 'dim'), pairs)  9.12 us
    ppermute x5, starting transfers between devices, across(): return lax.ppermute(x, 'dim', [(0, 1), (1, 0)])  8.63 us
  transfers between devices with their start and end apart: 38, of which 19 were waited for; matrix products, arithmetic and copies ran while one was open for 5% of the time, Pallas kernels for 14%

profile of v4, /device:TPU:5, one launch (start us, length us, event | category | flops | bytes accessed | tf_op | source)
XLA Modules:
  0.0 233.7 jit_solution(6456969023429726932)
XLA Ops:
  6.5 3.8 %precondition.2 = (bf16[64,2048]{1,0:T(8,128)(2,1)S(1)}, bf16[64,2048]{1,0:T(8,128)(2,1)S(1)}, bf16[64,2048]{1,0:T(8,128)(2,1)S(1)}, bf16[64,2048]{1,0:T(8,128)(2,1)S(1)}, f32[64,128]{1,0:T(8,128)S(1)}) custom-call(s32[3]{0:T(128)S(1)} %pad_add_fusion.spot, bf16[64,64,128]{2,1,0:T(8,128)(2,1)S(1)} %slice.483.own, ...), custom_call_target="tpu_custom_call" | custom-call | flops 1048576 | bytes 65536 | tf_op jit(solution)/shard_map/precondition/pallas_call | solution.py:197
  16.4 12.8 %precondition.3 = (bf16[208,2048]{1,0:T(8,128)(2,1)S(1)}, bf16[208,768]{1,0:T(8,128)(2,1)S(1)}, bf16[192,768]{1,0:T(8,128)(2,1)S(1)}, bf16[192,512]{1,0:T(8,128)...) custom-call(s32[3]{0:T(128)S(1)} %pad_add_fusion.spot, ...), custom_call_target="tpu_custom_call" | custom-call | flops 1048576 | bytes 65536 | tf_op jit(solution)/shard_map/precondition/pallas_call | solution.py:197
  33.0 5.8 %collective-permute-start.6 = (bf16[208,768]{1,0:T(8,128)(2,1)S(1)}, bf16[208,768]{1,0:T(8,128)(2,1)S(1)}, u32[]{:S(2)}, u32[]{:S(2)}) collective-permute-start(bf16[208,768]{1,0:T(8,128)(2,1)S(1)} %get-tuple-element.680), channel_id=1, source_target_pairs={{0,4},{2,6},{4,0},{6,2},{8,12},{10,14},{12,8},{14,10},{1,5},{3,7},... | collective-permute-start | bytes 958472 | tf_op jit(solution)/shard_map/ppermute | solution.py:360
  40.9 8.9 %collective-permute-done.6.rest_1_.rest_11_ = bf16[208,768]{1,0:T(8,128)(2,1)S(1)} collective-permute-done((bf16[208,768]{1,0:T(8,128)(2,1)S(1)}, bf16[208,768]{1,0:T(8,128)(2,1)S(1)}, u32[]{:S(2)}, u32[]{:S(2)}) %collective-permute-start.6) | collective-permute-done | bytes 319520 | tf_op jit(solution)/shard_map/ppermute | solution.py:360
  50.6 9.8 %collective-permute-done.8.rest_3_.rest_15_ = bf16[208,768]{1,0:T(8,128)(2,1)S(1)} collective-permute-done((bf16[208,768]{1,0:T(8,128)(2,1)S(1)}, bf16[208,768]{1,0:T(8,128)(2,1)S(1)}, u32[]{:S(2)}, u32[]{:S(2)}) %collective-permute-start.8) | collective-permute-done | bytes 319520 | tf_op jit(solution)/shard_map/ppermute | solution.py:360
  61.4 6.5 %collective-permute-start.11 = (bf16[192,768]{1,0:T(8,128)(2,1)S(1)}, bf16[192,768]{1,0:T(8,128)(2,1)S(1)}, u32[]{:S(2)}, u32[]{:S(2)}) collective-permute-start(bf16[192,768]{1,0:T(8,128)(2,1)S(1)} %get-tuple-element.694), channel_id=1, source_target_pairs={{0,4},{2,6},{4,0},{6,2},{8,12},{10,14},{12,8},{14,10},{1,5},{3,7},... | collective-permute-start | bytes 884744 | tf_op jit(solution)/shard_map/ppermute | solution.py:360
  71.3 13.3 %collective-permute-done.15.rest_22_ = bf16[64,2048]{1,0:T(8,128)(2,1)S(1)} collective-permute-done((bf16[64,2048]{1,0:T(8,128)(2,1)S(1)}, bf16[64,2048]{1,0:T(8,128)(2,1)S(1)}, u32[]{:S(2)}, u32[]{:S(2)}) %collective-permute-start.15) | collective-permute-done | bytes 262176 | tf_op jit(solution)/shard_map/ppermute | solution.py:363
  87.7 7.7 %collective-permute-start.16 = (bf16[192,512]{1,0:T(8,128)(2,1)S(1)}, bf16[192,512]{1,0:T(8,128)(2,1)S(1)}, u32[]{:S(2)}, u32[]{:S(2)}) collective-permute-start(bf16[192,512]{1,0:T(8,128)(2,1)S(1)} %get-tuple-element.717), channel_id=1, source_target_pairs={{0,4},{2,6},{4,0},{6,2},{8,12},{10,14},{12,8},{14,10},{1,5},{3,7},... | collective-permute-start | bytes 589832 | tf_op jit(solution)/shard_map/ppermute | solution.py:360
  98.1 7.0 %partial_tiles.3 = (f32[4,192,384]{2,1,0:T(8,128)S(1)}, f32[4,192,384]{2,1,0:T(8,128)S(1)}, f32[4,192,384]{2,1,0:T(8,128)S(1)}, f32[4,192,384]{2,1,0:T(8,128)S(1...) custom-call(s32[3]{0:T(128)S(1)} %pad_add_fusion.spot, ...), custom_call_target="tpu_custom_call" | custom-call | flops 1048576 | bytes 65536 | tf_op jit(solution)/shard_map/partial_tiles/pallas_call | solution.py:293
  105.1 2.7 %collective-permute-done.18.rest_15_ = bf16[192,512]{1,0:T(8,128)(2,1)S(1)} collective-permute-done((bf16[192,512]{1,0:T(8,128)(2,1)S(1)}, bf16[192,512]{1,0:T(8,128)(2,1)S(1)}, u32[]{:S(2)}, u32[]{:S(2)}) %collective-permute-start.18) | collective-permute-done | bytes 196640 | tf_op jit(solution)/shard_map/ppermute | solution.py:360
  109.6 7.3 %partial_tiles.4 = (f32[4,192,384]{2,1,0:T(8,128)S(1)}, f32[4,192,384]{2,1,0:T(8,128)S(1)}, f32[4,192,384]{2,1,0:T(8,128)S(1)}, f32[4,192,384]{2,1,0:T(8,128)S(1...) custom-call(s32[3]{0:T(128)S(1)} %pad_add_fusion.spot, ...), custom_call_target="tpu_custom_call" | custom-call | flops 1048576 | bytes 65536 | tf_op jit(solution)/shard_map/partial_tiles/pallas_call | solution.py:293
  116.9 6.3 %partial_tiles.5 = (f32[4,192,384]{2,1,0:T(8,128)S(1)}, f32[4,192,384]{2,1,0:T(8,128)S(1)}, f32[4,192,384]{2,1,0:T(8,128)S(1)}, f32[4,192,384]{2,1,0:T(8,128)}, ...) custom-call(s32[3]{0:T(128)S(1)} %pad_add_fusion.spot, bf16[208,2048]{1,0:T(8,128)(2,1)S(1)} %get-tuple-element.801.rest_0_.rest_9_, ...), custom_call_target="tpu_custom_call" | custom-call | flops 1048576 | bytes 65536 | tf_op jit(solution)/shard_map/partial_tiles/pallas_call | solution.py:293
  125.3 7.0 %collective-permute-start.25 = (f32[4,192,384]{2,1,0:T(8,128)S(1)}, f32[4,192,384]{2,1,0:T(8,128)S(1)}, u32[]{:S(2)}, u32[]{:S(2)}) collective-permute-start(f32[4,192,384]{2,1,0:T(8,128)S(1)} %get-tuple-element.788), channel_id=1, source_target_pairs={{0,1},{1,0},{2,3},{3,2},{4,5},{5,4},{6,7},{7,6},{8,9},{9,8},{10,11... | collective-permute-start | bytes 3538952 | tf_op jit(solution)/shard_map/ppermute | solution.py:357
  132.8 3.6 %collective-permute-done.25 = f32[4,192,384]{2,1,0:T(8,128)S(1)} collective-permute-done((f32[4,192,384]{2,1,0:T(8,128)S(1)}, f32[4,192,384]{2,1,0:T(8,128)S(1)}, u32[]{:S(2)}, u32[]{:S(2)}) %collective-permute-start.25) | collective-permute-done | bytes 1179680 | tf_op jit(solution)/shard_map/ppermute | solution.py:357
  137.8 6.4 %collective-permute-start.26 = (f32[2,192,384]{2,1,0:T(8,128)}, f32[2,192,384]{2,1,0:T(8,128)}, u32[]{:S(2)}, u32[]{:S(2)}) collective-permute-start(f32[2,192,384]{2,1,0:T(8,128)} %slice_add_fusion.17), channel_id=1, source_target_pairs={{0,4},{2,6},{4,0},{6,2},{8,12},{10,14},{12,8},{14,10},{1,5},{3,7},... | collective-permute-start | bytes 1769480 | tf_op jit(solution)/shard_map/ppermute | solution.py:360
  148.0 9.8 %collective-permute-done.26 = f32[2,192,384]{2,1,0:T(8,128)} collective-permute-done((f32[2,192,384]{2,1,0:T(8,128)}, f32[2,192,384]{2,1,0:T(8,128)}, u32[]{:S(2)}, u32[]{:S(2)}) %collective-permute-start.26) | collective-permute-done | bytes 589856 | tf_op jit(solution)/shard_map/ppermute | solution.py:360
  159.2 3.1 %collective-permute-start.27 = (f32[192,384]{1,0:T(8,128)S(1)}, f32[192,384]{1,0:T(8,128)S(1)}, u32[]{:S(2)}, u32[]{:S(2)}) collective-permute-start(f32[192,384]{1,0:T(8,128)S(1)} %get-tuple-element.923), channel_id=1, source_target_pairs={{0,8},{2,10},{4,12},{6,14},{8,0},{10,2},{12,4},{14,6},{1,9},{3,11}... | collective-permute-start | bytes 884744 | tf_op jit(solution)/shard_map/ppermute | solution.py:360
  163.9 12.8 %collective-permute-done.32 = f32[2,192,384]{2,1,0:T(8,128)S(1)} collective-permute-done((f32[2,192,384]{2,1,0:T(8,128)S(1)}, f32[2,192,384]{2,1,0:T(8,128)S(1)}, u32[]{:S(2)}, u32[]{:S(2)}) %collective-permute-start.32) | collective-permute-done | bytes 589856 | tf_op jit(solution)/shard_map/ppermute | solution.py:360
  181.8 3.5 %collective-permute-start.29 = (bf16[192,192]{1,0:T(8,128)(2,1)S(1)}, bf16[192,192]{1,0:T(8,128)(2,1)S(1)}, u32[]{:S(2)}, u32[]{:S(2)}) collective-permute-start(bf16[192,192]{1,0:T(8,128)(2,1)S(1)} %get-tuple-element.791), channel_id=1, source_target_pairs={{0,7},{1,6},{2,9},{3,8},{4,11},{5,10},{6,13},{7,12},{8,15},{9,14},... | collective-permute-start | bytes 221192 | tf_op jit(solution)/shard_map/ppermute | solution.py:458
  185.9 13.8 %collective-permute-done.24 = f32[2,192,384]{2,1,0:T(8,128)S(1)} collective-permute-done((f32[2,192,384]{2,1,0:T(8,128)S(1)}, f32[2,192,384]{2,1,0:T(8,128)S(1)}, u32[]{:S(2)}, u32[]{:S(2)}) %collective-permute-start.24) | collective-permute-done | bytes 589856 | tf_op jit(solution)/shard_map/ppermute | solution.py:360
  200.5 2.6 %collective-permute-done.29 = bf16[192,192]{1,0:T(8,128)(2,1)S(1)} collective-permute-done((bf16[192,192]{1,0:T(8,128)(2,1)S(1)}, bf16[192,192]{1,0:T(8,128)(2,1)S(1)}, u32[]{:S(2)}, u32[]{:S(2)}) %collective-permute-start.29) | collective-permute-done | bytes 73760 | tf_op jit(solution)/shard_map/ppermute | solution.py:458
  204.9 14.3 %collective-permute-done.30.rest_1_ = f32[192,384]{1,0:T(8,128)S(1)} collective-permute-done((f32[192,384]{1,0:T(8,128)S(1)}, f32[192,384]{1,0:T(8,128)S(1)}, u32[]{:S(2)}, u32[]{:S(2)}) %collective-permute-start.30) | collective-permute-done | bytes 294944 | tf_op jit(solution)/shard_map/ppermute | solution.py:360
  223.1 3.0 %collective-permute-start.37 = (bf16[192,192]{1,0:T(8,128)(2,1)S(1)}, bf16[192,192]{1,0:T(8,128)(2,1)S(1)}, u32[]{:S(2)}, u32[]{:S(2)}) collective-permute-start(bf16[192,192]{1,0:T(8,128)(2,1)S(1)} %get-tuple-element.854), channel_id=1, source_target_pairs={{0,5},{1,4},{2,7},{3,6},{4,9},{5,8},{6,11},{7,10},{8,13},{9,12},{1... | collective-permute-start | bytes 221192 | tf_op jit(solution)/shard_map/ppermute | solution.py:458
  226.7 3.7 %collective-permute-done.36 = bf16[192,192]{1,0:T(8,128)(2,1)S(1)} collective-permute-done((bf16[192,192]{1,0:T(8,128)(2,1)S(1)}, bf16[192,192]{1,0:T(8,128)(2,1)S(1)}, u32[]{:S(2)}, u32[]{:S(2)}) %collective-permute-start.36) | collective-permute-done | bytes 73760 | tf_op jit(solution)/shard_map/ppermute | solution.py:458
  (140 shorter events, 56.0 us)
Async XLA Ops:
  10.3 18.9 %collective-permute-start.2 = (bf16[64,2048]{1,0:T(8,128)(2,1)S(1)}, bf16[64,2048]{1,0:T(8,128)(2,1)S(1)}, u32[]{:S(2)}, u32[]{:S(2)}) collective-permute-start(bf16[64,2048]{1,0:T(8,128)(2,1)S(1)} %get-tuple-element.675), channel_id=1, source_target_pairs={{0,4},{2,6},{4,0},{6,2},{8,12},{10,14},{12,8},{14,10},{1,5},{3,7},... | collective-permute-start | bytes 786440 | tf_op jit(solution)/shard_map/ppermute | solution.py:360
  11.6 17.5 %collective-permute-start.3 = (bf16[64,2048]{1,0:T(8,128)(2,1)S(1)}, bf16[64,2048]{1,0:T(8,128)(2,1)S(1)}, u32[]{:S(2)}, u32[]{:S(2)}) collective-permute-start(bf16[64,2048]{1,0:T(8,128)(2,1)S(1)} %get-tuple-element.676), channel_id=1, source_target_pairs={{0,8},{2,10},{4,12},{6,14},{8,0},{10,2},{12,4},{14,6},{1,9},{3,11}... | collective-permute-start | bytes 786440 | tf_op jit(solution)/shard_map/ppermute | solution.py:360
  13.9 17.5 %collective-permute-start.4 = (bf16[64,2048]{1,0:T(8,128)(2,1)S(1)}, bf16[64,2048]{1,0:T(8,128)(2,1)S(1)}, u32[]{:S(2)}, u32[]{:S(2)}) collective-permute-start(bf16[64,2048]{1,0:T(8,128)(2,1)S(1)} %get-tuple-element.677), channel_id=1, source_target_pairs={{0,12},{2,14},{4,8},{6,10},{8,4},{10,6},{12,0},{14,2},{1,13},{3,15... | collective-permute-start | bytes 786440 | tf_op jit(solution)/shard_map/ppermute | solution.py:360
  13.9 17.5 %collective-permute-start.5 = (bf16[64,2048]{1,0:T(8,128)(2,1)S(1)}, bf16[64,2048]{1,0:T(8,128)(2,1)S(1)}, u32[]{:S(2)}, u32[]{:S(2)}) collective-permute-start(bf16[64,2048]{1,0:T(8,128)(2,1)S(1)} %get-tuple-element.764.rest_8_), channel_id=1, source_target_pairs={{0,2},{2,0},{4,6},{6,4},{8,10},{10,8},{12,14},{14,12},{1,3},{3,1},... | collective-permute-start | bytes 786440 | tf_op jit(solution)/shard_map/ppermute | solution.py:363
  31.4 29.7 %collective-permute-start.10 = (bf16[208,2048]{1,0:T(8,128)(2,1)S(1)}, bf16[208,2048]{1,0:T(8,128)(2,1)S(1)}, u32[]{:S(2)}, u32[]{:S(2)}) collective-permute-start(bf16[208,2048]{1,0:T(8,128)(2,1)S(1)} %get-tuple-element.801.rest_0_.rest_9_), channel_id=1, source_target_pairs={{0,2},{2,0},{4,6},{6,4},{8,10},{10,8},{12,14},{14,12},{1,3},{3,1},... | collective-permute-start | bytes 2555912 | tf_op jit(solution)/shard_map/ppermute | solution.py:363
  31.7 29.4 %collective-permute-start.9 = (bf16[128,2048]{1,0:T(8,128)(2,1)S(1)}, bf16[128,2048]{1,0:T(8,128)(2,1)S(1)}, u32[]{:S(2)}, u32[]{:S(2)}) collective-permute-start(bf16[128,2048]{1,0:T(8,128)(2,1)S(1)} %pad_maximum_fusion.2), channel_id=1, source_target_pairs={{0,2},{2,0},{4,6},{6,4},{8,10},{10,8},{12,14},{14,12},{1,3},{3,1},... | collective-permute-start | bytes 1572872 | tf_op jit(solution)/shard_map/ppermute | solution.py:363
  33.0 16.8 %collective-permute-start.6 = (bf16[208,768]{1,0:T(8,128)(2,1)S(1)}, bf16[208,768]{1,0:T(8,128)(2,1)S(1)}, u32[]{:S(2)}, u32[]{:S(2)}) collective-permute-start(bf16[208,768]{1,0:T(8,128)(2,1)S(1)} %get-tuple-element.680), channel_id=1, source_target_pairs={{0,4},{2,6},{4,0},{6,2},{8,12},{10,14},{12,8},{14,10},{1,5},{3,7},... | collective-permute-start | bytes 958472 | tf_op jit(solution)/shard_map/ppermute | solution.py:360
  39.7 20.6 %collective-permute-start.8 = (bf16[208,768]{1,0:T(8,128)(2,1)S(1)}, bf16[208,768]{1,0:T(8,128)(2,1)S(1)}, u32[]{:S(2)}, u32[]{:S(2)}) collective-permute-start(bf16[208,768]{1,0:T(8,128)(2,1)S(1)} %get-tuple-element.682), channel_id=1, source_target_pairs={{0,12},{2,14},{4,8},{6,10},{8,4},{10,6},{12,0},{14,2},{1,13},{3,15... | collective-permute-start | bytes 958472 | tf_op jit(solution)/shard_map/ppermute | solution.py:360
  61.1 25.2 %collective-permute-start.14 = (bf16[624,768]{1,0:T(8,128)(2,1)S(1)}, bf16[624,768]{1,0:T(8,128)(2,1)S(1)}, u32[]{:S(2)}, u32[]{:S(2)}) collective-permute-start(bf16[624,768]{1,0:T(8,128)(2,1)S(1)} %pad_maximum_fusion), channel_id=1, source_target_pairs={{0,2},{2,0},{4,6},{6,4},{8,10},{10,8},{12,14},{14,12},{1,3},{3,1},... | collective-permute-start | bytes 2875400 | tf_op jit(solution)/shard_map/ppermute | solution.py:363
  61.4 23.2 %collective-permute-start.11 = (bf16[192,768]{1,0:T(8,128)(2,1)S(1)}, bf16[192,768]{1,0:T(8,128)(2,1)S(1)}, u32[]{:S(2)}, u32[]{:S(2)}) collective-permute-start(bf16[192,768]{1,0:T(8,128)(2,1)S(1)} %get-tuple-element.694), channel_id=1, source_target_pairs={{0,4},{2,6},{4,0},{6,2},{8,12},{10,14},{12,8},{14,10},{1,5},{3,7},... | collective-permute-start | bytes 884744 | tf_op jit(solution)/shard_map/ppermute | solution.py:360
  67.9 16.7 %collective-permute-start.12 = (bf16[192,768]{1,0:T(8,128)(2,1)S(1)}, bf16[192,768]{1,0:T(8,128)(2,1)S(1)}, u32[]{:S(2)}, u32[]{:S(2)}) collective-permute-start(bf16[192,768]{1,0:T(8,128)(2,1)S(1)} %get-tuple-element.695), channel_id=1, source_target_pairs={{0,8},{2,10},{4,12},{6,14},{8,0},{10,2},{12,4},{14,6},{1,9},{3,11}... | collective-permute-start | bytes 884744 | tf_op jit(solution)/shard_map/ppermute | solution.py:360
  68.9 17.4 %collective-permute-start.13 = (bf16[192,768]{1,0:T(8,128)(2,1)S(1)}, bf16[192,768]{1,0:T(8,128)(2,1)S(1)}, u32[]{:S(2)}, u32[]{:S(2)}) collective-permute-start(bf16[192,768]{1,0:T(8,128)(2,1)S(1)} %get-tuple-element.696), channel_id=1, source_target_pairs={{0,12},{2,14},{4,8},{6,10},{8,4},{10,6},{12,0},{14,2},{1,13},{3,15... | collective-permute-start | bytes 884744 | tf_op jit(solution)/shard_map/ppermute | solution.py:360
  70.1 14.5 %collective-permute-start.15 = (bf16[64,2048]{1,0:T(8,128)(2,1)S(1)}, bf16[64,2048]{1,0:T(8,128)(2,1)S(1)}, u32[]{:S(2)}, u32[]{:S(2)}) collective-permute-start(bf16[64,2048]{1,0:T(8,128)(2,1)S(1)} %collective-permute-done.4.rest_14_), channel_id=1, source_target_pairs={{0,2},{2,0},{4,6},{6,4},{8,10},{10,8},{12,14},{14,12},{1,3},{3,1},... | collective-permute-start | bytes 786440 | tf_op jit(solution)/shard_map/ppermute | solution.py:363
  86.4 21.5 %collective-permute-start.19 = (bf16[576,768]{1,0:T(8,128)(2,1)S(1)}, bf16[576,768]{1,0:T(8,128)(2,1)S(1)}, u32[]{:S(2)}, u32[]{:S(2)}) collective-permute-start(bf16[576,768]{1,0:T(8,128)(2,1)S(1)} %pad_maximum_fusion.1), channel_id=1, source_target_pairs={{0,2},{2,0},{4,6},{6,4},{8,10},{10,8},{12,14},{14,12},{1,3},{3,1},... | collective-permute-start | bytes 2654216 | tf_op jit(solution)/shard_map/ppermute | solution.py:363
  87.7 17.4 %collective-permute-start.16 = (bf16[192,512]{1,0:T(8,128)(2,1)S(1)}, bf16[192,512]{1,0:T(8,128)(2,1)S(1)}, u32[]{:S(2)}, u32[]{:S(2)}) collective-permute-start(bf16[192,512]{1,0:T(8,128)(2,1)S(1)} %get-tuple-element.717), channel_id=1, source_target_pairs={{0,4},{2,6},{4,0},{6,2},{8,12},{10,14},{12,8},{14,10},{1,5},{3,7},... | collective-permute-start | bytes 589832 | tf_op jit(solution)/shard_map/ppermute | solution.py:360
  132.3 30.0 %collective-permute-start.23 = (f32[4,192,384]{2,1,0:T(8,128)}, f32[4,192,384]{2,1,0:T(8,128)}, u32[]{:S(2)}, u32[]{:S(2)}) collective-permute-start(f32[4,192,384]{2,1,0:T(8,128)} %get-tuple-element.786), channel_id=1, source_target_pairs={{0,1},{1,0},{2,3},{3,2},{4,5},{5,4},{6,7},{7,6},{8,9},{9,8},{10,11... | collective-permute-start | bytes 3538952 | tf_op jit(solution)/shard_map/ppermute | solution.py:357
  137.8 20.1 %collective-permute-start.26 = (f32[2,192,384]{2,1,0:T(8,128)}, f32[2,192,384]{2,1,0:T(8,128)}, u32[]{:S(2)}, u32[]{:S(2)}) collective-permute-start(f32[2,192,384]{2,1,0:T(8,128)} %slice_add_fusion.17), channel_id=1, source_target_pairs={{0,4},{2,6},{4,0},{6,2},{8,12},{10,14},{12,8},{14,10},{1,5},{3,7},... | collective-permute-start | bytes 1769480 | tf_op jit(solution)/shard_map/ppermute | solution.py:360
  145.6 31.1 %collective-permute-start.32 = (f32[2,192,384]{2,1,0:T(8,128)S(1)}, f32[2,192,384]{2,1,0:T(8,128)S(1)}, u32[]{:S(2)}, u32[]{:S(2)}) collective-permute-start(f32[2,192,384]{2,1,0:T(8,128)S(1)} %slice_add_fusion.16), channel_id=1, source_target_pairs={{0,4},{2,6},{4,0},{6,2},{8,12},{10,14},{12,8},{14,10},{1,5},{3,7},... | collective-permute-start | bytes 1769480 | tf_op jit(solution)/shard_map/ppermute | solution.py:360
  159.2 20.7 %collective-permute-start.27 = (f32[192,384]{1,0:T(8,128)S(1)}, f32[192,384]{1,0:T(8,128)S(1)}, u32[]{:S(2)}, u32[]{:S(2)}) collective-permute-start(f32[192,384]{1,0:T(8,128)S(1)} %get-tuple-element.923), channel_id=1, source_target_pairs={{0,8},{2,10},{4,12},{6,14},{8,0},{10,2},{12,4},{14,6},{1,9},{3,11}... | collective-permute-start | bytes 884744 | tf_op jit(solution)/shard_map/ppermute | solution.py:360
  163.5 36.3 %collective-permute-start.24 = (f32[2,192,384]{2,1,0:T(8,128)S(1)}, f32[2,192,384]{2,1,0:T(8,128)S(1)}, u32[]{:S(2)}, u32[]{:S(2)}) collective-permute-start(f32[2,192,384]{2,1,0:T(8,128)S(1)} %slice_add_fusion.18), channel_id=1, source_target_pairs={{0,4},{2,6},{4,0},{6,2},{8,12},{10,14},{12,8},{14,10},{1,5},{3,7},... | collective-permute-start | bytes 1769480 | tf_op jit(solution)/shard_map/ppermute | solution.py:360
  178.7 42.0 %collective-permute-start.33 = (f32[192,384]{1,0:T(8,128)}, f32[192,384]{1,0:T(8,128)}, u32[]{:S(2)}, u32[]{:S(2)}) collective-permute-start(f32[192,384]{1,0:T(8,128)} %get-tuple-element.919), channel_id=1, source_target_pairs={{0,8},{2,10},{4,12},{6,14},{8,0},{10,2},{12,4},{14,6},{1,9},{3,11}... | collective-permute-start | bytes 884744 | tf_op jit(solution)/shard_map/ppermute | solution.py:360
  180.6 19.9 %collective-permute-start.28 = (bf16[192,192]{1,0:T(8,128)(2,1)S(1)}, bf16[192,192]{1,0:T(8,128)(2,1)S(1)}, u32[]{:S(2)}, u32[]{:S(2)}) collective-permute-start(bf16[192,192]{1,0:T(8,128)(2,1)S(1)} %get-tuple-element.790), channel_id=1, source_target_pairs={{0,6},{1,7},{2,8},{3,9},{4,10},{5,11},{6,12},{7,13},{8,14},{9,15},... | collective-permute-start | bytes 221192 | tf_op jit(solution)/shard_map/ppermute | solution.py:458
  181.8 21.3 %collective-permute-start.29 = (bf16[192,192]{1,0:T(8,128)(2,1)S(1)}, bf16[192,192]{1,0:T(8,128)(2,1)S(1)}, u32[]{:S(2)}, u32[]{:S(2)}) collective-permute-start(bf16[192,192]{1,0:T(8,128)(2,1)S(1)} %get-tuple-element.791), channel_id=1, source_target_pairs={{0,7},{1,6},{2,9},{3,8},{4,11},{5,10},{6,13},{7,12},{8,15},{9,14},... | collective-permute-start | bytes 221192 | tf_op jit(solution)/shard_map/ppermute | solution.py:458
  204.3 14.9 %collective-permute-start.30 = (f32[192,384]{1,0:T(8,128)S(1)}, f32[192,384]{1,0:T(8,128)S(1)}, u32[]{:S(2)}, u32[]{:S(2)}) collective-permute-start(f32[192,384]{1,0:T(8,128)S(1)} %get-tuple-element.921), channel_id=1, source_target_pairs={{0,8},{2,10},{4,12},{6,14},{8,0},{10,2},{12,4},{14,6},{1,9},{3,11}... | collective-permute-start | bytes 884744 | tf_op jit(solution)/shard_map/ppermute | solution.py:360
  (30 other events, 316.5 us)

commit v5 on v4

--- a/solution.py
+++ b/solution.py
@@ -12,6 +12,7 @@
 SLICES = (3, 3, 2)
 NOTE = 16
 NOTE_BASE = 256
+PARTS = ((2,), (0,), (1,))
 GROUP = 8
 STEP = 32
 VMEM_BYTES = 30 * 2**20
@@ -219,8 +220,8 @@
     quads = owners // 2
     block = owners * slots
     notes, inputs = rest[:owners], rest[owners : 3 * owners]
-    bases = rest[3 * owners : 3 * owners + 2 * reach] if based else ()
-    outs, cluster = rest[-2 * reach - 1 : -1], rest[-1]
+    bases = rest[3 * owners : 3 * owners + 2 * len(PARTS)] if based else ()
+    outs, cluster = rest[-2 * len(PARTS) - 1 : -1], rest[-1]
     here, side, core = spot[0], spot[1], spot[2]
     count = early_rows + late_rows
     depth = cluster.shape[3]
@@ -260,9 +261,13 @@
             (((1,), (1,)), ((), ())),
             preferred_element_type=jnp.float32,
         )
-        for i in range(2 * reach):
-            part = product[i * rows : (i + 1) * rows]
-            outs[i][0] = part + bases[i][0] if based else part
+        for h in range(2):
+            for n, part in enumerate(PARTS):
+                out = h * len(PARTS) + n
+                for at, j in enumerate(part):
+                    first = (h * reach + j) * rows
+                    value = product[first : first + rows]
+                    outs[out][0, at] = value + bases[out][0, at] if based else value
 
 
 def partial_tiles(spot, notes, pieces, width, order, reach, slots, bases=()):
@@ -286,10 +291,11 @@
                 )
             )
             operands.append(array)
-    shape = (len(order), block // 2, block)
+    shapes = [(len(order), len(part), block // 2, block) for part in PARTS] * 2
     tile_specs = [
-        pl.BlockSpec((1,) + shape[1:], lambda i, s: (jnp.maximum(i - 1, 0), 0, 0))
-    ] * (2 * reach)
+        pl.BlockSpec((1,) + shape[1:], lambda i, s: (jnp.maximum(i - 1, 0), 0, 0, 0))
+        for shape in shapes
+    ]
     return pl.pallas_call(
         functools.partial(
             tiles_kernel, order, reach, (owners, slots, early_rows, late_rows), bool(bases)
@@ -301,7 +307,7 @@
             out_specs=tile_specs,
             scratch_shapes=[pltpu.VMEM((owners, owners, slots, width), jnp.bfloat16)],
         ),
-        out_shape=[jax.ShapeDtypeStruct(shape, jnp.float32)] * (2 * reach),
+        out_shape=[jax.ShapeDtypeStruct(shape, jnp.float32) for shape in shapes],
         compiler_params=pltpu.CompilerParams(vmem_limit_bytes=VMEM_BYTES),
         cost_estimate=SMALL_COST,
         name="partial_tiles",
@@ -310,7 +316,7 @@
 
 def finish_kernel(spot, flags, *rest):
     *terms, tile, straight, crossed = rest
-    total = sum([term[...] for term in terms[1:]], terms[0][...])
+    total = terms[0][0] + terms[1][0]
     done = (total * flags[0]).astype(tile.dtype)
     tile[...] = done
     turned = done.astype(jnp.float32).T.astype(tile.dtype)
@@ -321,8 +327,8 @@
     crossed[...] = jnp.where(core == 0, second, first)
 
 
-def finish(spot, factor, terms):
-    rows, block = terms[0].shape
+def finish(spot, factor, terms, at):
+    _, rows, block = terms[0].shape
     spec = lambda shape: pl.BlockSpec(shape, lambda i, s, f: (0, 0))
     out = [(rows, block), (rows, rows), (rows, rows)]
     return pl.pallas_call(
@@ -330,7 +336,7 @@
         grid_spec=pltpu.PrefetchScalarGridSpec(
             num_scalar_prefetch=2,
             grid=(1,),
-            in_specs=[spec(term.shape) for term in terms],
+            in_specs=[pl.BlockSpec((1, rows, block), lambda i, s, f: (at, 0, 0))] * 2,
             out_specs=[spec(shape) for shape in out],
         ),
         out_shape=[jax.ShapeDtypeStruct(shape, jnp.bfloat16) for shape in out],
@@ -448,7 +454,6 @@
 
     flags = lax.dynamic_index_in_dim(pair_flags, index, 0, keepdims=False).astype(jnp.float32)
     ahead, behind = [None] * reach, [None] * reach
-    gathered = [across(sums[reach + j]) for j in reversed(range(reach))][::-1]
     def back(x, by, turn):
         pairs = [
             (2 * i + c, 2 * ((i + by) % owners) + (1 - c if turn else c))
@@ -457,31 +462,33 @@
         ]
         return lax.ppermute(x, ("blk", "dim"), pairs)
 
-    spans = list(reversed(range(reach)))
-    odds, evens, nears, fars = {}, {}, {}, {}
-    for j in spans:
-        keep, got = sums[j], gathered[j]
-        odds[j] = along(keep[: quads // 2] + got[: quads // 2], 1)
-        evens[j] = [keep[2] + got[2], keep[3] + got[3]]
-
-    def halve(j):
-        nears[j] = evens[j][1] + odds[j][1]
-        fars[j] = along(evens[j][0] + odds[j][0], 2)
-
-    def complete(j):
-        factor = (flags[j] * feat ** (-0.5)).reshape(1)
-        ahead[j], straight, crossed = finish(spot, factor, [nears[j], fars[j]])
-        straight, crossed = back(straight, j + 1, False), back(crossed, j + 1, True)
-        behind[j] = [straight, crossed]
-
-    for n, j in enumerate(spans):
-        if n > 1:
-            complete(spans[n - 2])
-            (odds[j],) = after([odds[j]], ahead[spans[n - 2]], *behind[spans[n - 2]])
-        halve(j)
-    for n in range(max(0, reach - 2), reach):
-        j = spans[n]
-        complete(j)
+    keeps, gives = sums[: len(PARTS)], sums[len(PARTS) :]
+    gots = [across(give) for give in gives]
+    odds = [keep[:2] + got[:2] for keep, got in zip(keeps, gots)]
+    odds = [along(odd, 1) for odd in odds] + [odds[-1]]
+    evens = [[keep[2] + got[2], keep[3] + got[3]] for keep, got in zip(keeps, gots)]
+    (odds[0],) = after([odds[0]], odds.pop())
+    nears, fars = {}, {}
+
+    def halve(n):
+        nears[n] = evens[n][1] + odds[n][1]
+        fars[n] = along(evens[n][0] + odds[n][0], 2)
+
+    def complete(n):
+        for at, j in enumerate(PARTS[n]):
+            factor = (flags[j] * feat ** (-0.5)).reshape(1)
+            ahead[j], straight, crossed = finish(spot, factor, [nears[n], fars[n]], at)
+            behind[j] = [back(straight, j + 1, False), back(crossed, j + 1, True)]
+
+    last = len(PARTS) - 1
+    for n in range(last):
+        halve(n)
+    complete(0)
+    waits = [behind[j][0] for j in PARTS[0]]
+    (odds[last],) = after([odds[last]], *waits)
+    halve(last)
+    for n in range(1, last + 1):
+        complete(n)
     for j in range(reach):
         straight, crossed = behind[j]
         behind[j] = jnp.where(

time: 235 us -> 233 us (level)
    unnamed x41 -> x45, local copies, waits for them, and re-layouts: 6.27 us -> 6.94 us
  transfers between devices with their start and end apart: 38 -> 38, of which waited for: 19 -> 17; matrix products, arithmetic and copies ran while one was open for 5% -> 6% of each run, Pallas kernels for 14% -> 14%
where the time goes in v5:
time: 233 us
  waiting for transfers between devices  104 us (45%)
  starting transfers between devices  63.8 us (27%)
  Pallas kernels  39.6 us (17%)
  other arithmetic  12.6 us (5%)
  local copies, waits for them, and re-layouts  9.32 us (4%)
  between operations  2.76 us (1%)
    ppermute x18, waiting for transfers between devices, along(): return lax.ppermute(x, 'blk', [(i, i ^ 2 * k) for i in range(owners)])  75 us
    ppermute x18, starting transfers between devices, along(): return lax.ppermute(x, 'blk', [(i, i ^ 2 * k) for i in range(owners)])  42.1 us
    pallas_call x3, Pallas kernels, partial_tiles(): pl.pallas_call(functools.partial(tiles_kernel, order, reach, (owners, slo...  20.7 us
    pallas_call x2, Pallas kernels, precondition(): pl.pallas_call(functools.partial(precondition_kernel, plan, notes), grid_...  16.6 us
    ppermute x9, waiting for transfers between devices, beside(): return lax.ppermute(x, 'blk', [(i, i ^ 1) for i in range(owners)])  14 us
    ppermute x6, waiting for transfers between devices, back(): return lax.ppermute(x, ('blk', 'dim'), pairs)  10.7 us
    ppermute x5, starting transfers between devices, across(): return lax.ppermute(x, 'dim', [(0, 1), (1, 0)])  8.64 us
    unnamed x45, local copies, waits for them, and re-layouts  6.94 us
  transfers between devices with their start and end apart: 38, of which 17 were waited for; matrix products, arithmetic and copies ran while one was open for 6% of the time, Pallas kernels for 14%

profile of v5, /device:TPU:5, one launch (start us, length us, event | category | flops | bytes accessed | tf_op | source)
XLA Modules:
  0.0 232.5 jit_solution(548931448088153195)
XLA Ops:
  6.5 3.8 %precondition.2 = (bf16[64,2048]{1,0:T(8,128)(2,1)S(1)}, bf16[64,2048]{1,0:T(8,128)(2,1)S(1)}, bf16[64,2048]{1,0:T(8,128)(2,1)S(1)}, bf16[64,2048]{1,0:T(8,128)(2,1)S(1)}, f32[64,128]{1,0:T(8,128)S(1)}) custom-call(s32[3]{0:T(128)S(1)} %pad_add_fusion.spot, bf16[64,64,128]{2,1,0:T(8,128)(2,1)S(1)} %slice.483.own, ...), custom_call_target="tpu_custom_call" | custom-call | flops 1048576 | bytes 65536 | tf_op jit(solution)/shard_map/precondition/pallas_call | solution.py:198
  11.6 2.3 collective-permute-start.3
  16.4 12.8 %precondition.3 = (bf16[208,2048]{1,0:T(8,128)(2,1)S(1)}, bf16[208,768]{1,0:T(8,128)(2,1)S(1)}, bf16[192,768]{1,0:T(8,128)(2,1)S(1)}, bf16[192,512]{1,0:T(8,128)...) custom-call(s32[3]{0:T(128)S(1)} %pad_add_fusion.spot, ...), custom_call_target="tpu_custom_call" | custom-call | flops 1048576 | bytes 65536 | tf_op jit(solution)/shard_map/precondition/pallas_call | solution.py:198
  33.0 5.8 %collective-permute-start.6 = (bf16[208,768]{1,0:T(8,128)(2,1)S(1)}, bf16[208,768]{1,0:T(8,128)(2,1)S(1)}, u32[]{:S(2)}, u32[]{:S(2)}) collective-permute-start(bf16[208,768]{1,0:T(8,128)(2,1)S(1)} %get-tuple-element.681), channel_id=1, source_target_pairs={{0,4},{2,6},{4,0},{6,2},{8,12},{10,14},{12,8},{14,10},{1,5},{3,7},... | collective-permute-start | bytes 958472 | tf_op jit(solution)/shard_map/ppermute | solution.py:366
  40.9 8.9 %collective-permute-done.6.rest_1_.rest_11_ = bf16[208,768]{1,0:T(8,128)(2,1)S(1)} collective-permute-done((bf16[208,768]{1,0:T(8,128)(2,1)S(1)}, bf16[208,768]{1,0:T(8,128)(2,1)S(1)}, u32[]{:S(2)}, u32[]{:S(2)}) %collective-permute-start.6) | collective-permute-done | bytes 319520 | tf_op jit(solution)/shard_map/ppermute | solution.py:366
  50.6 9.8 %collective-permute-done.8.rest_3_.rest_15_ = bf16[208,768]{1,0:T(8,128)(2,1)S(1)} collective-permute-done((bf16[208,768]{1,0:T(8,128)(2,1)S(1)}, bf16[208,768]{1,0:T(8,128)(2,1)S(1)}, u32[]{:S(2)}, u32[]{:S(2)}) %collective-permute-start.8) | collective-permute-done | bytes 319520 | tf_op jit(solution)/shard_map/ppermute | solution.py:366
  61.4 6.5 %collective-permute-start.11 = (bf16[192,768]{1,0:T(8,128)(2,1)S(1)}, bf16[192,768]{1,0:T(8,128)(2,1)S(1)}, u32[]{:S(2)}, u32[]{:S(2)}) collective-permute-start(bf16[192,768]{1,0:T(8,128)(2,1)S(1)} %get-tuple-element.695), channel_id=1, source_target_pairs={{0,4},{2,6},{4,0},{6,2},{8,12},{10,14},{12,8},{14,10},{1,5},{3,7},... | collective-permute-start | bytes 884744 | tf_op jit(solution)/shard_map/ppermute | solution.py:366
  71.3 13.3 %collective-permute-done.15.rest_22_ = bf16[64,2048]{1,0:T(8,128)(2,1)S(1)} collective-permute-done((bf16[64,2048]{1,0:T(8,128)(2,1)S(1)}, bf16[64,2048]{1,0:T(8,128)(2,1)S(1)}, u32[]{:S(2)}, u32[]{:S(2)}) %collective-permute-start.15) | collective-permute-done | bytes 262176 | tf_op jit(solution)/shard_map/ppermute | solution.py:369
  87.7 7.7 %collective-permute-start.16 = (bf16[192,512]{1,0:T(8,128)(2,1)S(1)}, bf16[192,512]{1,0:T(8,128)(2,1)S(1)}, u32[]{:S(2)}, u32[]{:S(2)}) collective-permute-start(bf16[192,512]{1,0:T(8,128)(2,1)S(1)} %get-tuple-element.718), channel_id=1, source_target_pairs={{0,4},{2,6},{4,0},{6,2},{8,12},{10,14},{12,8},{14,10},{1,5},{3,7},... | collective-permute-start | bytes 589832 | tf_op jit(solution)/shard_map/ppermute | solution.py:366
  98.1 7.0 %partial_tiles.3 = (f32[4,1,192,384]{3,2,1,0:T(8,128)S(1)}, f32[4,1,192,384]{3,2,1,0:T(8,128)S(1)}, f32[4,1,192,384]{3,2,1,0:T(8,128)S(1)}, f32[4,1,192,384]{3,2...) custom-call(s32[3]{0:T(128)S(1)} %pad_add_fusion.spot, ...), custom_call_target="tpu_custom_call" | custom-call | flops 1048576 | bytes 65536 | tf_op jit(solution)/shard_map/partial_tiles/pallas_call | solution.py:299
  105.1 2.7 %collective-permute-done.18.rest_15_ = bf16[192,512]{1,0:T(8,128)(2,1)S(1)} collective-permute-done((bf16[192,512]{1,0:T(8,128)(2,1)S(1)}, bf16[192,512]{1,0:T(8,128)(2,1)S(1)}, u32[]{:S(2)}, u32[]{:S(2)}) %collective-permute-start.18) | collective-permute-done | bytes 196640 | tf_op jit(solution)/shard_map/ppermute | solution.py:366
  109.6 7.3 %partial_tiles.4 = (f32[4,1,192,384]{3,2,1,0:T(8,128)S(1)}, f32[4,1,192,384]{3,2,1,0:T(8,128)S(1)}, f32[4,1,192,384]{3,2,1,0:T(8,128)S(1)}, f32[4,1,192,384]{3,2...) custom-call(s32[3]{0:T(128)S(1)} %pad_add_fusion.spot, ...), custom_call_target="tpu_custom_call" | custom-call | flops 1048576 | bytes 65536 | tf_op jit(solution)/shard_map/partial_tiles/pallas_call | solution.py:299
  116.9 6.4 %partial_tiles.5 = (f32[4,1,192,384]{3,2,1,0:T(8,128)S(1)}, f32[4,1,192,384]{3,2,1,0:T(8,128)S(1)}, f32[4,1,192,384]{3,2,1,0:T(8,128)S(1)}, f32[4,1,192,384]{3,2...) custom-call(s32[3]{0:T(128)S(1)} %pad_add_fusion.spot, ...), custom_call_target="tpu_custom_call" | custom-call | flops 1048576 | bytes 65536 | tf_op jit(solution)/shard_map/partial_tiles/pallas_call | solution.py:299
  126.4 7.0 %collective-permute-start.28 = (f32[4,1,192,384]{3,2,1,0:T(8,128)}, f32[4,1,192,384]{3,2,1,0:T(8,128)}, u32[]{:S(2)}, u32[]{:S(2)}) collective-permute-start(f32[4,1,192,384]{3,2,1,0:T(8,128)} %get-tuple-element.792), channel_id=1, source_target_pairs={{0,1},{1,0},{2,3},{3,2},{4,5},{5,4},{6,7},{7,6},{8,9},{9,8},{10,11... | collective-permute-start | bytes 3538952 | tf_op jit(solution)/shard_map/ppermute | solution.py:363
  133.9 2.3 collective-permute-done.28
  137.5 6.4 %collective-permute-start.29 = (f32[2,1,192,384]{3,2,1,0:T(8,128)S(1)}, f32[2,1,192,384]{3,2,1,0:T(8,128)S(1)}, u32[]{:S(2)}, u32[]{:S(2)}) collective-permute-start(f32[2,1,192,384]{3,2,1,0:T(8,128)S(1)} %slice_add_fusion.16), channel_id=1, source_target_pairs={{0,4},{2,6},{4,0},{6,2},{8,12},{10,14},{12,8},{14,10},{1,5},{3,7},... | collective-permute-start | bytes 1769480 | tf_op jit(solution)/shard_map/ppermute | solution.py:366
  148.4 9.0 %collective-permute-done.29 = f32[2,1,192,384]{3,2,1,0:T(8,128)S(1)} collective-permute-done((f32[2,1,192,384]{3,2,1,0:T(8,128)S(1)}, f32[2,1,192,384]{3,2,1,0:T(8,128)S(1)}, u32[]{:S(2)}, u32[]{:S(2)}) %collective-permute-start.29) | collective-permute-done | bytes 589856 | tf_op jit(solution)/shard_map/ppermute | solution.py:366
  159.4 3.1 %collective-permute-start.30 = (f32[1,192,384]{2,1,0:T(8,128)}, f32[1,192,384]{2,1,0:T(8,128)}, u32[]{:S(2)}, u32[]{:S(2)}) collective-permute-start(f32[1,192,384]{2,1,0:T(8,128)} %get-tuple-element.923), channel_id=1, source_target_pairs={{0,8},{2,10},{4,12},{6,14},{8,0},{10,2},{12,4},{14,6},{1,9},{3,11}... | collective-permute-start | bytes 884744 | tf_op jit(solution)/shard_map/ppermute | solution.py:366
  165.2 11.2 %collective-permute-done.24 = f32[2,1,192,384]{3,2,1,0:T(8,128)} collective-permute-done((f32[2,1,192,384]{3,2,1,0:T(8,128)}, f32[2,1,192,384]{3,2,1,0:T(8,128)}, u32[]{:S(2)}, u32[]{:S(2)}) %collective-permute-start.24) | collective-permute-done | bytes 589856 | tf_op jit(solution)/shard_map/ppermute | solution.py:366
  182.8 14.6 %collective-permute-done.27 = f32[2,1,192,384]{3,2,1,0:T(8,128)S(1)} collective-permute-done((f32[2,1,192,384]{3,2,1,0:T(8,128)}, f32[2,1,192,384]{3,2,1,0:T(8,128)S(1)}, u32[]{:S(2)}, u32[]{:S(2)}) %collective-permute-start.27) | collective-permute-done | bytes 589856 | tf_op jit(solution)/shard_map/ppermute | solution.py:366
  197.4 2.8 %collective-permute-done.31 = bf16[192,192]{1,0:T(8,128)(2,1)S(1)} collective-permute-done((bf16[192,192]{1,0:T(8,128)(2,1)S(1)}, bf16[192,192]{1,0:T(8,128)(2,1)S(1)}, u32[]{:S(2)}, u32[]{:S(2)}) %collective-permute-start.31) | collective-permute-done | bytes 73760 | tf_op jit(solution)/shard_map/ppermute | solution.py:463
  207.9 14.2 %collective-permute-done.32 = f32[1,192,384]{2,1,0:T(8,128)S(1)} collective-permute-done((f32[1,192,384]{2,1,0:T(8,128)S(1)}, f32[1,192,384]{2,1,0:T(8,128)S(1)}, u32[]{:S(2)}, u32[]{:S(2)}) %collective-permute-start.32) | collective-permute-done | bytes 294944 | tf_op jit(solution)/shard_map/ppermute | solution.py:366
  223.3 4.8 %collective-permute-done.35 = bf16[192,192]{1,0:T(8,128)(2,1)S(1)} collective-permute-done((bf16[192,192]{1,0:T(8,128)(2,1)S(1)}, bf16[192,192]{1,0:T(8,128)(2,1)S(1)}, u32[]{:S(2)}, u32[]{:S(2)}) %collective-permute-start.35) | collective-permute-done | bytes 73760 | tf_op jit(solution)/shard_map/ppermute | solution.py:463
  228.1 3.2 %collective-permute-done.36 = bf16[192,192]{1,0:T(8,128)(2,1)S(1)} collective-permute-done((bf16[192,192]{1,0:T(8,128)(2,1)S(1)}, bf16[192,192]{1,0:T(8,128)(2,1)S(1)}, u32[]{:S(2)}, u32[]{:S(2)}) %collective-permute-start.36) | collective-permute-done | bytes 73760 | tf_op jit(solution)/shard_map/ppermute | solution.py:463
  (144 shorter events, 57.5 us)
Async XLA Ops:
  10.3 18.9 %collective-permute-start.2 = (bf16[64,2048]{1,0:T(8,128)(2,1)S(1)}, bf16[64,2048]{1,0:T(8,128)(2,1)S(1)}, u32[]{:S(2)}, u32[]{:S(2)}) collective-permute-start(bf16[64,2048]{1,0:T(8,128)(2,1)S(1)} %get-tuple-element.676), channel_id=1, source_target_pairs={{0,4},{2,6},{4,0},{6,2},{8,12},{10,14},{12,8},{14,10},{1,5},{3,7},... | collective-permute-start | bytes 786440 | tf_op jit(solution)/shard_map/ppermute | solution.py:366
  11.6 17.6 %collective-permute-start.3 = (bf16[64,2048]{1,0:T(8,128)(2,1)S(1)}, bf16[64,2048]{1,0:T(8,128)(2,1)S(1)}, u32[]{:S(2)}, u32[]{:S(2)}) collective-permute-start(bf16[64,2048]{1,0:T(8,128)(2,1)S(1)} %get-tuple-element.677), channel_id=1, source_target_pairs={{0,8},{2,10},{4,12},{6,14},{8,0},{10,2},{12,4},{14,6},{1,9},{3,11}... | collective-permute-start | bytes 786440 | tf_op jit(solution)/shard_map/ppermute | solution.py:366
  13.9 17.5 %collective-permute-start.4 = (bf16[64,2048]{1,0:T(8,128)(2,1)S(1)}, bf16[64,2048]{1,0:T(8,128)(2,1)S(1)}, u32[]{:S(2)}, u32[]{:S(2)}) collective-permute-start(bf16[64,2048]{1,0:T(8,128)(2,1)S(1)} %get-tuple-element.678), channel_id=1, source_target_pairs={{0,12},{2,14},{4,8},{6,10},{8,4},{10,6},{12,0},{14,2},{1,13},{3,15... | collective-permute-start | bytes 786440 | tf_op jit(solution)/shard_map/ppermute | solution.py:366
  13.9 17.5 %collective-permute-start.5 = (bf16[64,2048]{1,0:T(8,128)(2,1)S(1)}, bf16[64,2048]{1,0:T(8,128)(2,1)S(1)}, u32[]{:S(2)}, u32[]{:S(2)}) collective-permute-start(bf16[64,2048]{1,0:T(8,128)(2,1)S(1)} %get-tuple-element.765.rest_8_), channel_id=1, source_target_pairs={{0,2},{2,0},{4,6},{6,4},{8,10},{10,8},{12,14},{14,12},{1,3},{3,1},... | collective-permute-start | bytes 786440 | tf_op jit(solution)/shard_map/ppermute | solution.py:369
  31.4 29.7 %collective-permute-start.10 = (bf16[208,2048]{1,0:T(8,128)(2,1)S(1)}, bf16[208,2048]{1,0:T(8,128)(2,1)S(1)}, u32[]{:S(2)}, u32[]{:S(2)}) collective-permute-start(bf16[208,2048]{1,0:T(8,128)(2,1)S(1)} %get-tuple-element.803.rest_0_.rest_9_), channel_id=1, source_target_pairs={{0,2},{2,0},{4,6},{6,4},{8,10},{10,8},{12,14},{14,12},{1,3},{3,1},... | collective-permute-start | bytes 2555912 | tf_op jit(solution)/shard_map/ppermute | solution.py:369
  31.7 29.4 %collective-permute-start.9 = (bf16[128,2048]{1,0:T(8,128)(2,1)S(1)}, bf16[128,2048]{1,0:T(8,128)(2,1)S(1)}, u32[]{:S(2)}, u32[]{:S(2)}) collective-permute-start(bf16[128,2048]{1,0:T(8,128)(2,1)S(1)} %pad_maximum_fusion.2), channel_id=1, source_target_pairs={{0,2},{2,0},{4,6},{6,4},{8,10},{10,8},{12,14},{14,12},{1,3},{3,1},... | collective-permute-start | bytes 1572872 | tf_op jit(solution)/shard_map/ppermute | solution.py:369
  33.0 16.8 %collective-permute-start.6 = (bf16[208,768]{1,0:T(8,128)(2,1)S(1)}, bf16[208,768]{1,0:T(8,128)(2,1)S(1)}, u32[]{:S(2)}, u32[]{:S(2)}) collective-permute-start(bf16[208,768]{1,0:T(8,128)(2,1)S(1)} %get-tuple-element.681), channel_id=1, source_target_pairs={{0,4},{2,6},{4,0},{6,2},{8,12},{10,14},{12,8},{14,10},{1,5},{3,7},... | collective-permute-start | bytes 958472 | tf_op jit(solution)/shard_map/ppermute | solution.py:366
  39.7 20.6 %collective-permute-start.8 = (bf16[208,768]{1,0:T(8,128)(2,1)S(1)}, bf16[208,768]{1,0:T(8,128)(2,1)S(1)}, u32[]{:S(2)}, u32[]{:S(2)}) collective-permute-start(bf16[208,768]{1,0:T(8,128)(2,1)S(1)} %get-tuple-element.683), channel_id=1, source_target_pairs={{0,12},{2,14},{4,8},{6,10},{8,4},{10,6},{12,0},{14,2},{1,13},{3,15... | collective-permute-start | bytes 958472 | tf_op jit(solution)/shard_map/ppermute | solution.py:366
  61.1 25.2 %collective-permute-start.14 = (bf16[624,768]{1,0:T(8,128)(2,1)S(1)}, bf16[624,768]{1,0:T(8,128)(2,1)S(1)}, u32[]{:S(2)}, u32[]{:S(2)}) collective-permute-start(bf16[624,768]{1,0:T(8,128)(2,1)S(1)} %pad_maximum_fusion), channel_id=1, source_target_pairs={{0,2},{2,0},{4,6},{6,4},{8,10},{10,8},{12,14},{14,12},{1,3},{3,1},... | collective-permute-start | bytes 2875400 | tf_op jit(solution)/shard_map/ppermute | solution.py:369
  61.4 23.2 %collective-permute-start.11 = (bf16[192,768]{1,0:T(8,128)(2,1)S(1)}, bf16[192,768]{1,0:T(8,128)(2,1)S(1)}, u32[]{:S(2)}, u32[]{:S(2)}) collective-permute-start(bf16[192,768]{1,0:T(8,128)(2,1)S(1)} %get-tuple-element.695), channel_id=1, source_target_pairs={{0,4},{2,6},{4,0},{6,2},{8,12},{10,14},{12,8},{14,10},{1,5},{3,7},... | collective-permute-start | bytes 884744 | tf_op jit(solution)/shard_map/ppermute | solution.py:366
  67.9 16.7 %collective-permute-start.12 = (bf16[192,768]{1,0:T(8,128)(2,1)S(1)}, bf16[192,768]{1,0:T(8,128)(2,1)S(1)}, u32[]{:S(2)}, u32[]{:S(2)}) collective-permute-start(bf16[192,768]{1,0:T(8,128)(2,1)S(1)} %get-tuple-element.696), channel_id=1, source_target_pairs={{0,8},{2,10},{4,12},{6,14},{8,0},{10,2},{12,4},{14,6},{1,9},{3,11}... | collective-permute-start | bytes 884744 | tf_op jit(solution)/shard_map/ppermute | solution.py:366
  68.9 17.4 %collective-permute-start.13 = (bf16[192,768]{1,0:T(8,128)(2,1)S(1)}, bf16[192,768]{1,0:T(8,128)(2,1)S(1)}, u32[]{:S(2)}, u32[]{:S(2)}) collective-permute-start(bf16[192,768]{1,0:T(8,128)(2,1)S(1)} %get-tuple-element.697), channel_id=1, source_target_pairs={{0,12},{2,14},{4,8},{6,10},{8,4},{10,6},{12,0},{14,2},{1,13},{3,15... | collective-permute-start | bytes 884744 | tf_op jit(solution)/shard_map/ppermute | solution.py:366
  86.4 21.5 %collective-permute-start.19 = (bf16[576,768]{1,0:T(8,128)(2,1)S(1)}, bf16[576,768]{1,0:T(8,128)(2,1)S(1)}, u32[]{:S(2)}, u32[]{:S(2)}) collective-permute-start(bf16[576,768]{1,0:T(8,128)(2,1)S(1)} %pad_maximum_fusion.1), channel_id=1, source_target_pairs={{0,2},{2,0},{4,6},{6,4},{8,10},{10,8},{12,14},{14,12},{1,3},{3,1},... | collective-permute-start | bytes 2654216 | tf_op jit(solution)/shard_map/ppermute | solution.py:369
  87.7 17.4 %collective-permute-start.16 = (bf16[192,512]{1,0:T(8,128)(2,1)S(1)}, bf16[192,512]{1,0:T(8,128)(2,1)S(1)}, u32[]{:S(2)}, u32[]{:S(2)}) collective-permute-start(bf16[192,512]{1,0:T(8,128)(2,1)S(1)} %get-tuple-element.718), channel_id=1, source_target_pairs={{0,4},{2,6},{4,0},{6,2},{8,12},{10,14},{12,8},{14,10},{1,5},{3,7},... | collective-permute-start | bytes 589832 | tf_op jit(solution)/shard_map/ppermute | solution.py:366
  137.5 19.8 %collective-permute-start.29 = (f32[2,1,192,384]{3,2,1,0:T(8,128)S(1)}, f32[2,1,192,384]{3,2,1,0:T(8,128)S(1)}, u32[]{:S(2)}, u32[]{:S(2)}) collective-permute-start(f32[2,1,192,384]{3,2,1,0:T(8,128)S(1)} %slice_add_fusion.16), channel_id=1, source_target_pairs={{0,4},{2,6},{4,0},{6,2},{8,12},{10,14},{12,8},{14,10},{1,5},{3,7},... | collective-permute-start | bytes 1769480 | tf_op jit(solution)/shard_map/ppermute | solution.py:366
  146.0 30.4 %collective-permute-start.24 = (f32[2,1,192,384]{3,2,1,0:T(8,128)}, f32[2,1,192,384]{3,2,1,0:T(8,128)}, u32[]{:S(2)}, u32[]{:S(2)}) collective-permute-start(f32[2,1,192,384]{3,2,1,0:T(8,128)} %slice_add_fusion.18), channel_id=1, source_target_pairs={{0,4},{2,6},{4,0},{6,2},{8,12},{10,14},{12,8},{14,10},{1,5},{3,7},... | collective-permute-start | bytes 1769480 | tf_op jit(solution)/shard_map/ppermute | solution.py:366
  159.4 19.8 %collective-permute-start.30 = (f32[1,192,384]{2,1,0:T(8,128)}, f32[1,192,384]{2,1,0:T(8,128)}, u32[]{:S(2)}, u32[]{:S(2)}) collective-permute-start(f32[1,192,384]{2,1,0:T(8,128)} %get-tuple-element.923), channel_id=1, source_target_pairs={{0,8},{2,10},{4,12},{6,14},{8,0},{10,2},{12,4},{14,6},{1,9},{3,11}... | collective-permute-start | bytes 884744 | tf_op jit(solution)/shard_map/ppermute | solution.py:366
  164.8 32.6 %collective-permute-start.27 = (f32[2,1,192,384]{3,2,1,0:T(8,128)}, f32[2,1,192,384]{3,2,1,0:T(8,128)S(1)}, u32[]{:S(2)}, u32[]{:S(2)}) collective-permute-start(f32[2,1,192,384]{3,2,1,0:T(8,128)} %slice_add_fusion.17), channel_id=1, source_target_pairs={{0,4},{2,6},{4,0},{6,2},{8,12},{10,14},{12,8},{14,10},{1,5},{3,7},... | collective-permute-start | bytes 1769480 | tf_op jit(solution)/shard_map/ppermute | solution.py:366
  177.9 23.6 %collective-permute-start.25 = (f32[1,192,384]{2,1,0:T(8,128)S(1)}, f32[1,192,384]{2,1,0:T(8,128)S(1)}, u32[]{:S(2)}, u32[]{:S(2)}) collective-permute-start(f32[1,192,384]{2,1,0:T(8,128)S(1)} %get-tuple-element.925), channel_id=1, source_target_pairs={{0,8},{2,10},{4,12},{6,14},{8,0},{10,2},{12,4},{14,6},{1,9},{3,11}... | collective-permute-start | bytes 884744 | tf_op jit(solution)/shard_map/ppermute | solution.py:366
  180.8 19.3 %collective-permute-start.31 = (bf16[192,192]{1,0:T(8,128)(2,1)S(1)}, bf16[192,192]{1,0:T(8,128)(2,1)S(1)}, u32[]{:S(2)}, u32[]{:S(2)}) collective-permute-start(bf16[192,192]{1,0:T(8,128)(2,1)S(1)} %get-tuple-element.794), channel_id=1, source_target_pairs={{0,6},{1,7},{2,8},{3,9},{4,10},{5,11},{6,12},{7,13},{8,14},{9,15},... | collective-permute-start | bytes 221192 | tf_op jit(solution)/shard_map/ppermute | solution.py:463
  201.4 20.7 %collective-permute-start.32 = (f32[1,192,384]{2,1,0:T(8,128)S(1)}, f32[1,192,384]{2,1,0:T(8,128)S(1)}, u32[]{:S(2)}, u32[]{:S(2)}) collective-permute-start(f32[1,192,384]{2,1,0:T(8,128)S(1)} %get-tuple-element.921), channel_id=1, source_target_pairs={{0,8},{2,10},{4,12},{6,14},{8,0},{10,2},{12,4},{14,6},{1,9},{3,11}... | collective-permute-start | bytes 884744 | tf_op jit(solution)/shard_map/ppermute | solution.py:366
  202.2 20.9 %collective-permute-start.33 = (bf16[192,192]{1,0:T(8,128)(2,1)S(1)}, bf16[192,192]{1,0:T(8,128)(2,1)S(1)}, u32[]{:S(2)}, u32[]{:S(2)}) collective-permute-start(bf16[192,192]{1,0:T(8,128)(2,1)S(1)} %get-tuple-element.798), channel_id=1, source_target_pairs={{0,2},{1,3},{2,4},{3,5},{4,6},{5,7},{6,8},{7,9},{8,10},{9,11},{10,... | collective-permute-start | bytes 221192 | tf_op jit(solution)/shard_map/ppermute | solution.py:463
  203.5 19.7 %collective-permute-start.34 = (bf16[192,192]{1,0:T(8,128)(2,1)S(1)}, bf16[192,192]{1,0:T(8,128)(2,1)S(1)}, u32[]{:S(2)}, u32[]{:S(2)}) collective-permute-start(bf16[192,192]{1,0:T(8,128)(2,1)S(1)} %get-tuple-element.799), channel_id=1, source_target_pairs={{0,3},{1,2},{2,5},{3,4},{4,7},{5,6},{6,9},{7,8},{8,11},{9,10},{10,... | collective-permute-start | bytes 221192 | tf_op jit(solution)/shard_map/ppermute | solution.py:463
  205.5 25.9 %collective-permute-start.37 = (bf16[192,192]{1,0:T(8,128)(2,1)S(1)}, bf16[192,192]{1,0:T(8,128)(2,1)S(1)}, u32[]{:S(2)}, u32[]{:S(2)}) collective-permute-start(bf16[192,192]{1,0:T(8,128)(2,1)S(1)} %get-tuple-element.802), channel_id=1, source_target_pairs={{0,7},{1,6},{2,9},{3,8},{4,11},{5,10},{6,13},{7,12},{8,15},{9,14},... | collective-permute-start | bytes 221192 | tf_op jit(solution)/shard_map/ppermute | solution.py:463
  (32 other events, 357.1 us)

commit v6 on v5

--- a/solution.py
+++ b/solution.py
@@ -203,8 +203,8 @@
             in_specs=in_specs,
             out_specs=[whole(out.shape) for out in out_shape],
             scratch_shapes=[
-                pltpu.VMEM((batch * side, width), jnp.float32),
-                pltpu.VMEM((batch * 8, width), jnp.float32),
+                pltpu.VMEM(((batch + 1) * side, width), jnp.float32),
+                pltpu.VMEM(((batch + 1) * 8, width), jnp.float32),
                 pltpu.VMEM((GROUP * side, 2 * width), jnp.bfloat16),
             ],
         ),

time: 233 us -> 233 us (level)
  no operation moved by 1% of the time
where the time goes in v6:
time: 233 us
  waiting for transfers between devices  104 us (45%)
  starting transfers between devices  63.8 us (27%)
  Pallas kernels  39.6 us (17%)
  other arithmetic  12.6 us (5%)
  local copies, waits for them, and re-layouts  9.32 us (4%)
  between operations  2.76 us (1%)
    ppermute x18, waiting for transfers between devices, along(): return lax.ppermute(x, 'blk', [(i, i ^ 2 * k) for i in range(owners)])  75.1 us
    ppermute x18, starting transfers between devices, along(): return lax.ppermute(x, 'blk', [(i, i ^ 2 * k) for i in range(owners)])  42.1 us
    pallas_call x3, Pallas kernels, partial_tiles(): pl.pallas_call(functools.partial(tiles_kernel, order, reach, (owners, slo...  20.7 us
    pallas_call x2, Pallas kernels, precondition(): pl.pallas_call(functools.partial(precondition_kernel, plan, notes), grid_...  16.5 us
    ppermute x9, waiting for transfers between devices, beside(): return lax.ppermute(x, 'blk', [(i, i ^ 1) for i in range(owners)])  14 us
    ppermute x6, waiting for transfers between devices, back(): return lax.ppermute(x, ('blk', 'dim'), pairs)  10.7 us
    ppermute x5, starting transfers between devices, across(): return lax.ppermute(x, 'dim', [(0, 1), (1, 0)])  8.63 us
    unnamed x45, local copies, waits for them, and re-layouts  6.94 us
  transfers between devices with their start and end apart: 38, of which 17 were waited for; matrix products, arithmetic and copies ran while one was open for 6% of the time, Pallas kernels for 14%

profile of v6, /device:TPU:5, one launch (start us, length us, event | category | flops | bytes accessed | tf_op | source)
XLA Modules:
  0.0 232.5 jit_solution(1678799707296541666)
XLA Ops:
  6.5 3.7 %precondition.2 = (bf16[64,2048]{1,0:T(8,128)(2,1)S(1)}, bf16[64,2048]{1,0:T(8,128)(2,1)S(1)}, bf16[64,2048]{1,0:T(8,128)(2,1)S(1)}, bf16[64,2048]{1,0:T(8,128)(2,1)S(1)}, f32[64,128]{1,0:T(8,128)S(1)}) custom-call(s32[3]{0:T(128)S(1)} %pad_add_fusion.spot, bf16[64,64,128]{2,1,0:T(8,128)(2,1)S(1)} %slice.483.own, ...), custom_call_target="tpu_custom_call" | custom-call | flops 1048576 | bytes 65536 | tf_op jit(solution)/shard_map/precondition/pallas_call | solution.py:198
  11.6 2.3 collective-permute-start.3
  16.3 12.8 %precondition.3 = (bf16[208,2048]{1,0:T(8,128)(2,1)S(1)}, bf16[208,768]{1,0:T(8,128)(2,1)S(1)}, bf16[192,768]{1,0:T(8,128)(2,1)S(1)}, bf16[192,512]{1,0:T(8,128)...) custom-call(s32[3]{0:T(128)S(1)} %pad_add_fusion.spot, ...), custom_call_target="tpu_custom_call" | custom-call | flops 1048576 | bytes 65536 | tf_op jit(solution)/shard_map/precondition/pallas_call | solution.py:198
  33.0 5.8 %collective-permute-start.6 = (bf16[208,768]{1,0:T(8,128)(2,1)S(1)}, bf16[208,768]{1,0:T(8,128)(2,1)S(1)}, u32[]{:S(2)}, u32[]{:S(2)}) collective-permute-start(bf16[208,768]{1,0:T(8,128)(2,1)S(1)} %get-tuple-element.681), channel_id=1, source_target_pairs={{0,4},{2,6},{4,0},{6,2},{8,12},{10,14},{12,8},{14,10},{1,5},{3,7},... | collective-permute-start | bytes 958472 | tf_op jit(solution)/shard_map/ppermute | solution.py:366
  40.9 8.9 %collective-permute-done.6.rest_1_.rest_11_ = bf16[208,768]{1,0:T(8,128)(2,1)S(1)} collective-permute-done((bf16[208,768]{1,0:T(8,128)(2,1)S(1)}, bf16[208,768]{1,0:T(8,128)(2,1)S(1)}, u32[]{:S(2)}, u32[]{:S(2)}) %collective-permute-start.6) | collective-permute-done | bytes 319520 | tf_op jit(solution)/shard_map/ppermute | solution.py:366
  50.6 9.8 %collective-permute-done.8.rest_3_.rest_15_ = bf16[208,768]{1,0:T(8,128)(2,1)S(1)} collective-permute-done((bf16[208,768]{1,0:T(8,128)(2,1)S(1)}, bf16[208,768]{1,0:T(8,128)(2,1)S(1)}, u32[]{:S(2)}, u32[]{:S(2)}) %collective-permute-start.8) | collective-permute-done | bytes 319520 | tf_op jit(solution)/shard_map/ppermute | solution.py:366
  61.4 6.5 %collective-permute-start.11 = (bf16[192,768]{1,0:T(8,128)(2,1)S(1)}, bf16[192,768]{1,0:T(8,128)(2,1)S(1)}, u32[]{:S(2)}, u32[]{:S(2)}) collective-permute-start(bf16[192,768]{1,0:T(8,128)(2,1)S(1)} %get-tuple-element.695), channel_id=1, source_target_pairs={{0,4},{2,6},{4,0},{6,2},{8,12},{10,14},{12,8},{14,10},{1,5},{3,7},... | collective-permute-start | bytes 884744 | tf_op jit(solution)/shard_map/ppermute | solution.py:366
  71.3 13.3 %collective-permute-done.15.rest_22_ = bf16[64,2048]{1,0:T(8,128)(2,1)S(1)} collective-permute-done((bf16[64,2048]{1,0:T(8,128)(2,1)S(1)}, bf16[64,2048]{1,0:T(8,128)(2,1)S(1)}, u32[]{:S(2)}, u32[]{:S(2)}) %collective-permute-start.15) | collective-permute-done | bytes 262176 | tf_op jit(solution)/shard_map/ppermute | solution.py:369
  87.7 7.6 %collective-permute-start.16 = (bf16[192,512]{1,0:T(8,128)(2,1)S(1)}, bf16[192,512]{1,0:T(8,128)(2,1)S(1)}, u32[]{:S(2)}, u32[]{:S(2)}) collective-permute-start(bf16[192,512]{1,0:T(8,128)(2,1)S(1)} %get-tuple-element.718), channel_id=1, source_target_pairs={{0,4},{2,6},{4,0},{6,2},{8,12},{10,14},{12,8},{14,10},{1,5},{3,7},... | collective-permute-start | bytes 589832 | tf_op jit(solution)/shard_map/ppermute | solution.py:366
  98.1 7.0 %partial_tiles.3 = (f32[4,1,192,384]{3,2,1,0:T(8,128)S(1)}, f32[4,1,192,384]{3,2,1,0:T(8,128)S(1)}, f32[4,1,192,384]{3,2,1,0:T(8,128)S(1)}, f32[4,1,192,384]{3,2...) custom-call(s32[3]{0:T(128)S(1)} %pad_add_fusion.spot, ...), custom_call_target="tpu_custom_call" | custom-call | flops 1048576 | bytes 65536 | tf_op jit(solution)/shard_map/partial_tiles/pallas_call | solution.py:299
  105.1 2.7 %collective-permute-done.18.rest_15_ = bf16[192,512]{1,0:T(8,128)(2,1)S(1)} collective-permute-done((bf16[192,512]{1,0:T(8,128)(2,1)S(1)}, bf16[192,512]{1,0:T(8,128)(2,1)S(1)}, u32[]{:S(2)}, u32[]{:S(2)}) %collective-permute-start.18) | collective-permute-done | bytes 196640 | tf_op jit(solution)/shard_map/ppermute | solution.py:366
  109.6 7.3 %partial_tiles.4 = (f32[4,1,192,384]{3,2,1,0:T(8,128)S(1)}, f32[4,1,192,384]{3,2,1,0:T(8,128)S(1)}, f32[4,1,192,384]{3,2,1,0:T(8,128)S(1)}, f32[4,1,192,384]{3,2...) custom-call(s32[3]{0:T(128)S(1)} %pad_add_fusion.spot, ...), custom_call_target="tpu_custom_call" | custom-call | flops 1048576 | bytes 65536 | tf_op jit(solution)/shard_map/partial_tiles/pallas_call | solution.py:299
  116.9 6.4 %partial_tiles.5 = (f32[4,1,192,384]{3,2,1,0:T(8,128)S(1)}, f32[4,1,192,384]{3,2,1,0:T(8,128)S(1)}, f32[4,1,192,384]{3,2,1,0:T(8,128)S(1)}, f32[4,1,192,384]{3,2...) custom-call(s32[3]{0:T(128)S(1)} %pad_add_fusion.spot, ...), custom_call_target="tpu_custom_call" | custom-call | flops 1048576 | bytes 65536 | tf_op jit(solution)/shard_map/partial_tiles/pallas_call | solution.py:299
  126.4 7.0 %collective-permute-start.28 = (f32[4,1,192,384]{3,2,1,0:T(8,128)}, f32[4,1,192,384]{3,2,1,0:T(8,128)}, u32[]{:S(2)}, u32[]{:S(2)}) collective-permute-start(f32[4,1,192,384]{3,2,1,0:T(8,128)} %get-tuple-element.792), channel_id=1, source_target_pairs={{0,1},{1,0},{2,3},{3,2},{4,5},{5,4},{6,7},{7,6},{8,9},{9,8},{10,11... | collective-permute-start | bytes 3538952 | tf_op jit(solution)/shard_map/ppermute | solution.py:363
  133.9 2.3 collective-permute-done.28
  137.5 6.4 %collective-permute-start.29 = (f32[2,1,192,384]{3,2,1,0:T(8,128)S(1)}, f32[2,1,192,384]{3,2,1,0:T(8,128)S(1)}, u32[]{:S(2)}, u32[]{:S(2)}) collective-permute-start(f32[2,1,192,384]{3,2,1,0:T(8,128)S(1)} %slice_add_fusion.16), channel_id=1, source_target_pairs={{0,4},{2,6},{4,0},{6,2},{8,12},{10,14},{12,8},{14,10},{1,5},{3,7},... | collective-permute-start | bytes 1769480 | tf_op jit(solution)/shard_map/ppermute | solution.py:366
  148.4 9.0 %collective-permute-done.29 = f32[2,1,192,384]{3,2,1,0:T(8,128)S(1)} collective-permute-done((f32[2,1,192,384]{3,2,1,0:T(8,128)S(1)}, f32[2,1,192,384]{3,2,1,0:T(8,128)S(1)}, u32[]{:S(2)}, u32[]{:S(2)}) %collective-permute-start.29) | collective-permute-done | bytes 589856 | tf_op jit(solution)/shard_map/ppermute | solution.py:366
  159.4 3.1 %collective-permute-start.30 = (f32[1,192,384]{2,1,0:T(8,128)}, f32[1,192,384]{2,1,0:T(8,128)}, u32[]{:S(2)}, u32[]{:S(2)}) collective-permute-start(f32[1,192,384]{2,1,0:T(8,128)} %get-tuple-element.923), channel_id=1, source_target_pairs={{0,8},{2,10},{4,12},{6,14},{8,0},{10,2},{12,4},{14,6},{1,9},{3,11}... | collective-permute-start | bytes 884744 | tf_op jit(solution)/shard_map/ppermute | solution.py:366
  165.2 11.2 %collective-permute-done.24 = f32[2,1,192,384]{3,2,1,0:T(8,128)} collective-permute-done((f32[2,1,192,384]{3,2,1,0:T(8,128)}, f32[2,1,192,384]{3,2,1,0:T(8,128)}, u32[]{:S(2)}, u32[]{:S(2)}) %collective-permute-start.24) | collective-permute-done | bytes 589856 | tf_op jit(solution)/shard_map/ppermute | solution.py:366
  182.8 14.6 %collective-permute-done.27 = f32[2,1,192,384]{3,2,1,0:T(8,128)S(1)} collective-permute-done((f32[2,1,192,384]{3,2,1,0:T(8,128)}, f32[2,1,192,384]{3,2,1,0:T(8,128)S(1)}, u32[]{:S(2)}, u32[]{:S(2)}) %collective-permute-start.27) | collective-permute-done | bytes 589856 | tf_op jit(solution)/shard_map/ppermute | solution.py:366
  197.4 2.7 %collective-permute-done.31 = bf16[192,192]{1,0:T(8,128)(2,1)S(1)} collective-permute-done((bf16[192,192]{1,0:T(8,128)(2,1)S(1)}, bf16[192,192]{1,0:T(8,128)(2,1)S(1)}, u32[]{:S(2)}, u32[]{:S(2)}) %collective-permute-start.31) | collective-permute-done | bytes 73760 | tf_op jit(solution)/shard_map/ppermute | solution.py:463
  207.9 14.2 %collective-permute-done.32 = f32[1,192,384]{2,1,0:T(8,128)S(1)} collective-permute-done((f32[1,192,384]{2,1,0:T(8,128)S(1)}, f32[1,192,384]{2,1,0:T(8,128)S(1)}, u32[]{:S(2)}, u32[]{:S(2)}) %collective-permute-start.32) | collective-permute-done | bytes 294944 | tf_op jit(solution)/shard_map/ppermute | solution.py:366
  223.3 4.8 %collective-permute-done.35 = bf16[192,192]{1,0:T(8,128)(2,1)S(1)} collective-permute-done((bf16[192,192]{1,0:T(8,128)(2,1)S(1)}, bf16[192,192]{1,0:T(8,128)(2,1)S(1)}, u32[]{:S(2)}, u32[]{:S(2)}) %collective-permute-start.35) | collective-permute-done | bytes 73760 | tf_op jit(solution)/shard_map/ppermute | solution.py:463
  228.1 3.2 %collective-permute-done.36 = bf16[192,192]{1,0:T(8,128)(2,1)S(1)} collective-permute-done((bf16[192,192]{1,0:T(8,128)(2,1)S(1)}, bf16[192,192]{1,0:T(8,128)(2,1)S(1)}, u32[]{:S(2)}, u32[]{:S(2)}) %collective-permute-start.36) | collective-permute-done | bytes 73760 | tf_op jit(solution)/shard_map/ppermute | solution.py:463
  (144 shorter events, 57.5 us)
Async XLA Ops:
  10.3 18.9 %collective-permute-start.2 = (bf16[64,2048]{1,0:T(8,128)(2,1)S(1)}, bf16[64,2048]{1,0:T(8,128)(2,1)S(1)}, u32[]{:S(2)}, u32[]{:S(2)}) collective-permute-start(bf16[64,2048]{1,0:T(8,128)(2,1)S(1)} %get-tuple-element.676), channel_id=1, source_target_pairs={{0,4},{2,6},{4,0},{6,2},{8,12},{10,14},{12,8},{14,10},{1,5},{3,7},... | collective-permute-start | bytes 786440 | tf_op jit(solution)/shard_map/ppermute | solution.py:366
  11.6 17.5 %collective-permute-start.3 = (bf16[64,2048]{1,0:T(8,128)(2,1)S(1)}, bf16[64,2048]{1,0:T(8,128)(2,1)S(1)}, u32[]{:S(2)}, u32[]{:S(2)}) collective-permute-start(bf16[64,2048]{1,0:T(8,128)(2,1)S(1)} %get-tuple-element.677), channel_id=1, source_target_pairs={{0,8},{2,10},{4,12},{6,14},{8,0},{10,2},{12,4},{14,6},{1,9},{3,11}... | collective-permute-start | bytes 786440 | tf_op jit(solution)/shard_map/ppermute | solution.py:366
  13.9 17.5 %collective-permute-start.4 = (bf16[64,2048]{1,0:T(8,128)(2,1)S(1)}, bf16[64,2048]{1,0:T(8,128)(2,1)S(1)}, u32[]{:S(2)}, u32[]{:S(2)}) collective-permute-start(bf16[64,2048]{1,0:T(8,128)(2,1)S(1)} %get-tuple-element.678), channel_id=1, source_target_pairs={{0,12},{2,14},{4,8},{6,10},{8,4},{10,6},{12,0},{14,2},{1,13},{3,15... | collective-permute-start | bytes 786440 | tf_op jit(solution)/shard_map/ppermute | solution.py:366
  13.9 17.5 %collective-permute-start.5 = (bf16[64,2048]{1,0:T(8,128)(2,1)S(1)}, bf16[64,2048]{1,0:T(8,128)(2,1)S(1)}, u32[]{:S(2)}, u32[]{:S(2)}) collective-permute-start(bf16[64,2048]{1,0:T(8,128)(2,1)S(1)} %get-tuple-element.765.rest_8_), channel_id=1, source_target_pairs={{0,2},{2,0},{4,6},{6,4},{8,10},{10,8},{12,14},{14,12},{1,3},{3,1},... | collective-permute-start | bytes 786440 | tf_op jit(solution)/shard_map/ppermute | solution.py:369
  31.4 29.7 %collective-permute-start.10 = (bf16[208,2048]{1,0:T(8,128)(2,1)S(1)}, bf16[208,2048]{1,0:T(8,128)(2,1)S(1)}, u32[]{:S(2)}, u32[]{:S(2)}) collective-permute-start(bf16[208,2048]{1,0:T(8,128)(2,1)S(1)} %get-tuple-element.803.rest_0_.rest_9_), channel_id=1, source_target_pairs={{0,2},{2,0},{4,6},{6,4},{8,10},{10,8},{12,14},{14,12},{1,3},{3,1},... | collective-permute-start | bytes 2555912 | tf_op jit(solution)/shard_map/ppermute | solution.py:369
  31.7 29.4 %collective-permute-start.9 = (bf16[128,2048]{1,0:T(8,128)(2,1)S(1)}, bf16[128,2048]{1,0:T(8,128)(2,1)S(1)}, u32[]{:S(2)}, u32[]{:S(2)}) collective-permute-start(bf16[128,2048]{1,0:T(8,128)(2,1)S(1)} %pad_maximum_fusion.2), channel_id=1, source_target_pairs={{0,2},{2,0},{4,6},{6,4},{8,10},{10,8},{12,14},{14,12},{1,3},{3,1},... | collective-permute-start | bytes 1572872 | tf_op jit(solution)/shard_map/ppermute | solution.py:369
  33.0 16.8 %collective-permute-start.6 = (bf16[208,768]{1,0:T(8,128)(2,1)S(1)}, bf16[208,768]{1,0:T(8,128)(2,1)S(1)}, u32[]{:S(2)}, u32[]{:S(2)}) collective-permute-start(bf16[208,768]{1,0:T(8,128)(2,1)S(1)} %get-tuple-element.681), channel_id=1, source_target_pairs={{0,4},{2,6},{4,0},{6,2},{8,12},{10,14},{12,8},{14,10},{1,5},{3,7},... | collective-permute-start | bytes 958472 | tf_op jit(solution)/shard_map/ppermute | solution.py:366
  39.7 20.6 %collective-permute-start.8 = (bf16[208,768]{1,0:T(8,128)(2,1)S(1)}, bf16[208,768]{1,0:T(8,128)(2,1)S(1)}, u32[]{:S(2)}, u32[]{:S(2)}) collective-permute-start(bf16[208,768]{1,0:T(8,128)(2,1)S(1)} %get-tuple-element.683), channel_id=1, source_target_pairs={{0,12},{2,14},{4,8},{6,10},{8,4},{10,6},{12,0},{14,2},{1,13},{3,15... | collective-permute-start | bytes 958472 | tf_op jit(solution)/shard_map/ppermute | solution.py:366
  61.1 25.2 %collective-permute-start.14 = (bf16[624,768]{1,0:T(8,128)(2,1)S(1)}, bf16[624,768]{1,0:T(8,128)(2,1)S(1)}, u32[]{:S(2)}, u32[]{:S(2)}) collective-permute-start(bf16[624,768]{1,0:T(8,128)(2,1)S(1)} %pad_maximum_fusion), channel_id=1, source_target_pairs={{0,2},{2,0},{4,6},{6,4},{8,10},{10,8},{12,14},{14,12},{1,3},{3,1},... | collective-permute-start | bytes 2875400 | tf_op jit(solution)/shard_map/ppermute | solution.py:369
  61.4 23.2 %collective-permute-start.11 = (bf16[192,768]{1,0:T(8,128)(2,1)S(1)}, bf16[192,768]{1,0:T(8,128)(2,1)S(1)}, u32[]{:S(2)}, u32[]{:S(2)}) collective-permute-start(bf16[192,768]{1,0:T(8,128)(2,1)S(1)} %get-tuple-element.695), channel_id=1, source_target_pairs={{0,4},{2,6},{4,0},{6,2},{8,12},{10,14},{12,8},{14,10},{1,5},{3,7},... | collective-permute-start | bytes 884744 | tf_op jit(solution)/shard_map/ppermute | solution.py:366
  67.9 16.7 %collective-permute-start.12 = (bf16[192,768]{1,0:T(8,128)(2,1)S(1)}, bf16[192,768]{1,0:T(8,128)(2,1)S(1)}, u32[]{:S(2)}, u32[]{:S(2)}) collective-permute-start(bf16[192,768]{1,0:T(8,128)(2,1)S(1)} %get-tuple-element.696), channel_id=1, source_target_pairs={{0,8},{2,10},{4,12},{6,14},{8,0},{10,2},{12,4},{14,6},{1,9},{3,11}... | collective-permute-start | bytes 884744 | tf_op jit(solution)/shard_map/ppermute | solution.py:366
  68.9 17.4 %collective-permute-start.13 = (bf16[192,768]{1,0:T(8,128)(2,1)S(1)}, bf16[192,768]{1,0:T(8,128)(2,1)S(1)}, u32[]{:S(2)}, u32[]{:S(2)}) collective-permute-start(bf16[192,768]{1,0:T(8,128)(2,1)S(1)} %get-tuple-element.697), channel_id=1, source_target_pairs={{0,12},{2,14},{4,8},{6,10},{8,4},{10,6},{12,0},{14,2},{1,13},{3,15... | collective-permute-start | bytes 884744 | tf_op jit(solution)/shard_map/ppermute | solution.py:366
  86.4 21.5 %collective-permute-start.19 = (bf16[576,768]{1,0:T(8,128)(2,1)S(1)}, bf16[576,768]{1,0:T(8,128)(2,1)S(1)}, u32[]{:S(2)}, u32[]{:S(2)}) collective-permute-start(bf16[576,768]{1,0:T(8,128)(2,1)S(1)} %pad_maximum_fusion.1), channel_id=1, source_target_pairs={{0,2},{2,0},{4,6},{6,4},{8,10},{10,8},{12,14},{14,12},{1,3},{3,1},... | collective-permute-start | bytes 2654216 | tf_op jit(solution)/shard_map/ppermute | solution.py:369
  87.7 17.4 %collective-permute-start.16 = (bf16[192,512]{1,0:T(8,128)(2,1)S(1)}, bf16[192,512]{1,0:T(8,128)(2,1)S(1)}, u32[]{:S(2)}, u32[]{:S(2)}) collective-permute-start(bf16[192,512]{1,0:T(8,128)(2,1)S(1)} %get-tuple-element.718), channel_id=1, source_target_pairs={{0,4},{2,6},{4,0},{6,2},{8,12},{10,14},{12,8},{14,10},{1,5},{3,7},... | collective-permute-start | bytes 589832 | tf_op jit(solution)/shard_map/ppermute | solution.py:366
  137.5 19.8 %collective-permute-start.29 = (f32[2,1,192,384]{3,2,1,0:T(8,128)S(1)}, f32[2,1,192,384]{3,2,1,0:T(8,128)S(1)}, u32[]{:S(2)}, u32[]{:S(2)}) collective-permute-start(f32[2,1,192,384]{3,2,1,0:T(8,128)S(1)} %slice_add_fusion.16), channel_id=1, source_target_pairs={{0,4},{2,6},{4,0},{6,2},{8,12},{10,14},{12,8},{14,10},{1,5},{3,7},... | collective-permute-start | bytes 1769480 | tf_op jit(solution)/shard_map/ppermute | solution.py:366
  146.1 30.4 %collective-permute-start.24 = (f32[2,1,192,384]{3,2,1,0:T(8,128)}, f32[2,1,192,384]{3,2,1,0:T(8,128)}, u32[]{:S(2)}, u32[]{:S(2)}) collective-permute-start(f32[2,1,192,384]{3,2,1,0:T(8,128)} %slice_add_fusion.18), channel_id=1, source_target_pairs={{0,4},{2,6},{4,0},{6,2},{8,12},{10,14},{12,8},{14,10},{1,5},{3,7},... | collective-permute-start | bytes 1769480 | tf_op jit(solution)/shard_map/ppermute | solution.py:366
  159.4 19.8 %collective-permute-start.30 = (f32[1,192,384]{2,1,0:T(8,128)}, f32[1,192,384]{2,1,0:T(8,128)}, u32[]{:S(2)}, u32[]{:S(2)}) collective-permute-start(f32[1,192,384]{2,1,0:T(8,128)} %get-tuple-element.923), channel_id=1, source_target_pairs={{0,8},{2,10},{4,12},{6,14},{8,0},{10,2},{12,4},{14,6},{1,9},{3,11}... | collective-permute-start | bytes 884744 | tf_op jit(solution)/shard_map/ppermute | solution.py:366
  164.8 32.6 %collective-permute-start.27 = (f32[2,1,192,384]{3,2,1,0:T(8,128)}, f32[2,1,192,384]{3,2,1,0:T(8,128)S(1)}, u32[]{:S(2)}, u32[]{:S(2)}) collective-permute-start(f32[2,1,192,384]{3,2,1,0:T(8,128)} %slice_add_fusion.17), channel_id=1, source_target_pairs={{0,4},{2,6},{4,0},{6,2},{8,12},{10,14},{12,8},{14,10},{1,5},{3,7},... | collective-permute-start | bytes 1769480 | tf_op jit(solution)/shard_map/ppermute | solution.py:366
  177.9 23.6 %collective-permute-start.25 = (f32[1,192,384]{2,1,0:T(8,128)S(1)}, f32[1,192,384]{2,1,0:T(8,128)S(1)}, u32[]{:S(2)}, u32[]{:S(2)}) collective-permute-start(f32[1,192,384]{2,1,0:T(8,128)S(1)} %get-tuple-element.925), channel_id=1, source_target_pairs={{0,8},{2,10},{4,12},{6,14},{8,0},{10,2},{12,4},{14,6},{1,9},{3,11}... | collective-permute-start | bytes 884744 | tf_op jit(solution)/shard_map/ppermute | solution.py:366
  180.9 19.3 %collective-permute-start.31 = (bf16[192,192]{1,0:T(8,128)(2,1)S(1)}, bf16[192,192]{1,0:T(8,128)(2,1)S(1)}, u32[]{:S(2)}, u32[]{:S(2)}) collective-permute-start(bf16[192,192]{1,0:T(8,128)(2,1)S(1)} %get-tuple-element.794), channel_id=1, source_target_pairs={{0,6},{1,7},{2,8},{3,9},{4,10},{5,11},{6,12},{7,13},{8,14},{9,15},... | collective-permute-start | bytes 221192 | tf_op jit(solution)/shard_map/ppermute | solution.py:463
  201.4 20.7 %collective-permute-start.32 = (f32[1,192,384]{2,1,0:T(8,128)S(1)}, f32[1,192,384]{2,1,0:T(8,128)S(1)}, u32[]{:S(2)}, u32[]{:S(2)}) collective-permute-start(f32[1,192,384]{2,1,0:T(8,128)S(1)} %get-tuple-element.921), channel_id=1, source_target_pairs={{0,8},{2,10},{4,12},{6,14},{8,0},{10,2},{12,4},{14,6},{1,9},{3,11}... | collective-permute-start | bytes 884744 | tf_op jit(solution)/shard_map/ppermute | solution.py:366
  202.2 20.9 %collective-permute-start.33 = (bf16[192,192]{1,0:T(8,128)(2,1)S(1)}, bf16[192,192]{1,0:T(8,128)(2,1)S(1)}, u32[]{:S(2)}, u32[]{:S(2)}) collective-permute-start(bf16[192,192]{1,0:T(8,128)(2,1)S(1)} %get-tuple-element.798), channel_id=1, source_target_pairs={{0,2},{1,3},{2,4},{3,5},{4,6},{5,7},{6,8},{7,9},{8,10},{9,11},{10,... | collective-permute-start | bytes 221192 | tf_op jit(solution)/shard_map/ppermute | solution.py:463
  203.5 19.7 %collective-permute-start.34 = (bf16[192,192]{1,0:T(8,128)(2,1)S(1)}, bf16[192,192]{1,0:T(8,128)(2,1)S(1)}, u32[]{:S(2)}, u32[]{:S(2)}) collective-permute-start(bf16[192,192]{1,0:T(8,128)(2,1)S(1)} %get-tuple-element.799), channel_id=1, source_target_pairs={{0,3},{1,2},{2,5},{3,4},{4,7},{5,6},{6,9},{7,8},{8,11},{9,10},{10,... | collective-permute-start | bytes 221192 | tf_op jit(solution)/shard_map/ppermute | solution.py:463
  205.5 25.9 %collective-permute-start.37 = (bf16[192,192]{1,0:T(8,128)(2,1)S(1)}, bf16[192,192]{1,0:T(8,128)(2,1)S(1)}, u32[]{:S(2)}, u32[]{:S(2)}) collective-permute-start(bf16[192,192]{1,0:T(8,128)(2,1)S(1)} %get-tuple-element.802), channel_id=1, source_target_pairs={{0,7},{1,6},{2,9},{3,8},{4,11},{5,10},{6,13},{7,12},{8,15},{9,14},... | collective-permute-start | bytes 221192 | tf_op jit(solution)/shard_map/ppermute | solution.py:463
  (32 other events, 357.2 us)

commit v7 on v6

--- a/solution.py
+++ b/solution.py
@@ -15,7 +15,7 @@
 PARTS = ((2,), (0,), (1,))
 GROUP = 8
 STEP = 32
-VMEM_BYTES = 30 * 2**20
+VMEM_BYTES = 22 * 2**20
 SMALL_COST = pl.CostEstimate(flops=2**20, bytes_accessed=2**16, transcendentals=0)
 
 
@@ -389,11 +389,11 @@
         (0, first, first),
         [[features]] * quads,
     )
+    *parts, mean_early = after([*parts, mean_early])
+    (owner_of,) = after([owner_of], parts[0])
     target = slot_targets(owner_of, owners, slots)
     slot_note = jnp.stack([target % NOTE_BASE, target // NOTE_BASE] + [target] * (NOTE - 2))
     slot_note = slot_note.astype(jnp.bfloat16)
-
-    *parts, mean_early, slot_note = after([*parts, mean_early, slot_note])
     early = send(parts)
     early.append(beside(early[0]))
     own, *parts, means, _ = precondition(

time: 233 us -> 237 us (1.017)
  local copies, waits for them, and re-layouts: 9.32 us -> 12.2 us
    unnamed x45 -> x71, local copies, waits for them, and re-layouts: 6.94 us -> 9.86 us
where the time goes in v7:
time: 237 us; the launch traced here: 236 us
  waiting for transfers between devices  104 us (44%)
  starting transfers between devices  64.5 us (27%)
  Pallas kernels  39.4 us (17%)
  other arithmetic  12.8 us (5%)
  local copies, waits for them, and re-layouts  12.2 us (5%)
  between operations  2.99 us (1%)
    ppermute x18, waiting for transfers between devices, along(): return lax.ppermute(x, 'blk', [(i, i ^ 2 * k) for i in range(owners)])  75.4 us
    ppermute x18, starting transfers between devices, along(): return lax.ppermute(x, 'blk', [(i, i ^ 2 * k) for i in range(owners)])  42.5 us
    pallas_call x3, Pallas kernels, partial_tiles(): pl.pallas_call(functools.partial(tiles_kernel, order, reach, (owners, slo...  20.5 us
    pallas_call x2, Pallas kernels, precondition(): pl.pallas_call(functools.partial(precondition_kernel, plan, notes), grid_...  16.6 us
    ppermute x9, waiting for transfers between devices, beside(): return lax.ppermute(x, 'blk', [(i, i ^ 1) for i in range(owners)])  12.9 us
    ppermute x6, waiting for transfers between devices, back(): return lax.ppermute(x, ('blk', 'dim'), pairs)  11.4 us
    unnamed x71, local copies, waits for them, and re-layouts  9.86 us
    ppermute x5, starting transfers between devices, across(): return lax.ppermute(x, 'dim', [(0, 1), (1, 0)])  8.57 us
  transfers between devices with their start and end apart: 38, of which 17 were waited for; matrix products, arithmetic and copies ran while one was open for 6% of the time, Pallas kernels for 14%

profile of v7, /device:TPU:5, one launch (start us, length us, event | category | flops | bytes accessed | tf_op | source)
XLA Modules:
  0.0 236.2 jit_solution(4975985317612144135)
XLA Ops:
  5.5 3.7 %precondition.2 = (bf16[64,2048]{1,0:T(8,128)(2,1)S(1)}, bf16[64,2048]{1,0:T(8,128)(2,1)S(1)}, bf16[64,2048]{1,0:T(8,128)(2,1)S(1)}, bf16[64,2048]{1,0:T(8,128)(2,1)S(1)}, f32[64,128]{1,0:T(8,128)S(1)}) custom-call(s32[3]{0:T(128)S(1)} %pad_add_fusion.spot, bf16[64,64,128]{2,1,0:T(8,128)(2,1)S(1)} %slice.483.own, ...), custom_call_target="tpu_custom_call" | custom-call | flops 1048576 | bytes 65536 | tf_op jit(solution)/shard_map/precondition/pallas_call | solution.py:198
  18.6 12.8 %precondition.3 = (bf16[208,2048]{1,0:T(8,128)(2,1)S(1)}, bf16[208,768]{1,0:T(8,128)(2,1)S(1)}, bf16[192,768]{1,0:T(8,128)(2,1)S(1)}, bf16[192,512]{1,0:T(8,128)...) custom-call(s32[3]{0:T(128)S(1)} %pad_add_fusion.spot, ...), custom_call_target="tpu_custom_call" | custom-call | flops 1048576 | bytes 65536 | tf_op jit(solution)/shard_map/precondition/pallas_call | solution.py:198
  36.0 5.8 %collective-permute-start.6 = (bf16[208,768]{1,0:T(8,128)(2,1)S(1)}, bf16[208,768]{1,0:T(8,128)(2,1)S(1)}, u32[]{:S(2)}, u32[]{:S(2)}) collective-permute-start(bf16[208,768]{1,0:T(8,128)(2,1)S(1)} %get-tuple-element.671), channel_id=1, source_target_pairs={{0,4},{2,6},{4,0},{6,2},{8,12},{10,14},{12,8},{14,10},{1,5},{3,7},... | collective-permute-start | bytes 958472 | tf_op jit(solution)/shard_map/ppermute | solution.py:366
  44.0 8.4 %collective-permute-done.6.rest_1_.rest_11_ = bf16[208,768]{1,0:T(8,128)(2,1)S(1)} collective-permute-done((bf16[208,768]{1,0:T(8,128)(2,1)S(1)}, bf16[208,768]{1,0:T(8,128)(2,1)S(1)}, u32[]{:S(2)}, u32[]{:S(2)}) %collective-permute-start.6) | collective-permute-done | bytes 319520 | tf_op jit(solution)/shard_map/ppermute | solution.py:366
  53.5 9.8 %collective-permute-done.8.rest_3_.rest_15_ = bf16[208,768]{1,0:T(8,128)(2,1)S(1)} collective-permute-done((bf16[208,768]{1,0:T(8,128)(2,1)S(1)}, bf16[208,768]{1,0:T(8,128)(2,1)S(1)}, u32[]{:S(2)}, u32[]{:S(2)}) %collective-permute-start.8) | collective-permute-done | bytes 319520 | tf_op jit(solution)/shard_map/ppermute | solution.py:366
  64.6 6.9 %collective-permute-start.11 = (bf16[192,768]{1,0:T(8,128)(2,1)S(1)}, bf16[192,768]{1,0:T(8,128)(2,1)S(1)}, u32[]{:S(2)}, u32[]{:S(2)}) collective-permute-start(bf16[192,768]{1,0:T(8,128)(2,1)S(1)} %get-tuple-element.685), channel_id=1, source_target_pairs={{0,4},{2,6},{4,0},{6,2},{8,12},{10,14},{12,8},{14,10},{1,5},{3,7},... | collective-permute-start | bytes 884744 | tf_op jit(solution)/shard_map/ppermute | solution.py:366
  74.3 12.5 %collective-permute-done.15.rest_22_ = bf16[64,2048]{1,0:T(8,128)(2,1)S(1)} collective-permute-done((bf16[64,2048]{1,0:T(8,128)(2,1)S(1)}, bf16[64,2048]{1,0:T(8,128)(2,1)S(1)}, u32[]{:S(2)}, u32[]{:S(2)}) %collective-permute-start.15) | collective-permute-done | bytes 262176 | tf_op jit(solution)/shard_map/ppermute | solution.py:369
  86.8 2.9 %collective-permute-done.13.rest_15_ = bf16[192,768]{1,0:T(8,128)(2,1)S(1)} collective-permute-done((bf16[192,768]{1,0:T(8,128)(2,1)S(1)}, bf16[192,768]{1,0:T(8,128)(2,1)S(1)}, u32[]{:S(2)}, u32[]{:S(2)}) %collective-permute-start.13) | collective-permute-done | bytes 294944 | tf_op jit(solution)/shard_map/ppermute | solution.py:366
  90.4 7.8 %collective-permute-start.16 = (bf16[192,512]{1,0:T(8,128)(2,1)S(1)}, bf16[192,512]{1,0:T(8,128)(2,1)S(1)}, u32[]{:S(2)}, u32[]{:S(2)}) collective-permute-start(bf16[192,512]{1,0:T(8,128)(2,1)S(1)} %get-tuple-element.708), channel_id=1, source_target_pairs={{0,4},{2,6},{4,0},{6,2},{8,12},{10,14},{12,8},{14,10},{1,5},{3,7},... | collective-permute-start | bytes 589832 | tf_op jit(solution)/shard_map/ppermute | solution.py:366
  101.1 7.0 %partial_tiles.3 = (f32[4,1,192,384]{3,2,1,0:T(8,128)S(1)}, f32[4,1,192,384]{3,2,1,0:T(8,128)S(1)}, f32[4,1,192,384]{3,2,1,0:T(8,128)S(1)}, f32[4,1,192,384]{3,2...) custom-call(s32[3]{0:T(128)S(1)} %pad_add_fusion.spot, ...), custom_call_target="tpu_custom_call" | custom-call | flops 1048576 | bytes 65536 | tf_op jit(solution)/shard_map/partial_tiles/pallas_call | solution.py:299
  108.1 2.7 %collective-permute-done.18.rest_15_ = bf16[192,512]{1,0:T(8,128)(2,1)S(1)} collective-permute-done((bf16[192,512]{1,0:T(8,128)(2,1)S(1)}, bf16[192,512]{1,0:T(8,128)(2,1)S(1)}, u32[]{:S(2)}, u32[]{:S(2)}) %collective-permute-start.18) | collective-permute-done | bytes 196640 | tf_op jit(solution)/shard_map/ppermute | solution.py:366
  113.2 7.1 %partial_tiles.4 = (f32[4,1,192,384]{3,2,1,0:T(8,128)S(1)}, f32[4,1,192,384]{3,2,1,0:T(8,128)S(1)}, f32[4,1,192,384]{3,2,1,0:T(8,128)S(1)}, f32[4,1,192,384]{3,2...) custom-call(s32[3]{0:T(128)S(1)} %pad_add_fusion.spot, ...), custom_call_target="tpu_custom_call" | custom-call | flops 1048576 | bytes 65536 | tf_op jit(solution)/shard_map/partial_tiles/pallas_call | solution.py:299
  120.4 6.4 %partial_tiles.5 = (f32[4,1,192,384]{3,2,1,0:T(8,128)S(1)}, f32[4,1,192,384]{3,2,1,0:T(8,128)S(1)}, f32[4,1,192,384]{3,2,1,0:T(8,128)S(1)}, f32[4,1,192,384]{3,2...) custom-call(s32[3]{0:T(128)S(1)} %pad_add_fusion.spot, ...), custom_call_target="tpu_custom_call" | custom-call | flops 1048576 | bytes 65536 | tf_op jit(solution)/shard_map/partial_tiles/pallas_call | solution.py:299
  129.9 6.9 %collective-permute-start.28 = (f32[4,1,192,384]{3,2,1,0:T(8,128)}, f32[4,1,192,384]{3,2,1,0:T(8,128)}, u32[]{:S(2)}, u32[]{:S(2)}) collective-permute-start(f32[4,1,192,384]{3,2,1,0:T(8,128)} %get-tuple-element.782), channel_id=1, source_target_pairs={{0,1},{1,0},{2,3},{3,2},{4,5},{5,4},{6,7},{7,6},{8,9},{9,8},{10,11... | collective-permute-start | bytes 3538952 | tf_op jit(solution)/shard_map/ppermute | solution.py:363
  141.0 6.0 %collective-permute-start.29 = (f32[2,1,192,384]{3,2,1,0:T(8,128)S(1)}, f32[2,1,192,384]{3,2,1,0:T(8,128)S(1)}, u32[]{:S(2)}, u32[]{:S(2)}) collective-permute-start(f32[2,1,192,384]{3,2,1,0:T(8,128)S(1)} %slice_add_fusion.16), channel_id=1, source_target_pairs={{0,4},{2,6},{4,0},{6,2},{8,12},{10,14},{12,8},{14,10},{1,5},{3,7},... | collective-permute-start | bytes 1769480 | tf_op jit(solution)/shard_map/ppermute | solution.py:366
  151.4 9.0 %collective-permute-done.29 = f32[2,1,192,384]{3,2,1,0:T(8,128)S(1)} collective-permute-done((f32[2,1,192,384]{3,2,1,0:T(8,128)S(1)}, f32[2,1,192,384]{3,2,1,0:T(8,128)S(1)}, u32[]{:S(2)}, u32[]{:S(2)}) %collective-permute-start.29) | collective-permute-done | bytes 589856 | tf_op jit(solution)/shard_map/ppermute | solution.py:366
  162.4 3.1 %collective-permute-start.30 = (f32[1,192,384]{2,1,0:T(8,128)}, f32[1,192,384]{2,1,0:T(8,128)}, u32[]{:S(2)}, u32[]{:S(2)}) collective-permute-start(f32[1,192,384]{2,1,0:T(8,128)} %get-tuple-element.913), channel_id=1, source_target_pairs={{0,8},{2,10},{4,12},{6,14},{8,0},{10,2},{12,4},{14,6},{1,9},{3,11}... | collective-permute-start | bytes 884744 | tf_op jit(solution)/shard_map/ppermute | solution.py:366
  168.3 11.2 %collective-permute-done.24 = f32[2,1,192,384]{3,2,1,0:T(8,128)} collective-permute-done((f32[2,1,192,384]{3,2,1,0:T(8,128)}, f32[2,1,192,384]{3,2,1,0:T(8,128)}, u32[]{:S(2)}, u32[]{:S(2)}) %collective-permute-start.24) | collective-permute-done | bytes 589856 | tf_op jit(solution)/shard_map/ppermute | solution.py:366
  186.5 14.0 %collective-permute-done.27 = f32[2,1,192,384]{3,2,1,0:T(8,128)S(1)} collective-permute-done((f32[2,1,192,384]{3,2,1,0:T(8,128)}, f32[2,1,192,384]{3,2,1,0:T(8,128)S(1)}, u32[]{:S(2)}, u32[]{:S(2)}) %collective-permute-start.27) | collective-permute-done | bytes 589856 | tf_op jit(solution)/shard_map/ppermute | solution.py:366
  200.4 3.4 %collective-permute-done.31 = bf16[192,192]{1,0:T(8,128)(2,1)S(1)} collective-permute-done((bf16[192,192]{1,0:T(8,128)(2,1)S(1)}, bf16[192,192]{1,0:T(8,128)(2,1)S(1)}, u32[]{:S(2)}, u32[]{:S(2)}) %collective-permute-start.31) | collective-permute-done | bytes 73760 | tf_op jit(solution)/shard_map/ppermute | solution.py:463
  206.5 2.6 %collective-permute-start.34 = (bf16[192,192]{1,0:T(8,128)(2,1)S(1)}, bf16[192,192]{1,0:T(8,128)(2,1)S(1)}, u32[]{:S(2)}, u32[]{:S(2)}) collective-permute-start(bf16[192,192]{1,0:T(8,128)(2,1)S(1)} %get-tuple-element.789), channel_id=1, source_target_pairs={{0,3},{1,2},{2,5},{3,4},{4,7},{5,6},{6,9},{7,8},{8,11},{9,10},{10,... | collective-permute-start | bytes 221192 | tf_op jit(solution)/shard_map/ppermute | solution.py:463
  211.6 14.2 %collective-permute-done.32 = f32[1,192,384]{2,1,0:T(8,128)S(1)} collective-permute-done((f32[1,192,384]{2,1,0:T(8,128)S(1)}, f32[1,192,384]{2,1,0:T(8,128)S(1)}, u32[]{:S(2)}, u32[]{:S(2)}) %collective-permute-start.32) | collective-permute-done | bytes 294944 | tf_op jit(solution)/shard_map/ppermute | solution.py:366
  227.0 4.8 %collective-permute-done.35 = bf16[192,192]{1,0:T(8,128)(2,1)S(1)} collective-permute-done((bf16[192,192]{1,0:T(8,128)(2,1)S(1)}, bf16[192,192]{1,0:T(8,128)(2,1)S(1)}, u32[]{:S(2)}, u32[]{:S(2)}) %collective-permute-start.35) | collective-permute-done | bytes 73760 | tf_op jit(solution)/shard_map/ppermute | solution.py:463
  231.8 3.2 %collective-permute-done.36 = bf16[192,192]{1,0:T(8,128)(2,1)S(1)} collective-permute-done((bf16[192,192]{1,0:T(8,128)(2,1)S(1)}, bf16[192,192]{1,0:T(8,128)(2,1)S(1)}, u32[]{:S(2)}, u32[]{:S(2)}) %collective-permute-start.36) | collective-permute-done | bytes 73760 | tf_op jit(solution)/shard_map/ppermute | solution.py:463
  (170 shorter events, 61.5 us)
Async XLA Ops:
  11.3 22.3 %collective-permute-start.5 = (bf16[64,2048]{1,0:T(8,128)(2,1)S(1)}, bf16[64,2048]{1,0:T(8,128)(2,1)S(1)}, u32[]{:S(2)}, u32[]{:S(2)}) collective-permute-start(bf16[64,2048]{1,0:T(8,128)(2,1)S(1)} %get-tuple-element.755.rest_8_), channel_id=1, source_target_pairs={{0,2},{2,0},{4,6},{6,4},{8,10},{10,8},{12,14},{14,12},{1,3},{3,1},... | collective-permute-start | bytes 786440 | tf_op jit(solution)/shard_map/ppermute | solution.py:369
  12.4 19.0 %collective-permute-start.2 = (bf16[64,2048]{1,0:T(8,128)(2,1)}, bf16[64,2048]{1,0:T(8,128)(2,1)S(1)}, u32[]{:S(2)}, u32[]{:S(2)}) collective-permute-start(bf16[64,2048]{1,0:T(8,128)(2,1)} %copy-done.24), channel_id=1, source_target_pairs={{0,4},{2,6},{4,0},{6,2},{8,12},{10,14},{12,8},{14,10},{1,5},{3,7},... | collective-permute-start | bytes 786440 | tf_op jit(solution)/shard_map/ppermute | solution.py:366
  13.9 17.5 %collective-permute-start.3 = (bf16[64,2048]{1,0:T(8,128)(2,1)}, bf16[64,2048]{1,0:T(8,128)(2,1)S(1)}, u32[]{:S(2)}, u32[]{:S(2)}) collective-permute-start(bf16[64,2048]{1,0:T(8,128)(2,1)} %copy-done.23), channel_id=1, source_target_pairs={{0,8},{2,10},{4,12},{6,14},{8,0},{10,2},{12,4},{14,6},{1,9},{3,11}... | collective-permute-start | bytes 786440 | tf_op jit(solution)/shard_map/ppermute | solution.py:366
  16.2 17.5 %collective-permute-start.4 = (bf16[64,2048]{1,0:T(8,128)(2,1)}, bf16[64,2048]{1,0:T(8,128)(2,1)S(1)}, u32[]{:S(2)}, u32[]{:S(2)}) collective-permute-start(bf16[64,2048]{1,0:T(8,128)(2,1)} %copy-done.22), channel_id=1, source_target_pairs={{0,12},{2,14},{4,8},{6,10},{8,4},{10,6},{12,0},{14,2},{1,13},{3,15... | collective-permute-start | bytes 786440 | tf_op jit(solution)/shard_map/ppermute | solution.py:366
  34.4 29.3 %collective-permute-start.10 = (bf16[208,2048]{1,0:T(8,128)(2,1)S(1)}, bf16[208,2048]{1,0:T(8,128)(2,1)S(1)}, u32[]{:S(2)}, u32[]{:S(2)}) collective-permute-start(bf16[208,2048]{1,0:T(8,128)(2,1)S(1)} %get-tuple-element.793.rest_0_.rest_9_), channel_id=1, source_target_pairs={{0,2},{2,0},{4,6},{6,4},{8,10},{10,8},{12,14},{14,12},{1,3},{3,1},... | collective-permute-start | bytes 2555912 | tf_op jit(solution)/shard_map/ppermute | solution.py:369
  35.4 28.2 %collective-permute-start.9 = (bf16[128,2048]{1,0:T(8,128)(2,1)S(1)}, bf16[128,2048]{1,0:T(8,128)(2,1)S(1)}, u32[]{:S(2)}, u32[]{:S(2)}) collective-permute-start(bf16[128,2048]{1,0:T(8,128)(2,1)S(1)} %pad_maximum_fusion.2), channel_id=1, source_target_pairs={{0,2},{2,0},{4,6},{6,4},{8,10},{10,8},{12,14},{14,12},{1,3},{3,1},... | collective-permute-start | bytes 1572872 | tf_op jit(solution)/shard_map/ppermute | solution.py:369
  36.0 16.4 %collective-permute-start.6 = (bf16[208,768]{1,0:T(8,128)(2,1)S(1)}, bf16[208,768]{1,0:T(8,128)(2,1)S(1)}, u32[]{:S(2)}, u32[]{:S(2)}) collective-permute-start(bf16[208,768]{1,0:T(8,128)(2,1)S(1)} %get-tuple-element.671), channel_id=1, source_target_pairs={{0,4},{2,6},{4,0},{6,2},{8,12},{10,14},{12,8},{14,10},{1,5},{3,7},... | collective-permute-start | bytes 958472 | tf_op jit(solution)/shard_map/ppermute | solution.py:366
  42.8 20.5 %collective-permute-start.8 = (bf16[208,768]{1,0:T(8,128)(2,1)S(1)}, bf16[208,768]{1,0:T(8,128)(2,1)S(1)}, u32[]{:S(2)}, u32[]{:S(2)}) collective-permute-start(bf16[208,768]{1,0:T(8,128)(2,1)S(1)} %get-tuple-element.673), channel_id=1, source_target_pairs={{0,12},{2,14},{4,8},{6,10},{8,4},{10,6},{12,0},{14,2},{1,13},{3,15... | collective-permute-start | bytes 958472 | tf_op jit(solution)/shard_map/ppermute | solution.py:366
  63.8 25.9 %collective-permute-start.14 = (bf16[624,768]{1,0:T(8,128)(2,1)S(1)}, bf16[624,768]{1,0:T(8,128)(2,1)S(1)}, u32[]{:S(2)}, u32[]{:S(2)}) collective-permute-start(bf16[624,768]{1,0:T(8,128)(2,1)S(1)} %pad_maximum_fusion), channel_id=1, source_target_pairs={{0,2},{2,0},{4,6},{6,4},{8,10},{10,8},{12,14},{14,12},{1,3},{3,1},... | collective-permute-start | bytes 2875400 | tf_op jit(solution)/shard_map/ppermute | solution.py:369
  64.6 22.1 %collective-permute-start.11 = (bf16[192,768]{1,0:T(8,128)(2,1)S(1)}, bf16[192,768]{1,0:T(8,128)(2,1)S(1)}, u32[]{:S(2)}, u32[]{:S(2)}) collective-permute-start(bf16[192,768]{1,0:T(8,128)(2,1)S(1)} %get-tuple-element.685), channel_id=1, source_target_pairs={{0,4},{2,6},{4,0},{6,2},{8,12},{10,14},{12,8},{14,10},{1,5},{3,7},... | collective-permute-start | bytes 884744 | tf_op jit(solution)/shard_map/ppermute | solution.py:366
  71.5 15.2 %collective-permute-start.12 = (bf16[192,768]{1,0:T(8,128)(2,1)S(1)}, bf16[192,768]{1,0:T(8,128)(2,1)S(1)}, u32[]{:S(2)}, u32[]{:S(2)}) collective-permute-start(bf16[192,768]{1,0:T(8,128)(2,1)S(1)} %get-tuple-element.686), channel_id=1, source_target_pairs={{0,8},{2,10},{4,12},{6,14},{8,0},{10,2},{12,4},{14,6},{1,9},{3,11}... | collective-permute-start | bytes 884744 | tf_op jit(solution)/shard_map/ppermute | solution.py:366
  72.5 17.1 %collective-permute-start.13 = (bf16[192,768]{1,0:T(8,128)(2,1)S(1)}, bf16[192,768]{1,0:T(8,128)(2,1)S(1)}, u32[]{:S(2)}, u32[]{:S(2)}) collective-permute-start(bf16[192,768]{1,0:T(8,128)(2,1)S(1)} %get-tuple-element.687), channel_id=1, source_target_pairs={{0,12},{2,14},{4,8},{6,10},{8,4},{10,6},{12,0},{14,2},{1,13},{3,15... | collective-permute-start | bytes 884744 | tf_op jit(solution)/shard_map/ppermute | solution.py:366
  89.7 21.1 %collective-permute-start.19 = (bf16[576,768]{1,0:T(8,128)(2,1)S(1)}, bf16[576,768]{1,0:T(8,128)(2,1)S(1)}, u32[]{:S(2)}, u32[]{:S(2)}) collective-permute-start(bf16[576,768]{1,0:T(8,128)(2,1)S(1)} %pad_maximum_fusion.1), channel_id=1, source_target_pairs={{0,2},{2,0},{4,6},{6,4},{8,10},{10,8},{12,14},{14,12},{1,3},{3,1},... | collective-permute-start | bytes 2654216 | tf_op jit(solution)/shard_map/ppermute | solution.py:369
  90.4 17.7 %collective-permute-start.16 = (bf16[192,512]{1,0:T(8,128)(2,1)S(1)}, bf16[192,512]{1,0:T(8,128)(2,1)S(1)}, u32[]{:S(2)}, u32[]{:S(2)}) collective-permute-start(bf16[192,512]{1,0:T(8,128)(2,1)S(1)} %get-tuple-element.708), channel_id=1, source_target_pairs={{0,4},{2,6},{4,0},{6,2},{8,12},{10,14},{12,8},{14,10},{1,5},{3,7},... | collective-permute-start | bytes 589832 | tf_op jit(solution)/shard_map/ppermute | solution.py:366
  141.0 19.4 %collective-permute-start.29 = (f32[2,1,192,384]{3,2,1,0:T(8,128)S(1)}, f32[2,1,192,384]{3,2,1,0:T(8,128)S(1)}, u32[]{:S(2)}, u32[]{:S(2)}) collective-permute-start(f32[2,1,192,384]{3,2,1,0:T(8,128)S(1)} %slice_add_fusion.16), channel_id=1, source_target_pairs={{0,4},{2,6},{4,0},{6,2},{8,12},{10,14},{12,8},{14,10},{1,5},{3,7},... | collective-permute-start | bytes 1769480 | tf_op jit(solution)/shard_map/ppermute | solution.py:366
  149.1 30.4 %collective-permute-start.24 = (f32[2,1,192,384]{3,2,1,0:T(8,128)}, f32[2,1,192,384]{3,2,1,0:T(8,128)}, u32[]{:S(2)}, u32[]{:S(2)}) collective-permute-start(f32[2,1,192,384]{3,2,1,0:T(8,128)} %slice_add_fusion.18), channel_id=1, source_target_pairs={{0,4},{2,6},{4,0},{6,2},{8,12},{10,14},{12,8},{14,10},{1,5},{3,7},... | collective-permute-start | bytes 1769480 | tf_op jit(solution)/shard_map/ppermute | solution.py:366
  162.4 19.8 %collective-permute-start.30 = (f32[1,192,384]{2,1,0:T(8,128)}, f32[1,192,384]{2,1,0:T(8,128)}, u32[]{:S(2)}, u32[]{:S(2)}) collective-permute-start(f32[1,192,384]{2,1,0:T(8,128)} %get-tuple-element.913), channel_id=1, source_target_pairs={{0,8},{2,10},{4,12},{6,14},{8,0},{10,2},{12,4},{14,6},{1,9},{3,11}... | collective-permute-start | bytes 884744 | tf_op jit(solution)/shard_map/ppermute | solution.py:366
  167.9 32.5 %collective-permute-start.27 = (f32[2,1,192,384]{3,2,1,0:T(8,128)}, f32[2,1,192,384]{3,2,1,0:T(8,128)S(1)}, u32[]{:S(2)}, u32[]{:S(2)}) collective-permute-start(f32[2,1,192,384]{3,2,1,0:T(8,128)} %slice_add_fusion.17), channel_id=1, source_target_pairs={{0,4},{2,6},{4,0},{6,2},{8,12},{10,14},{12,8},{14,10},{1,5},{3,7},... | collective-permute-start | bytes 1769480 | tf_op jit(solution)/shard_map/ppermute | solution.py:366
  181.0 24.2 %collective-permute-start.25 = (f32[1,192,384]{2,1,0:T(8,128)S(1)}, f32[1,192,384]{2,1,0:T(8,128)S(1)}, u32[]{:S(2)}, u32[]{:S(2)}) collective-permute-start(f32[1,192,384]{2,1,0:T(8,128)S(1)} %get-tuple-element.915), channel_id=1, source_target_pairs={{0,8},{2,10},{4,12},{6,14},{8,0},{10,2},{12,4},{14,6},{1,9},{3,11}... | collective-permute-start | bytes 884744 | tf_op jit(solution)/shard_map/ppermute | solution.py:366
  183.9 20.0 %collective-permute-start.31 = (bf16[192,192]{1,0:T(8,128)(2,1)S(1)}, bf16[192,192]{1,0:T(8,128)(2,1)S(1)}, u32[]{:S(2)}, u32[]{:S(2)}) collective-permute-start(bf16[192,192]{1,0:T(8,128)(2,1)S(1)} %get-tuple-element.784), channel_id=1, source_target_pairs={{0,6},{1,7},{2,8},{3,9},{4,10},{5,11},{6,12},{7,13},{8,14},{9,15},... | collective-permute-start | bytes 221192 | tf_op jit(solution)/shard_map/ppermute | solution.py:463
  205.1 20.7 %collective-permute-start.32 = (f32[1,192,384]{2,1,0:T(8,128)S(1)}, f32[1,192,384]{2,1,0:T(8,128)S(1)}, u32[]{:S(2)}, u32[]{:S(2)}) collective-permute-start(f32[1,192,384]{2,1,0:T(8,128)S(1)} %get-tuple-element.911), channel_id=1, source_target_pairs={{0,8},{2,10},{4,12},{6,14},{8,0},{10,2},{12,4},{14,6},{1,9},{3,11}... | collective-permute-start | bytes 884744 | tf_op jit(solution)/shard_map/ppermute | solution.py:366
  205.9 20.9 %collective-permute-start.33 = (bf16[192,192]{1,0:T(8,128)(2,1)S(1)}, bf16[192,192]{1,0:T(8,128)(2,1)S(1)}, u32[]{:S(2)}, u32[]{:S(2)}) collective-permute-start(bf16[192,192]{1,0:T(8,128)(2,1)S(1)} %get-tuple-element.788), channel_id=1, source_target_pairs={{0,2},{1,3},{2,4},{3,5},{4,6},{5,7},{6,8},{7,9},{8,10},{9,11},{10,... | collective-permute-start | bytes 221192 | tf_op jit(solution)/shard_map/ppermute | solution.py:463
  206.5 20.3 %collective-permute-start.34 = (bf16[192,192]{1,0:T(8,128)(2,1)S(1)}, bf16[192,192]{1,0:T(8,128)(2,1)S(1)}, u32[]{:S(2)}, u32[]{:S(2)}) collective-permute-start(bf16[192,192]{1,0:T(8,128)(2,1)S(1)} %get-tuple-element.789), channel_id=1, source_target_pairs={{0,3},{1,2},{2,5},{3,4},{4,7},{5,6},{6,9},{7,8},{8,11},{9,10},{10,... | collective-permute-start | bytes 221192 | tf_op jit(solution)/shard_map/ppermute | solution.py:463
  209.1 26.1 %collective-permute-start.37 = (bf16[192,192]{1,0:T(8,128)(2,1)S(1)}, bf16[192,192]{1,0:T(8,128)(2,1)S(1)}, u32[]{:S(2)}, u32[]{:S(2)}) collective-permute-start(bf16[192,192]{1,0:T(8,128)(2,1)S(1)} %get-tuple-element.792), channel_id=1, source_target_pairs={{0,7},{1,6},{2,9},{3,8},{4,11},{5,10},{6,13},{7,12},{8,15},{9,14},... | collective-permute-start | bytes 221192 | tf_op jit(solution)/shard_map/ppermute | solution.py:463
  (45 other events, 664.4 us)
